TPU v7x, 128 devices: a whole 4x4x4 slice. The times are simulated.
128 devices in a mesh: section: 2 (over z_lo), dp: 4 (over z_hi, core), tensor: 16 (over y, x).
Axes of the slice: x: 4, y: 4, z: 4 (z_hi: 2, z_lo: 2; z = z_hi * 2 + z_lo), core: 2. Of those that a mesh axis runs over, the one named last changes fastest.
Arguments:
- encoder_tokens: bfloat16 [8, 1280, 1024], P('dp', 'tensor'), may hold values from -6 to 6
- encoder_segments: int32 [8, 1280], P('dp'), may hold values from 0 to 3, as said below
- decoder_tokens: bfloat16 [8, 128, 1024], P('dp', 'tensor'), may hold values from -6 to 6
- decoder_segments: int32 [8, 128], P('dp'), may hold values from 0 to 3, as said below
- cotangent: bfloat16 [8, 128, 1024], P('dp', 'tensor'), may hold values from -6 to 6
- attention_weight: bfloat16 [2, 6, 1024, 1024], P('section', None, None, 'tensor'), may hold values from -2 to 2
- feedforward_weight: bfloat16 [2, 2, 1024, 4096], P('section', None, None, 'tensor'), may hold values from -0.1875 to 0.1875
- norm_gain: float32 [2, 3, 1024], P('section'), may hold values from 0.5 to 1.5
- norm_shift: float32 [2, 3, 1024], P('section'), may hold values from -1.5 to 1.5
Outputs:
- decoder_output: bfloat16 [8, 128, 1024], P('dp', 'tensor', 'section')
- encoder_grad: float32 [8, 1280, 1024], P('dp', 'tensor', 'section')
- decoder_grad: float32 [8, 128, 1024], P('dp', 'tensor', 'section')
- attention_grad: float32 [2, 6, 1024, 1024], P('section', None, None, 'tensor')
- feedforward_grad: float32 [2, 2, 1024, 4096], P('section', None, None, 'tensor')
- gain_grad: float32 [2, 3, 1024], P('section')
- shift_grad: float32 [2, 3, 1024], P('section')
Inputs may be any that keep to these rules, and one draw needn't show every extreme that they name: In each pack the ids start at 0, never fall and rise by at most one from token to token; decoder_segments of a pack hold exactly the ids of encoder_segments of that pack, each at least once; among the 2 packs of each index of dp one holds a single item, and some pack holds four items. `decoder_segments`: ids as in encoder_segments, with the same items per pack.
All inputs are finite; a program needn't handle non-finite values.
Results may differ from a plain program's by a relative error of at most 0.034.
Values may be sent and summed in bfloat16 or wider, within the bound.
A program may use at most 128 MiB of HBM per device.

v0:
```python
import jax
import jax.numpy as jnp
from jax import lax
from jax.sharding import PartitionSpec as P

HEAD = 64


EPSILON = 1e-05
MASKED = -1000000000.0


def passed_along(value, axis, steps):
    count = lax.axis_size(axis)
    initial, last = (max(0, -steps), min(count, count - steps))
    return lax.ppermute(value, axis, [(source, source + steps) for source in range(initial, last)])


def norm_rows(values, gains, shifts):
    center = values - jnp.mean(values, -1, keepdims=True)
    variance = jnp.mean(center * center, -1, keepdims=True)
    return center * lax.rsqrt(variance + EPSILON) * gains + shifts


def gelu_exact(values):
    return jax.nn.gelu(values, approximate=False)


def gather_rows(values):
    return lax.all_gather(values, "tensor", axis=0, tiled=True)


def sum_rows(values):
    return lax.psum_scatter(
        values.astype(jnp.bfloat16), "tensor", scatter_dimension=0, tiled=True
    ).astype(jnp.float32)


def by_head(values):
    return values.reshape(values.shape[0], -1, HEAD)


def scores_of(queries, key_rows, allowed):
    scores = jnp.einsum(
        "qhd,khd->hqk", by_head(queries), by_head(key_rows), preferred_element_type=jnp.float32
    )
    return jnp.where(allowed[None], scores * HEAD ** (-0.5), MASKED)


def attend(queries, key_rows, value_rows, allowed):
    scores = scores_of(queries, key_rows, allowed)
    row_max = jnp.max(scores, -1, keepdims=True)
    exponent = jnp.exp(scores - row_max)
    row_sum = jnp.sum(exponent, -1, keepdims=True)
    probs_low = (exponent / row_sum).astype(jnp.bfloat16)
    attended = jnp.einsum(
        "hqk,khd->qhd", probs_low, by_head(value_rows), preferred_element_type=jnp.float32
    )
    log_total = (row_max + jnp.log(row_sum))[..., 0]
    return (attended.reshape(queries.shape[0], -1).astype(jnp.bfloat16), log_total)


def attend_back(queries, key_rows, value_rows, log_total, allowed, attended_grad):
    scores = scores_of(queries, key_rows, allowed)
    probs = jnp.exp(scores - log_total[..., None])
    probs_low = probs.astype(jnp.bfloat16)
    grad_heads = by_head(attended_grad)
    value_grad = jnp.einsum(
        "hqk,qhd->khd", probs_low, grad_heads, preferred_element_type=jnp.float32
    )
    probs_grad = jnp.einsum(
        "qhd,khd->hqk", grad_heads, by_head(value_rows), preferred_element_type=jnp.float32
    )
    scores_grad = (probs * (probs_grad - jnp.sum(probs * probs_grad, -1, keepdims=True))).astype(
        jnp.bfloat16
    )
    query_grad = jnp.einsum(
        "hqk,khd->qhd", scores_grad, by_head(key_rows), preferred_element_type=jnp.float32
    ) * HEAD ** (-0.5)
    key_grad = jnp.einsum(
        "hqk,qhd->khd", scores_grad, by_head(queries), preferred_element_type=jnp.float32
    ) * HEAD ** (-0.5)
    query_grad = query_grad.reshape(queries.shape[0], -1).astype(jnp.bfloat16)
    key_grad = key_grad.reshape(key_rows.shape[0], -1).astype(jnp.bfloat16)
    value_grad = value_grad.reshape(key_rows.shape[0], -1).astype(jnp.bfloat16)
    return (query_grad, key_grad, value_grad)


def project_in(full_rows, weights):
    return jnp.einsum("ld,sdh->slh", full_rows, weights, preferred_element_type=jnp.float32).astype(
        jnp.bfloat16
    )


def project_out(values, weights):
    return jnp.einsum("lh,dh->ld", values, weights, preferred_element_type=jnp.float32)


def weight_grad(full_rows, grads):
    return jnp.einsum("ld,lh->dh", full_rows, grads, preferred_element_type=jnp.float32)


def feedforward_back(full_back, full_in, ffn_mats):
    hidden_raw, gelu_pull = jax.vjp(
        gelu_exact, jnp.dot(full_in, ffn_mats[0], preferred_element_type=jnp.float32)
    )
    hidden = hidden_raw.astype(jnp.bfloat16)
    down_grad = weight_grad(full_back, hidden)
    pre_grad = gelu_pull(jnp.dot(full_back, ffn_mats[1], preferred_element_type=jnp.float32))[
        0
    ].astype(jnp.bfloat16)
    up_grad = weight_grad(full_in, pre_grad)
    return (pre_grad, up_grad, down_grad)


def encoder_forward(tokens, segment, weights, ffn_mats, gains, shifts):
    inputs = tokens.astype(jnp.float32)
    normed_zero = norm_rows(inputs, gains[0], shifts[0])
    full_zero = gather_rows(normed_zero.astype(jnp.bfloat16))
    projections = project_in(full_zero, weights[0:3])
    queries, key_rows, value_rows = (projections[0], projections[1], projections[2])
    allowed = segment[:, None] == segment[None, :]
    attended, log_total = attend(queries, key_rows, value_rows, allowed)
    inner_one = normed_zero + sum_rows(project_out(attended, weights[3]))
    normed_one = norm_rows(inner_one, gains[1], shifts[1])
    full_one = gather_rows(normed_one.astype(jnp.bfloat16))
    hidden = gelu_exact(jnp.dot(full_one, ffn_mats[0], preferred_element_type=jnp.float32)).astype(
        jnp.bfloat16
    )
    inner_two = normed_one + sum_rows(project_out(hidden, ffn_mats[1]))
    memory = norm_rows(inner_two, gains[2], shifts[2])
    full_two = gather_rows(memory.astype(jnp.bfloat16))
    cross_pair = project_in(full_two, weights[4:6])
    kept = (inner_one, inner_two, queries, key_rows, value_rows, attended, log_total)
    return (cross_pair, kept)


def encoder_backward(tokens, segment, weights, ffn_mats, gains, shifts, kept, pair_grad):
    inner_one, inner_two, queries, key_rows, value_rows, attended, log_total = kept[:7]
    inputs = tokens.astype(jnp.float32)
    allowed = segment[:, None] == segment[None, :]
    normed_zero, pull_zero = jax.vjp(norm_rows, inputs, gains[0], shifts[0])
    normed_one, pull_one = jax.vjp(norm_rows, inner_one, gains[1], shifts[1])
    memory, pull_two = jax.vjp(norm_rows, inner_two, gains[2], shifts[2])
    full_two = gather_rows(memory.astype(jnp.bfloat16))
    full_one = gather_rows(normed_one.astype(jnp.bfloat16))
    full_zero = gather_rows(normed_zero.astype(jnp.bfloat16))
    cross_key_grad = weight_grad(full_two, pair_grad[0])
    cross_value_grad = weight_grad(full_two, pair_grad[1])
    memory_grad = sum_rows(
        project_out(pair_grad[0], weights[4]) + project_out(pair_grad[1], weights[5])
    )
    two_grad, gain_two, shift_two = pull_two(memory_grad)
    full_back = gather_rows(two_grad.astype(jnp.bfloat16))
    pre_grad, up_grad, down_grad = feedforward_back(full_back, full_one, ffn_mats)
    one_grad, gain_one, shift_one = pull_one(
        two_grad + sum_rows(project_out(pre_grad, ffn_mats[0]))
    )
    full_mixed = gather_rows(one_grad.astype(jnp.bfloat16))
    attended_grad = jnp.dot(full_mixed, weights[3], preferred_element_type=jnp.float32).astype(
        jnp.bfloat16
    )
    output_grad = weight_grad(full_mixed, attended)
    query_grad, key_grad, value_grad = attend_back(
        queries, key_rows, value_rows, log_total, allowed, attended_grad
    )
    stacked = jnp.stack([query_grad, key_grad, value_grad])
    input_grads = jnp.einsum("ld,slh->sdh", full_zero, stacked, preferred_element_type=jnp.float32)
    back_rows = jnp.einsum("slh,sdh->ld", stacked, weights[0:3], preferred_element_type=jnp.float32)
    zero_grad, gain_zero, shift_zero = pull_zero(one_grad + sum_rows(back_rows))
    grads = (
        jnp.concatenate(
            [input_grads, output_grad[None], cross_key_grad[None], cross_value_grad[None]], 0
        ),
        jnp.stack([up_grad, down_grad]),
        jnp.stack([gain_zero, gain_one, gain_two]),
        jnp.stack([shift_zero, shift_one, shift_two]),
    )
    return (zero_grad, grads)


def decoder_pass(
    tokens, cotangent_rows, enc_segment, segment, pair_in, weights, ffn_mats, gains, shifts
):
    inputs = tokens.astype(jnp.float32)
    full_in = gather_rows(tokens)
    projections = project_in(full_in, weights[0:3])
    queries, key_rows, value_rows = (projections[0], projections[1], projections[2])
    position = jnp.arange(segment.shape[0])
    allowed = (segment[:, None] == segment[None, :]) & (position[:, None] >= position[None, :])
    attended, log_total = attend(queries, key_rows, value_rows, allowed)
    inner_zero = inputs + sum_rows(project_out(attended, weights[3]))
    normed_zero, pull_zero = jax.vjp(norm_rows, inner_zero, gains[0], shifts[0])
    full_zero = gather_rows(normed_zero.astype(jnp.bfloat16))
    cross_query = jnp.dot(full_zero, weights[4], preferred_element_type=jnp.float32).astype(
        jnp.bfloat16
    )
    cross_allowed = segment[:, None] == enc_segment[None, :]
    crossed, cross_total = attend(cross_query, pair_in[0], pair_in[1], cross_allowed)
    inner_one = normed_zero + sum_rows(project_out(crossed, weights[5]))
    normed_one, pull_one = jax.vjp(norm_rows, inner_one, gains[1], shifts[1])
    full_one = gather_rows(normed_one.astype(jnp.bfloat16))
    hidden = gelu_exact(jnp.dot(full_one, ffn_mats[0], preferred_element_type=jnp.float32)).astype(
        jnp.bfloat16
    )
    inner_two = normed_one + sum_rows(project_out(hidden, ffn_mats[1]))
    normed_two, pull_two = jax.vjp(norm_rows, inner_two, gains[2], shifts[2])
    two_grad, gain_two, shift_two = pull_two(cotangent_rows.astype(jnp.float32))
    full_back = gather_rows(two_grad.astype(jnp.bfloat16))
    pre_grad, up_grad, down_grad = feedforward_back(full_back, full_one, ffn_mats)
    one_grad, gain_one, shift_one = pull_one(
        two_grad + sum_rows(project_out(pre_grad, ffn_mats[0]))
    )
    full_cross = gather_rows(one_grad.astype(jnp.bfloat16))
    crossed_grad = jnp.dot(full_cross, weights[5], preferred_element_type=jnp.float32).astype(
        jnp.bfloat16
    )
    cross_out_grad = weight_grad(full_cross, crossed)
    cross_query_grad, cross_key_grad, cross_value_grad = attend_back(
        cross_query, pair_in[0], pair_in[1], cross_total, cross_allowed, crossed_grad
    )
    cross_in_grad = weight_grad(full_zero, cross_query_grad)
    zero_grad, gain_zero, shift_zero = pull_zero(
        one_grad + sum_rows(project_out(cross_query_grad, weights[4]))
    )
    full_mixed = gather_rows(zero_grad.astype(jnp.bfloat16))
    attended_grad = jnp.dot(full_mixed, weights[3], preferred_element_type=jnp.float32).astype(
        jnp.bfloat16
    )
    output_grad = weight_grad(full_mixed, attended)
    query_grad, key_grad, value_grad = attend_back(
        queries, key_rows, value_rows, log_total, allowed, attended_grad
    )
    stacked = jnp.stack([query_grad, key_grad, value_grad])
    input_grads = jnp.einsum("ld,slh->sdh", full_in, stacked, preferred_element_type=jnp.float32)
    back_rows = jnp.einsum("slh,sdh->ld", stacked, weights[0:3], preferred_element_type=jnp.float32)
    tokens_grad = zero_grad + sum_rows(back_rows)
    grads = (
        jnp.concatenate(
            [input_grads, output_grad[None], cross_in_grad[None], cross_out_grad[None]], 0
        ),
        jnp.stack([up_grad, down_grad]),
        jnp.stack([gain_zero, gain_one, gain_two]),
        jnp.stack([shift_zero, shift_one, shift_two]),
    )
    pair_grad = jnp.stack([cross_key_grad, cross_value_grad])
    return (normed_two.astype(jnp.bfloat16), tokens_grad, pair_grad, grads)


def on_device(
    encoder_tokens,
    encoder_segments,
    decoder_tokens,
    decoder_segments,
    cotangent,
    attention_weight,
    feedforward_weight,
    norm_gain,
    norm_shift,
):
    on_encoder = lax.axis_index("section") == 0
    weights = attention_weight[0]
    ffn_mats = feedforward_weight[0]
    gains = norm_gain[0]
    shifts = norm_shift[0]
    model_width = encoder_tokens.shape[2]
    head_width = weights.shape[2]
    ffn_width = ffn_mats.shape[2]

    def zero_grads():
        return (
            jnp.zeros((6, model_width, head_width), jnp.float32),
            jnp.zeros((2, model_width, ffn_width), jnp.float32),
            jnp.zeros((3, model_width), jnp.float32),
            jnp.zeros((3, model_width), jnp.float32),
        )

    def one_pack(sliced):
        return encoder_forward(sliced[0], sliced[1], weights, ffn_mats, gains, shifts)

    cross_pairs, kept_all = lax.map(one_pack, (encoder_tokens, encoder_segments))
    received = passed_along(cross_pairs, "section", 1)

    def decoder_step(carry, sliced):
        result, tokens_grad, pair_grad, grads = decoder_pass(
            sliced[0], sliced[1], sliced[2], sliced[3], sliced[4], weights, ffn_mats, gains, shifts
        )
        return (jax.tree.map(jnp.add, carry, grads), (pair_grad, result, tokens_grad))

    decoder_totals, decoder_outputs = lax.scan(
        decoder_step,
        zero_grads(),
        (decoder_tokens, cotangent, encoder_segments, decoder_segments, received),
    )
    pair_grads, results, decoder_grads = decoder_outputs
    returned = passed_along(pair_grads, "section", -1)

    def encoder_step(carry, sliced):
        tokens_grad, grads = encoder_backward(
            sliced[0], sliced[1], weights, ffn_mats, gains, shifts, sliced[3], sliced[2]
        )
        return (jax.tree.map(jnp.add, carry, grads), tokens_grad)

    encoder_totals, encoder_grads = lax.scan(
        encoder_step, zero_grads(), (encoder_tokens, encoder_segments, returned, kept_all)
    )
    totals = jax.tree.map(
        lambda from_encoder, from_decoder: jnp.where(on_encoder, from_encoder, from_decoder),
        encoder_totals,
        decoder_totals,
    )
    attention_sum, feedforward_sum = (
        lax.psum(totals[0].astype(jnp.bfloat16), "dp").astype(jnp.float32),
        lax.psum(totals[1].astype(jnp.bfloat16), "dp").astype(jnp.float32),
    )
    gain_sum, shift_sum = lax.psum((totals[2], totals[3]), ("dp", "tensor"))
    half_width = model_width // 2
    to_decoder = passed_along(
        encoder_grads[..., half_width:].astype(jnp.bfloat16), "section", 1
    ).astype(jnp.float32)
    outgoing = jnp.stack(
        [results.astype(jnp.float32)[..., :half_width], decoder_grads[..., :half_width]]
    )
    to_encoder = passed_along(outgoing.astype(jnp.bfloat16), "section", -1).astype(outgoing.dtype)
    encoder_grad = jnp.where(on_encoder, encoder_grads[..., :half_width], to_decoder)
    decoder_output = jnp.where(
        on_encoder, to_encoder[0].astype(jnp.bfloat16), results[..., half_width:]
    )
    decoder_grad = jnp.where(on_encoder, to_encoder[1], decoder_grads[..., half_width:])
    return (
        decoder_output,
        encoder_grad,
        decoder_grad,
        attention_sum[None],
        feedforward_sum[None],
        gain_sum[None],
        shift_sum[None],
    )


def solution(mesh):
    in_specs = (
        P("dp", "tensor", None),
        P("dp", None),
        P("dp", "tensor", None),
        P("dp", None),
        P("dp", "tensor", None),
        P("section", None, None, "tensor"),
        P("section", None, None, "tensor"),
        P("section", None, None),
        P("section", None, None),
    )
    out_specs = (
        P("dp", "tensor", "section"),
        P("dp", "tensor", "section"),
        P("dp", "tensor", "section"),
        P("section", None, None, "tensor"),
        P("section", None, None, "tensor"),
        P("section", None, None),
        P("section", None, None),
    )
    return jax.shard_map(
        on_device, mesh=mesh, in_specs=in_specs, out_specs=out_specs, check_vma=False
    )
```

profile of v0, /device:TPU:0, one launch (start us, length us, event | category | flops | bytes accessed | tf_op | source)
XLA Modules:
  0.0 3401.8 jit_solution(292176596049670340)
XLA Ops:
  10.5 639.1 %while.66 = (s32[]{:T(128)}, bf16[2,2,1280,64]{2,3,1,0:T(8,128)(2,1)}, f32[2,80,1024]{2,1,0:T(8,128)S(1)}, f32[2,80,1024]{2,1,0:T(8,128)S(1)}, bf16[2,1280,64]{1...) while((s32[]{:T(128)}, ...), condition=%wide.region_11.12_spmd, body=%wide.region_0.11_spmd.sunk | while | flops 2812640256 | bytes 101500880 | solution.py:281
  13.5 49.3 %all-gather.13.cloned.1.call-done = bf16[1280,1024]{1,0:T(8,128)(2,1)} async-done(((bf16[80,1024]{1,0:T(8,128)(2,1)}), bf16[1280,1024]{1,0:T(8,128)(2,1)}) %all-gather.13.cloned.1.call-update) | async-done | bytes 2621456 | tf_op jit(solution)/shard_map/while/body/eval_jaxpr/all_gather | solution.py:30
  72.2 74.6 %reduce-scatter.6.cloned.1.call-done = bf16[80,1024]{1,0:T(8,128)(2,1)} async-done(((bf16[1280,1024]{1,0:T(8,128)(2,1)}), bf16[80,1024]{1,0:T(8,128)(2,1)}) %reduce-scatter.6.cloned.1.call-update) | async-done | bytes 163856 | tf_op jit(solution)/shard_map/while/body/eval_jaxpr/reduce_scatter | solution.py:34
  151.1 45.5 %all-gather.15.cloned.1.call-done = bf16[1280,1024]{1,0:T(8,128)(2,1)} async-done(((bf16[80,1024]{1,0:T(8,128)(2,1)}), bf16[1280,1024]{1,0:T(8,128)(2,1)}) %all-gather.15.cloned.1.call-update) | async-done | bytes 2621456 | tf_op jit(solution)/shard_map/while/body/eval_jaxpr/all_gather | solution.py:30
  205.5 74.5 %reduce-scatter.8.cloned.1.call-done = bf16[80,1024]{1,0:T(8,128)(2,1)} async-done(((bf16[1280,1024]{1,0:T(8,128)(2,1)}), bf16[80,1024]{1,0:T(8,128)(2,1)}) %reduce-scatter.8.cloned.1.call-update) | async-done | bytes 163856 | tf_op jit(solution)/shard_map/while/body/eval_jaxpr/reduce_scatter | solution.py:34
  284.3 43.8 %all-gather.17.cloned.1.call-done = bf16[1280,1024]{1,0:T(8,128)(2,1)} async-done(((bf16[80,1024]{1,0:T(8,128)(2,1)}), bf16[1280,1024]{1,0:T(8,128)(2,1)}) %all-gather.17.cloned.1.call-update) | async-done | bytes 2621456 | tf_op jit(solution)/shard_map/while/body/eval_jaxpr/all_gather | solution.py:30
  334.7 45.9 %all-gather.13.cloned.1.call-done = bf16[1280,1024]{1,0:T(8,128)(2,1)} async-done(((bf16[80,1024]{1,0:T(8,128)(2,1)}), bf16[1280,1024]{1,0:T(8,128)(2,1)}) %all-gather.13.cloned.1.call-update) | async-done | bytes 2621456 | tf_op jit(solution)/shard_map/while/body/eval_jaxpr/all_gather | solution.py:30
  390.0 74.5 %reduce-scatter.6.cloned.1.call-done = bf16[80,1024]{1,0:T(8,128)(2,1)} async-done(((bf16[1280,1024]{1,0:T(8,128)(2,1)}), bf16[80,1024]{1,0:T(8,128)(2,1)}) %reduce-scatter.6.cloned.1.call-update) | async-done | bytes 163856 | tf_op jit(solution)/shard_map/while/body/eval_jaxpr/reduce_scatter | solution.py:34
  468.9 45.6 %all-gather.15.cloned.1.call-done = bf16[1280,1024]{1,0:T(8,128)(2,1)} async-done(((bf16[80,1024]{1,0:T(8,128)(2,1)}), bf16[1280,1024]{1,0:T(8,128)(2,1)}) %all-gather.15.cloned.1.call-update) | async-done | bytes 2621456 | tf_op jit(solution)/shard_map/while/body/eval_jaxpr/all_gather | solution.py:30
  523.3 74.6 %reduce-scatter.8.cloned.1.call-done = bf16[80,1024]{1,0:T(8,128)(2,1)} async-done(((bf16[1280,1024]{1,0:T(8,128)(2,1)}), bf16[80,1024]{1,0:T(8,128)(2,1)}) %reduce-scatter.8.cloned.1.call-update) | async-done | bytes 163856 | tf_op jit(solution)/shard_map/while/body/eval_jaxpr/reduce_scatter | solution.py:34
  602.1 43.8 %all-gather.17.cloned.1.call-done = bf16[1280,1024]{1,0:T(8,128)(2,1)} async-done(((bf16[80,1024]{1,0:T(8,128)(2,1)}), bf16[1280,1024]{1,0:T(8,128)(2,1)}) %all-gather.17.cloned.1.call-update) | async-done | bytes 2621456 | tf_op jit(solution)/shard_map/while/body/eval_jaxpr/all_gather | solution.py:30
  668.0 1349.7 %while.67 = (s32[]{:T(128)}, f32[6,1024,64]{1,2,0:T(8,128)}, f32[2,1024,256]{2,1,0:T(8,128)}, f32[3,1024]{1,0:T(4,128)}, f32[3,1024]{1,0:T(4,128)}, /*index=5*/b...) while((s32[]{:T(128)}, f32[6,1024,64]{1,2,0:T(8,128)}, ...), condition=%wide.region_43.44_spmd.clone, body=%wide.region_12.43_spmd.clone.sunk | while | flops 860235456 | bytes 59591896 | solution.py:290
  699.0 78.5 %all-reduce.30.cloned.1.call-done = bf16[128,1024]{1,0:T(8,128)(2,1)} async-done(((bf16[128,1024]{1,0:T(8,128)(2,1)}), bf16[128,1024]{1,0:T(8,128)(2,1)}) %all-reduce.30.cloned.1.call-update) | async-done | bytes 262160 | tf_op jit(solution)/shard_map/while
  808.4 82.6 %all-reduce.32.cloned.1.call-done = bf16[128,1024]{1,0:T(8,128)(2,1)} async-done(((bf16[128,1024]{1,0:T(8,128)(2,1)}), bf16[128,1024]{1,0:T(8,128)(2,1)}) %all-reduce.32.cloned.1.call-update) | async-done | bytes 262160 | tf_op jit(solution)/shard_map/while
  892.9 23.0 all_gather.69
  921.9 79.6 %all-reduce.34.cloned.1.call-done = bf16[128,1024]{1,0:T(8,128)(2,1)} async-done(((bf16[128,1024]{1,0:T(8,128)(2,1)}), bf16[128,1024]{1,0:T(8,128)(2,1)}) %all-reduce.34.cloned.1.call-update) | async-done | bytes 262160 | tf_op jit(solution)/shard_map/while
  1037.6 79.0 %all-reduce.36.cloned.1.call-done = bf16[128,1024]{1,0:T(8,128)(2,1)} async-done(((bf16[128,1024]{1,0:T(8,128)(2,1)}), bf16[128,1024]{1,0:T(8,128)(2,1)}) %all-reduce.36.cloned.1.call-update) | async-done | bytes 262160 | tf_op jit(solution)/shard_map/while
  1119.7 23.0 all_gather.71
  1149.0 81.7 %all-reduce.38.cloned.1.call-done = bf16[128,1024]{1,0:T(8,128)(2,1)} async-done(((bf16[128,1024]{1,0:T(8,128)(2,1)}), bf16[128,1024]{1,0:T(8,128)(2,1)}) %all-reduce.38.cloned.1.call-update) | async-done | bytes 262160 | tf_op jit(solution)/shard_map/while
  1232.8 23.0 all_gather.72
  1261.5 80.0 %all-reduce.40.cloned.1.call-done = bf16[128,1024]{1,0:T(8,128)(2,1)} async-done(((bf16[128,1024]{1,0:T(8,128)(2,1)}), bf16[128,1024]{1,0:T(8,128)(2,1)}) %all-reduce.40.cloned.1.call-update) | async-done | bytes 262160 | tf_op jit(solution)/shard_map/while
  1374.6 77.6 %all-reduce.30.cloned.1.call-done = bf16[128,1024]{1,0:T(8,128)(2,1)} async-done(((bf16[128,1024]{1,0:T(8,128)(2,1)}), bf16[128,1024]{1,0:T(8,128)(2,1)}) %all-reduce.30.cloned.1.call-update) | async-done | bytes 262160 | tf_op jit(solution)/shard_map/while
  1483.1 82.6 %all-reduce.32.cloned.1.call-done = bf16[128,1024]{1,0:T(8,128)(2,1)} async-done(((bf16[128,1024]{1,0:T(8,128)(2,1)}), bf16[128,1024]{1,0:T(8,128)(2,1)}) %all-reduce.32.cloned.1.call-update) | async-done | bytes 262160 | tf_op jit(solution)/shard_map/while
  1596.6 79.6 %all-reduce.34.cloned.1.call-done = bf16[128,1024]{1,0:T(8,128)(2,1)} async-done(((bf16[128,1024]{1,0:T(8,128)(2,1)}), bf16[128,1024]{1,0:T(8,128)(2,1)}) %all-reduce.34.cloned.1.call-update) | async-done | bytes 262160 | tf_op jit(solution)/shard_map/while
  1680.3 23.0 all_gather.70
  1713.0 78.3 %all-reduce.36.cloned.1.call-done = bf16[128,1024]{1,0:T(8,128)(2,1)} async-done(((bf16[128,1024]{1,0:T(8,128)(2,1)}), bf16[128,1024]{1,0:T(8,128)(2,1)}) %all-reduce.36.cloned.1.call-update) | async-done | bytes 262160 | tf_op jit(solution)/shard_map/while
  1794.4 23.0 all_gather.71
  1823.8 81.7 %all-reduce.38.cloned.1.call-done = bf16[128,1024]{1,0:T(8,128)(2,1)} async-done(((bf16[128,1024]{1,0:T(8,128)(2,1)}), bf16[128,1024]{1,0:T(8,128)(2,1)}) %all-reduce.38.cloned.1.call-update) | async-done | bytes 262160 | tf_op jit(solution)/shard_map/while
  1907.5 23.0 all_gather.72
  1936.8 79.4 %all-reduce.40.cloned.1.call-done = bf16[128,1024]{1,0:T(8,128)(2,1)} async-done(((bf16[128,1024]{1,0:T(8,128)(2,1)}), bf16[128,1024]{1,0:T(8,128)(2,1)}) %all-reduce.40.cloned.1.call-update) | async-done | bytes 262160 | tf_op jit(solution)/shard_map/while
  2036.0 1009.4 %while.68 = (s32[]{:T(128)}, f32[6,1024,64]{1,2,0:T(8,128)}, f32[2,1024,256]{2,1,0:T(8,128)}, f32[3,1024]{1,0:T(4,128)}, f32[3,1024]{1,0:T(4,128)}, /*index=5*/f...) while((s32[]{:T(128)}, f32[6,1024,64]{1,2,0:T(8,128)}, ...), condition=%wide.region_67.68_spmd.clone, body=%wide.region_44.67_spmd.clone.sunk | while | flops 6496537088 | bytes 298257984 | solution.py:304
  2061.1 70.1 %reduce-scatter.10.cloned.1.call-done = bf16[80,1024]{1,0:T(8,128)(2,1)} async-done(((bf16[1280,1024]{1,0:T(8,128)(2,1)}), bf16[80,1024]{1,0:T(8,128)(2,1)}) %reduce-scatter.10.cloned.1.call-update) | async-done | bytes 163856 | tf_op jit(solution)/shard_map/while/body/eval_jaxpr/reduce_scatter | solution.py:34
  2135.6 43.1 %all-gather.21.cloned.1.call-done = bf16[1280,1024]{1,0:T(8,128)(2,1)} async-done(((bf16[80,1024]{1,0:T(8,128)(2,1)}), bf16[1280,1024]{1,0:T(8,128)(2,1)}) %all-gather.21.cloned.1.call-update) | async-done | bytes 2621456 | tf_op jit(solution)/shard_map/while/body/eval_jaxpr/all_gather | solution.py:30
  2182.6 43.8 %all-gather.23.cloned.1.call-done = bf16[1280,1024]{1,0:T(8,128)(2,1)} async-done(((bf16[80,1024]{1,0:T(8,128)(2,1)}), bf16[1280,1024]{1,0:T(8,128)(2,1)}) %all-gather.23.cloned.1.call-update) | async-done | bytes 2621456 | tf_op jit(solution)/shard_map/while/body/eval_jaxpr/all_gather | solution.py:30
  2235.8 74.5 %reduce-scatter.12.cloned.1.call-done = bf16[80,1024]{1,0:T(8,128)(2,1)} async-done(((bf16[1280,1024]{1,0:T(8,128)(2,1)}), bf16[80,1024]{1,0:T(8,128)(2,1)}) %reduce-scatter.12.cloned.1.call-update) | async-done | bytes 163856 | tf_op jit(solution)/shard_map/while/body/eval_jaxpr/reduce_scatter | solution.py:34
  2315.0 44.8 %all-gather.25.cloned.1.call-done = bf16[1280,1024]{1,0:T(8,128)(2,1)} async-done(((bf16[80,1024]{1,0:T(8,128)(2,1)}), bf16[1280,1024]{1,0:T(8,128)(2,1)}) %all-gather.25.cloned.1.call-update) | async-done | bytes 2621456 | tf_op jit(solution)/shard_map/while/body/eval_jaxpr/all_gather | solution.py:30
  2375.4 73.6 %reduce-scatter.14.cloned.1.call-done = bf16[80,1024]{1,0:T(8,128)(2,1)} async-done(((bf16[1280,1024]{1,0:T(8,128)(2,1)}), bf16[80,1024]{1,0:T(8,128)(2,1)}) %reduce-scatter.14.cloned.1.call-update) | async-done | bytes 163856 | tf_op jit(solution)/shard_map/while/body/eval_jaxpr/reduce_scatter | solution.py:34
  2451.4 45.3 %all-gather.19.cloned.1.call-done = bf16[1280,1024]{1,0:T(8,128)(2,1)} async-done(((bf16[80,1024]{1,0:T(8,128)(2,1)}), bf16[1280,1024]{1,0:T(8,128)(2,1)}) %all-gather.19.cloned.1.call-update) | async-done | bytes 2621456 | tf_op jit(solution)/shard_map/while/body/eval_jaxpr/all_gather | solution.py:30
  2510.5 33.6 all-gather.27.cloned.1.call-done
  2557.6 70.6 %reduce-scatter.10.cloned.1.call-done = bf16[80,1024]{1,0:T(8,128)(2,1)} async-done(((bf16[1280,1024]{1,0:T(8,128)(2,1)}), bf16[80,1024]{1,0:T(8,128)(2,1)}) %reduce-scatter.10.cloned.1.call-update) | async-done | bytes 163856 | tf_op jit(solution)/shard_map/while/body/eval_jaxpr/reduce_scatter | solution.py:34
  2632.7 43.2 %all-gather.21.cloned.1.call-done = bf16[1280,1024]{1,0:T(8,128)(2,1)} async-done(((bf16[80,1024]{1,0:T(8,128)(2,1)}), bf16[1280,1024]{1,0:T(8,128)(2,1)}) %all-gather.21.cloned.1.call-update) | async-done | bytes 2621456 | tf_op jit(solution)/shard_map/while/body/eval_jaxpr/all_gather | solution.py:30
  2679.7 43.7 %all-gather.23.cloned.1.call-done = bf16[1280,1024]{1,0:T(8,128)(2,1)} async-done(((bf16[80,1024]{1,0:T(8,128)(2,1)}), bf16[1280,1024]{1,0:T(8,128)(2,1)}) %all-gather.23.cloned.1.call-update) | async-done | bytes 2621456 | tf_op jit(solution)/shard_map/while/body/eval_jaxpr/all_gather | solution.py:30
  2732.8 74.5 %reduce-scatter.12.cloned.1.call-done = bf16[80,1024]{1,0:T(8,128)(2,1)} async-done(((bf16[1280,1024]{1,0:T(8,128)(2,1)}), bf16[80,1024]{1,0:T(8,128)(2,1)}) %reduce-scatter.12.cloned.1.call-update) | async-done | bytes 163856 | tf_op jit(solution)/shard_map/while/body/eval_jaxpr/reduce_scatter | solution.py:34
  2812.0 44.8 %all-gather.25.cloned.1.call-done = bf16[1280,1024]{1,0:T(8,128)(2,1)} async-done(((bf16[80,1024]{1,0:T(8,128)(2,1)}), bf16[1280,1024]{1,0:T(8,128)(2,1)}) %all-gather.25.cloned.1.call-update) | async-done | bytes 2621456 | tf_op jit(solution)/shard_map/while/body/eval_jaxpr/all_gather | solution.py:30
  2872.2 73.8 %reduce-scatter.14.cloned.1.call-done = bf16[80,1024]{1,0:T(8,128)(2,1)} async-done(((bf16[1280,1024]{1,0:T(8,128)(2,1)}), bf16[80,1024]{1,0:T(8,128)(2,1)}) %reduce-scatter.14.cloned.1.call-update) | async-done | bytes 163856 | tf_op jit(solution)/shard_map/while/body/eval_jaxpr/reduce_scatter | solution.py:34
  2948.3 45.2 %all-gather.19.cloned.1.call-done = bf16[1280,1024]{1,0:T(8,128)(2,1)} async-done(((bf16[80,1024]{1,0:T(8,128)(2,1)}), bf16[1280,1024]{1,0:T(8,128)(2,1)}) %all-gather.19.cloned.1.call-update) | async-done | bytes 2621456 | tf_op jit(solution)/shard_map/while/body/eval_jaxpr/all_gather | solution.py:30
  3007.4 33.8 all-gather.27.cloned.1.call-done
  3061.2 326.7 %all-reduce.6 = (f32[1,3,1024]{2,1,0:T(4,128)S(1)}, f32[1,3,1024]{2,0,1:T(1,128)}) all-reduce(f32[1,3,1024]{2,1,0:T(4,128)S(1)} %select_bitcast_fusion, f32[1,3,1024]{2,0,1:T(1,128)S(1)} %broadcast_in_dim.182), channel_id=1, replica_groups=mesh['section'=2,'dp'=4,'tensor'=16] {'dp','tensor'}, use_global_device_ids=true, to_apply=%region_70.71 | all-reduce | flops 6144 | bytes 49152 | tf_op jit(solution)/shard_map/psum | solution.py:316
  (891 shorter events, 509.6 us)
Async XLA Ops:
  10.5 657.4 %copy-start.28 = (bf16[2,8,1024]{2,1,0:T(8,128)(2,1)S(1)}, bf16[2,8,1024]{2,1,0:T(8,128)(2,1)}, u32[]{:S(2)}) copy-start(bf16[2,8,1024]{2,1,0:T(8,128)(2,1)} %param.17) | copy-start | bytes 98308
  10.5 657.4 %copy-start.113 = (u32[128]{0:T(128)S(1)}, u32[128]{0:T(128)}, u32[]{:S(2)}) copy-start(u32[128]{0:T(128)} %constant.763) | copy-start | bytes 1540
  10.6 52.2 %all-gather.13.cloned.1.call-start = ((), (), s32[]{:S(2)}) async-start(), calls=%async_computation.6 | async-start | bytes 2785280 | tf_op jit(solution)/shard_map/while/body/eval_jaxpr/all_gather | solution.py:30
  12.7 134.0 %reduce-scatter.6.cloned.1.call-start = ((), (), s32[]{:S(2)}) async-start(), calls=%async_computation.7 | async-start | bytes 2785280 | tf_op jit(solution)/shard_map/while/body/eval_jaxpr/reduce_scatter | solution.py:34
  72.1 124.5 %all-gather.15.cloned.1.call-start = ((), (), s32[]{:S(2)}) async-start(), calls=%async_computation.8 | async-start | bytes 2785280 | tf_op jit(solution)/shard_map/while/body/eval_jaxpr/all_gather | solution.py:30
  151.0 129.0 %reduce-scatter.8.cloned.1.call-start = ((), (), s32[]{:S(2)}) async-start(), calls=%async_computation.9 | async-start | bytes 2785280 | tf_op jit(solution)/shard_map/while/body/eval_jaxpr/reduce_scatter | solution.py:34
  205.5 122.6 %all-gather.17.cloned.1.call-start = ((), (), s32[]{:S(2)}) async-start(), calls=%async_computation.10 | async-start | bytes 2785280 | tf_op jit(solution)/shard_map/while/body/eval_jaxpr/all_gather | solution.py:30
  331.8 48.8 %all-gather.13.cloned.1.call-start = ((), (), s32[]{:S(2)}) async-start(), calls=%async_computation.6 | async-start | bytes 2785280 | tf_op jit(solution)/shard_map/while/body/eval_jaxpr/all_gather | solution.py:30
  333.9 130.6 %reduce-scatter.6.cloned.1.call-start = ((), (), s32[]{:S(2)}) async-start(), calls=%async_computation.7 | async-start | bytes 2785280 | tf_op jit(solution)/shard_map/while/body/eval_jaxpr/reduce_scatter | solution.py:34
  389.9 124.5 %all-gather.15.cloned.1.call-start = ((), (), s32[]{:S(2)}) async-start(), calls=%async_computation.8 | async-start | bytes 2785280 | tf_op jit(solution)/shard_map/while/body/eval_jaxpr/all_gather | solution.py:30
  468.8 129.1 %reduce-scatter.8.cloned.1.call-start = ((), (), s32[]{:S(2)}) async-start(), calls=%async_computation.9 | async-start | bytes 2785280 | tf_op jit(solution)/shard_map/while/body/eval_jaxpr/reduce_scatter | solution.py:34
  523.3 122.6 %all-gather.17.cloned.1.call-start = ((), (), s32[]{:S(2)}) async-start(), calls=%async_computation.10 | async-start | bytes 2785280 | tf_op jit(solution)/shard_map/while/body/eval_jaxpr/all_gather | solution.py:30
  649.7 17.4 collective-permute-start
  667.9 1368.0 %copy-start.3 = (bf16[2,80,1024]{2,1,0:T(8,128)(2,1)S(1)}, bf16[2,80,1024]{2,1,0:T(8,128)(2,1)}, u32[]{:S(2)}) copy-start(bf16[2,80,1024]{2,1,0:T(8,128)(2,1)} %param.15) | copy-start | bytes 983044
  668.0 109.5 %all-reduce.30.cloned.1.call-start = ((), (), s32[]{:S(2)}) async-start(), calls=%async_computation.11 | async-start | bytes 524288 | tf_op jit(solution)/shard_map/while
  693.9 197.0 %all-reduce.32.cloned.1.call-start = ((), (), s32[]{:S(2)}) async-start(), calls=%async_computation.12 | async-start | bytes 524288 | tf_op jit(solution)/shard_map/while
  808.3 193.1 %all-reduce.34.cloned.1.call-start = ((), (), s32[]{:S(2)}) async-start(), calls=%async_computation.13 | async-start | bytes 524288 | tf_op jit(solution)/shard_map/while
  918.8 197.8 %all-reduce.36.cloned.1.call-start = ((), (), s32[]{:S(2)}) async-start(), calls=%async_computation.14 | async-start | bytes 524288 | tf_op jit(solution)/shard_map/while
  1033.9 196.8 %all-reduce.38.cloned.1.call-start = ((), (), s32[]{:S(2)}) async-start(), calls=%async_computation.15 | async-start | bytes 524288 | tf_op jit(solution)/shard_map/while
  1148.1 193.4 %all-reduce.40.cloned.1.call-start = ((), (), s32[]{:S(2)}) async-start(), calls=%async_computation.16 | async-start | bytes 524288 | tf_op jit(solution)/shard_map/while
  1342.9 109.3 %all-reduce.30.cloned.1.call-start = ((), (), s32[]{:S(2)}) async-start(), calls=%async_computation.11 | async-start | bytes 524288 | tf_op jit(solution)/shard_map/while
  1369.6 196.1 %all-reduce.32.cloned.1.call-start = ((), (), s32[]{:S(2)}) async-start(), calls=%async_computation.12 | async-start | bytes 524288 | tf_op jit(solution)/shard_map/while
  1483.1 193.1 %all-reduce.34.cloned.1.call-start = ((), (), s32[]{:S(2)}) async-start(), calls=%async_computation.13 | async-start | bytes 524288 | tf_op jit(solution)/shard_map/while
  1593.5 197.8 %all-reduce.36.cloned.1.call-start = ((), (), s32[]{:S(2)}) async-start(), calls=%async_computation.14 | async-start | bytes 524288 | tf_op jit(solution)/shard_map/while
  1708.7 196.8 %all-reduce.38.cloned.1.call-start = ((), (), s32[]{:S(2)}) async-start(), calls=%async_computation.15 | async-start | bytes 524288 | tf_op jit(solution)/shard_map/while
  1822.8 193.4 %all-reduce.40.cloned.1.call-start = ((), (), s32[]{:S(2)}) async-start(), calls=%async_computation.16 | async-start | bytes 524288 | tf_op jit(solution)/shard_map/while
  2017.6 17.4 collective-permute-start.2
  2051.8 260.3 %copy-start.5 = (f32[2,80,1024]{2,1,0:T(8,128)}, f32[2,80,1024]{2,1,0:T(8,128)S(1)}, u32[]{:S(2)}) copy-start(f32[2,80,1024]{2,1,0:T(8,128)S(1)} %get-tuple-element.1346) | copy-start | bytes 1966084 | tf_op jit(solution)/shard_map/while
  2051.8 79.5 %reduce-scatter.10.cloned.1.call-start = ((), (), s32[]{:S(2)}) async-start(), calls=%async_computation.17 | async-start | bytes 2785280 | tf_op jit(solution)/shard_map/while/body/eval_jaxpr/reduce_scatter | solution.py:34
  2057.2 121.6 %all-gather.21.cloned.1.call-start = ((), (), s32[]{:S(2)}) async-start(), calls=%async_computation.19 | async-start | bytes 2785280 | tf_op jit(solution)/shard_map/while/body/eval_jaxpr/all_gather | solution.py:30
  2060.7 165.7 %all-gather.23.cloned.1.call-start = ((), (), s32[]{:S(2)}) async-start(), calls=%async_computation.20 | async-start | bytes 2785280 | tf_op jit(solution)/shard_map/while/body/eval_jaxpr/all_gather | solution.py:30
  2135.6 174.8 %reduce-scatter.12.cloned.1.call-start = ((), (), s32[]{:S(2)}) async-start(), calls=%async_computation.21 | async-start | bytes 2785280 | tf_op jit(solution)/shard_map/while/body/eval_jaxpr/reduce_scatter | solution.py:34
  2235.8 124.0 %all-gather.25.cloned.1.call-start = ((), (), s32[]{:S(2)}) async-start(), calls=%async_computation.22 | async-start | bytes 2785280 | tf_op jit(solution)/shard_map/while/body/eval_jaxpr/all_gather | solution.py:30
  2314.1 134.9 %reduce-scatter.14.cloned.1.call-start = ((), (), s32[]{:S(2)}) async-start(), calls=%async_computation.23 | async-start | bytes 2785280 | tf_op jit(solution)/shard_map/while/body/eval_jaxpr/reduce_scatter | solution.py:34
  2374.5 122.1 %all-gather.19.cloned.1.call-start = ((), (), s32[]{:S(2)}) async-start(), calls=%async_computation.18 | async-start | bytes 2785280 | tf_op jit(solution)/shard_map/while/body/eval_jaxpr/all_gather | solution.py:30
  2375.2 168.9 %all-gather.27.cloned.1.call-start = ((), (), s32[]{:S(2)}) async-start(), calls=%async_computation.24 | async-start | bytes 2785280 | tf_op jit(solution)/shard_map/while/body/eval_jaxpr/all_gather | solution.py:30
  2548.4 260.7 %copy-start.5 = (f32[2,80,1024]{2,1,0:T(8,128)}, f32[2,80,1024]{2,1,0:T(8,128)S(1)}, u32[]{:S(2)}) copy-start(f32[2,80,1024]{2,1,0:T(8,128)S(1)} %get-tuple-element.1346) | copy-start | bytes 1966084 | tf_op jit(solution)/shard_map/while
  2548.4 79.9 %reduce-scatter.10.cloned.1.call-start = ((), (), s32[]{:S(2)}) async-start(), calls=%async_computation.17 | async-start | bytes 2785280 | tf_op jit(solution)/shard_map/while/body/eval_jaxpr/reduce_scatter | solution.py:34
  2553.7 122.2 %all-gather.21.cloned.1.call-start = ((), (), s32[]{:S(2)}) async-start(), calls=%async_computation.19 | async-start | bytes 2785280 | tf_op jit(solution)/shard_map/while/body/eval_jaxpr/all_gather | solution.py:30
  2557.2 166.2 %all-gather.23.cloned.1.call-start = ((), (), s32[]{:S(2)}) async-start(), calls=%async_computation.20 | async-start | bytes 2785280 | tf_op jit(solution)/shard_map/while/body/eval_jaxpr/all_gather | solution.py:30
  2632.6 174.7 %reduce-scatter.12.cloned.1.call-start = ((), (), s32[]{:S(2)}) async-start(), calls=%async_computation.21 | async-start | bytes 2785280 | tf_op jit(solution)/shard_map/while/body/eval_jaxpr/reduce_scatter | solution.py:34
  2732.8 123.9 %all-gather.25.cloned.1.call-start = ((), (), s32[]{:S(2)}) async-start(), calls=%async_computation.22 | async-start | bytes 2785280 | tf_op jit(solution)/shard_map/while/body/eval_jaxpr/all_gather | solution.py:30
  2811.1 134.9 %reduce-scatter.14.cloned.1.call-start = ((), (), s32[]{:S(2)}) async-start(), calls=%async_computation.23 | async-start | bytes 2785280 | tf_op jit(solution)/shard_map/while/body/eval_jaxpr/reduce_scatter | solution.py:34
  2871.4 122.1 %all-gather.19.cloned.1.call-start = ((), (), s32[]{:S(2)}) async-start(), calls=%async_computation.18 | async-start | bytes 2785280 | tf_op jit(solution)/shard_map/while/body/eval_jaxpr/all_gather | solution.py:30
  2872.0 169.2 %all-gather.27.cloned.1.call-start = ((), (), s32[]{:S(2)}) async-start(), calls=%async_computation.24 | async-start | bytes 2785280 | tf_op jit(solution)/shard_map/while/body/eval_jaxpr/all_gather | solution.py:30
  3045.4 344.9 %all-reduce.28.cloned.1.call-start = ((), (), s32[]{:S(2)}) async-start(), calls=%async_computation.5 | async-start | bytes 3670016 | tf_op jit(solution)/shard_map/psum | solution.py:313
  3050.3 6.3 collective-permute-start.1
  3059.6 329.0 %collective-permute-start.3 = (bf16[2,80,512]{2,1,0:T(8,128)(2,1)S(1)}, bf16[2,80,512]{2,1,0:T(8,128)(2,1)S(1)}, u32[]{:S(2)}, u32[]{:S(2)}) collective-permute-start(bf16[2,80,512]{2,1,0:T(8,128)(2,1)S(1)} %slice.350), channel_id=1, source_target_pairs={{0,64},{1,65},{2,66},{3,67},{4,68},{5,69},{6,70},{7,71},{8,72},{9,... | collective-permute-start | bytes 491528 | tf_op jit(solution)/shard_map/ppermute | solution.py:16
  (212 other events, 5617.3 us)
Sparse Core Ops, SparseCore 0:
  14.1 48.6 all-gather.12
  72.2 74.4 reduce-scatter.5
  151.2 45.4 all-gather.14
  205.6 74.4 reduce-scatter.7
  282.6 45.4 all-gather.16
  335.1 45.4 all-gather.12
  390.1 74.4 reduce-scatter.5
  468.9 45.4 all-gather.14
  523.4 74.4 reduce-scatter.7
  600.5 45.4 all-gather.16
  694.1 83.3 all-reduce.29
  808.4 82.4 all-reduce.31
  918.9 82.5 all-reduce.33
  1034.0 82.4 all-reduce.35
  1148.1 82.5 all-reduce.37
  1259.0 82.4 all-reduce.39
  1369.7 82.4 all-reduce.29
  1483.2 82.4 all-reduce.31
  1593.6 82.5 all-reduce.33
  1708.8 82.4 all-reduce.35
  1822.9 82.5 all-reduce.37
  1933.7 82.4 all-reduce.39
  2057.3 73.9 reduce-scatter.9
  2133.2 45.4 all-gather.20
  2180.9 45.4 all-gather.22
  2235.9 74.4 reduce-scatter.11
  2314.3 45.4 all-gather.24
  2374.6 74.3 reduce-scatter.13
  2451.2 45.4 all-gather.18
  2498.6 45.4 all-gather.26
  2553.8 74.4 reduce-scatter.9
  2630.4 45.4 all-gather.20
  2677.9 45.4 all-gather.22
  2732.9 74.4 reduce-scatter.11
  2811.2 45.4 all-gather.24
  2871.5 74.4 reduce-scatter.13
  2948.0 45.4 all-gather.18
  2995.6 45.4 all-gather.26
Sparse Core Ops, SparseCore 1:
  3049.5 57.6 all-reduce.27
where the time goes:
time: 3420 us; the launch traced here: 3400 us
  waiting for transfers between devices  2430 us (71%)
  blocking collectives  602 us (18%)
  matrix products  162 us (5%)
  other arithmetic  109 us (3%)
  local copies, waits for them, and re-layouts  55.2 us (2%)
    while x50, waiting for transfers between devices  962 us
    reduce_scatter x10, waiting for transfers between devices, sum_rows(): lax.psum_scatter(values.astype(jnp.bfloat16), 'tensor', scatter_dimension...  735 us
    all_gather x16, waiting for transfers between devices, gather_rows(): return lax.all_gather(values, 'tensor', axis=0, tiled=True)  695 us
    psum x1, blocking collectives, on_device(): gain_sum, shift_sum = lax.psum((totals[2], totals[3]), ('dp', 'tensor'))  327 us
    all_gather x12, blocking collectives, gather_rows(): return lax.all_gather(values, 'tensor', axis=0, tiled=True)  275 us
  transfers between devices with their start and end apart: 43, of which 41 were waited for; matrix products, arithmetic and copies ran while one was open for 3% of the time, Pallas kernels for 0%

commit v1 on v0

v1 whole, which is shorter than its diff:
```python
import jax
import jax.numpy as jnp
from jax import lax
from jax.sharding import PartitionSpec as P

HEAD = 64
EPSILON = 1e-05
MASKED = -1000000000.0
F32 = jnp.float32
BF16 = jnp.bfloat16


def swapped(value, axis):
    return lax.ppermute(value, axis, [(0, 1), (1, 0)])


def norm_parts(values):
    center = values - jnp.mean(values, -1, keepdims=True)
    scale = lax.rsqrt(jnp.mean(center * center, -1, keepdims=True) + EPSILON)
    return center * scale, scale


def norm_back(grad, unit, scale, gains):
    inner = grad * gains
    back = scale * (
        inner
        - jnp.mean(inner, -1, keepdims=True)
        - unit * jnp.mean(inner * unit, -1, keepdims=True)
    )
    return back, jnp.sum(grad * unit, 0), jnp.sum(grad, 0)


def gelu_exact(values):
    return jax.nn.gelu(values, approximate=False)


def gather_rows(values):
    return lax.all_gather(values.astype(BF16), "tensor", axis=0, tiled=True)


def sum_rows(values):
    return lax.psum_scatter(
        values.astype(BF16), "tensor", scatter_dimension=0, tiled=True
    ).astype(F32)


def gather_both(enc, dec):
    size, ra, rb = lax.axis_size("tensor"), enc.shape[0], dec.shape[0]
    full = gather_rows(jnp.concatenate([enc, dec], 0)).reshape(size, ra + rb, -1)
    return full[:, :ra].reshape(size * ra, -1), full[:, ra:].reshape(size * rb, -1)


def sum_both(enc, dec):
    size = lax.axis_size("tensor")
    ra, rb = enc.shape[0] // size, dec.shape[0] // size
    both = jnp.concatenate(
        [enc.astype(BF16).reshape(size, ra, -1), dec.astype(BF16).reshape(size, rb, -1)], 1
    )
    mine = sum_rows(both.reshape(size * (ra + rb), -1))
    return mine[:ra], mine[ra:]


def dot(a, b):
    return jnp.dot(a, b, preferred_element_type=F32)


def dot_t(a, b):
    return lax.dot_general(a, b, (((1,), (1,)), ((), ())), preferred_element_type=F32)


def t_dot(a, b):
    return lax.dot_general(a, b, (((0,), (0,)), ((), ())), preferred_element_type=F32)


def scores_of(queries, key_rows, allowed):
    return jnp.where(allowed, dot_t(queries, key_rows) * HEAD ** (-0.5), MASKED)


def attend(queries, key_rows, value_rows, allowed):
    scores = scores_of(queries, key_rows, allowed)
    row_max = jnp.max(scores, -1, keepdims=True)
    exponent = jnp.exp(scores - row_max)
    row_sum = jnp.sum(exponent, -1, keepdims=True)
    probs_low = (exponent / row_sum).astype(BF16)
    return dot(probs_low, value_rows).astype(BF16), row_max + jnp.log(row_sum)


def attend_back(queries, key_rows, value_rows, log_total, allowed, attended_grad):
    scores = scores_of(queries, key_rows, allowed)
    probs = jnp.exp(scores - log_total)
    value_grad = t_dot(probs.astype(BF16), attended_grad)
    probs_grad = dot_t(attended_grad, value_rows)
    scores_grad = (probs * (probs_grad - jnp.sum(probs * probs_grad, -1, keepdims=True))).astype(
        BF16
    )
    query_grad = dot(scores_grad, key_rows) * HEAD ** (-0.5)
    key_grad = t_dot(scores_grad, queries) * HEAD ** (-0.5)
    return query_grad.astype(BF16), key_grad.astype(BF16), value_grad.astype(BF16)


def feedforward_back(full_back, full_in, up, down):
    hidden_raw, gelu_pull = jax.vjp(gelu_exact, dot(full_in, up))
    hidden = hidden_raw.astype(BF16)
    down_grad = t_dot(full_back, hidden)
    pre_grad = gelu_pull(dot(full_back, down))[0].astype(BF16)
    up_grad = t_dot(full_in, pre_grad)
    return pre_grad, up_grad, down_grad


def slot(weights, first, last):
    return weights[:, first * HEAD : last * HEAD]


def on_device(
    encoder_tokens,
    encoder_segments,
    decoder_tokens,
    decoder_segments,
    cotangent,
    attention_weight,
    feedforward_weight,
    norm_gain,
    norm_shift,
):
    section = lax.axis_index("section")
    on_encoder = section == 0
    mine = lambda a: lax.dynamic_index_in_dim(a, section, 0, keepdims=False)

    def layers(own):
        other = swapped(own, "section")
        return jnp.where(on_encoder, own, other), jnp.where(on_encoder, other, own)

    own_attention = jnp.concatenate([attention_weight[0, j] for j in range(6)], 1)
    we, wd = layers(own_attention)
    fe, fd = layers(feedforward_weight[0])
    ge, gd = layers(norm_gain[0])
    se, sd = layers(norm_shift[0])

    x = mine(encoder_tokens).astype(F32)
    y = mine(decoder_tokens).astype(F32)
    cot = mine(cotangent).astype(F32)
    e = mine(encoder_segments)
    c = mine(decoder_segments)
    position = jnp.arange(c.shape[0])
    allow_e = e[:, None] == e[None, :]
    allow_d = (c[:, None] == c[None, :]) & (position[:, None] >= position[None, :])
    allow_c = c[:, None] == e[None, :]

    unit0, scale0 = norm_parts(x)
    h0 = unit0 * ge[0] + se[0]
    full_h0, full_y = gather_both(h0, y)
    qkv = dot(full_h0, slot(we, 0, 3)).astype(BF16)
    q, k, v = (slot(qkv, j, j + 1) for j in range(3))
    att_e, log_e = attend(q, k, v, allow_e)
    dqkv = dot(full_y, slot(wd, 0, 3)).astype(BF16)
    sq, sk, sv = (slot(dqkv, j, j + 1) for j in range(3))
    att_d, log_d = attend(sq, sk, sv, allow_d)
    part_e, part_d = sum_both(dot_t(att_e, slot(we, 3, 4)), dot_t(att_d, slot(wd, 3, 4)))
    unit1, scale1 = norm_parts(h0 + part_e)
    h1 = unit1 * ge[1] + se[1]
    dunit0, dscale0 = norm_parts(y + part_d)
    d1 = dunit0 * gd[0] + sd[0]
    full_h1, full_d1 = gather_both(h1, d1)
    hidden = gelu_exact(dot(full_h1, fe[0])).astype(BF16)
    cq = dot(full_d1, slot(wd, 4, 5)).astype(BF16)
    unit2, scale2 = norm_parts(h1 + sum_rows(dot_t(hidden, fe[1])))
    full_m = gather_rows(unit2 * ge[2] + se[2])
    kvc = dot(full_m, slot(we, 4, 6)).astype(BF16)
    kc, vc = slot(kvc, 0, 1), slot(kvc, 1, 2)

    att_c, log_c = attend(cq, kc, vc, allow_c)
    dunit1, dscale1 = norm_parts(d1 + sum_rows(dot_t(att_c, slot(wd, 5, 6))))
    d2 = dunit1 * gd[1] + sd[1]
    full_d2 = gather_rows(d2)
    dhidden = gelu_exact(dot(full_d2, fd[0])).astype(BF16)
    dunit2, dscale2 = norm_parts(d2 + sum_rows(dot_t(dhidden, fd[1])))
    d3 = dunit2 * gd[2] + sd[2]
    dback2, dgain2, dshift2 = norm_back(cot, dunit2, dscale2, gd[2])
    full_db2 = gather_rows(dback2)
    dpre, dup, ddown = feedforward_back(full_db2, full_d2, fd[0], fd[1])
    dback1, dgain1, dshift1 = norm_back(
        dback2 + sum_rows(dot_t(dpre, fd[0])), dunit1, dscale1, gd[1]
    )
    full_db1 = gather_rows(dback1)
    att_c_grad = dot(full_db1, slot(wd, 5, 6)).astype(BF16)
    d_w5 = t_dot(full_db1, att_c)
    cq_grad, kc_grad, vc_grad = attend_back(cq, kc, vc, log_c, allow_c, att_c_grad)
    kvc_grad = jnp.concatenate([kc_grad, vc_grad], 1)
    d_w4 = t_dot(full_d1, cq_grad)
    e_w45 = t_dot(full_m, kvc_grad)

    mem_grad, d1_grad = sum_both(
        dot_t(kvc_grad, slot(we, 4, 6)), dot_t(cq_grad, slot(wd, 4, 5))
    )
    back2, gain2, shift2 = norm_back(mem_grad, unit2, scale2, ge[2])
    dback0, dgain0, dshift0 = norm_back(dback1 + d1_grad, dunit0, dscale0, gd[0])
    full_b2, full_db0 = gather_both(back2, dback0)
    pre, up, down = feedforward_back(full_b2, full_h1, fe[0], fe[1])
    att_d_grad = dot(full_db0, slot(wd, 3, 4)).astype(BF16)
    d_w3 = t_dot(full_db0, att_d)
    dqkv_grad = jnp.concatenate(attend_back(sq, sk, sv, log_d, allow_d, att_d_grad), 1)
    d_w012 = t_dot(full_y, dqkv_grad)
    part_e, part_d = sum_both(dot_t(pre, fe[0]), dot_t(dqkv_grad, slot(wd, 0, 3)))
    dec_grad = dback0 + part_d
    back1, gain1, shift1 = norm_back(back2 + part_e, unit1, scale1, ge[1])
    full_b1 = gather_rows(back1)
    att_e_grad = dot(full_b1, slot(we, 3, 4)).astype(BF16)
    e_w3 = t_dot(full_b1, att_e)
    qkv_grad = jnp.concatenate(attend_back(q, k, v, log_e, allow_e, att_e_grad), 1)
    e_w012 = t_dot(full_h0, qkv_grad)
    enc_grad, gain0, shift0 = norm_back(
        back1 + sum_rows(dot_t(qkv_grad, slot(we, 0, 3))), unit0, scale0, ge[0]
    )

    att_grads = jnp.stack(
        [jnp.concatenate([e_w012, e_w3, e_w45], 1), jnp.concatenate([d_w012, d_w3, d_w4, d_w5], 1)]
    ).astype(BF16)
    ffn_grads = jnp.stack([jnp.stack([up, down]), jnp.stack([dup, ddown])]).astype(BF16)
    small = jnp.stack(
        [
            jnp.stack([gain0, gain1, gain2, shift0, shift1, shift2]),
            jnp.stack([dgain0, dgain1, dgain2, dshift0, dshift1, dshift2]),
        ]
    )

    def own_layer(both):
        own = lax.dynamic_index_in_dim(both, section, 0, keepdims=False)
        other = lax.dynamic_index_in_dim(both, 1 - section, 0, keepdims=False)
        return own + swapped(other, "section")

    att_sum = lax.psum(own_layer(att_grads), "dp").astype(F32)
    ffn_sum = lax.psum(own_layer(ffn_grads), "dp").astype(F32)
    small_sum = lax.psum(own_layer(small), ("dp", "tensor"))

    half = x.shape[1] // 2

    def both_packs(rows, kind):
        halves = rows.reshape(rows.shape[0], 2, half)
        keep = lax.dynamic_index_in_dim(halves, section, 1, keepdims=False)
        give = lax.dynamic_index_in_dim(halves, 1 - section, 1, keepdims=False)
        got = swapped(give.astype(BF16), "section").astype(kind)
        keep = keep.astype(kind)
        return jnp.where(on_encoder, jnp.stack([keep, got]), jnp.stack([got, keep]))

    att_out = jnp.stack([slot(att_sum, j, j + 1) for j in range(6)])
    return (
        both_packs(d3, BF16),
        both_packs(enc_grad, F32),
        both_packs(dec_grad, F32),
        att_out[None],
        ffn_sum[None],
        small_sum[None, :3],
        small_sum[None, 3:],
    )


def solution(mesh):
    in_specs = (
        P("dp", "tensor", None),
        P("dp", None),
        P("dp", "tensor", None),
        P("dp", None),
        P("dp", "tensor", None),
        P("section", None, None, "tensor"),
        P("section", None, None, "tensor"),
        P("section", None, None),
        P("section", None, None),
    )
    out_specs = (
        P("dp", "tensor", "section"),
        P("dp", "tensor", "section"),
        P("dp", "tensor", "section"),
        P("section", None, None, "tensor"),
        P("section", None, None, "tensor"),
        P("section", None, None),
        P("section", None, None),
    )
    return jax.shard_map(
        on_device, mesh=mesh, in_specs=in_specs, out_specs=out_specs, check_vma=False
    )
```

time: 3420 us -> 1460 us (0.43)
  waiting for transfers between devices: 2430 us -> 893 us
  blocking collectives: 602 us -> 394 us
  matrix products: 162 us -> 59.5 us
  other arithmetic: 109 us -> 50.2 us
    while x50 -> x0, waiting for transfers between devices: 962 us -> none
    reduce_scatter x10 -> x2, waiting for transfers between devices: 735 us -> 149 us  [sum_rows(): lax.psum_scatter(values.astype(BF16), 'tensor', scatter_dimension=0, tile...]
    all_gather x16 -> x5, waiting for transfers between devices: 695 us -> 174 us  [gather_rows(): return lax.all_gather(values.astype(BF16), 'tensor', axis=0, tiled=True)]
    unnamed x1 -> x20, waiting for transfers between devices: 0.02 us -> 469 us
    all_gather x12 -> x3, blocking collectives: 275 us -> 69.1 us  [gather_rows(): return lax.all_gather(values.astype(BF16), 'tensor', axis=0, tiled=True)]
    dot_general x102 -> x51, matrix products: 151 us -> 59.5 us  [the longest x17 23.1 us: dot(): return jnp.dot(a, b, preferred_element_type=F32)]
    psum x1, waiting for transfers between devices: 0.01 us -> 40.1 us  [on_device(): att_sum = lax.psum(own_layer(att_grads), 'dp').astype(F32)]
    reduce_sum x60 -> x19, other arithmetic: 47.6 us -> 12.9 us  [the longest x7 6.34 us: norm_back(): return (back, jnp.sum(grad * unit, 0), jnp.sum(grad, 0))]
  transfers between devices with their start and end apart: 43 -> 24, of which waited for: 41 -> 21; matrix products, arithmetic and copies ran while one was open for 3% -> 3% of each run, Pallas kernels for 0% -> 0%
where the time goes in v1:
time: 1460 us; the launch traced here: 1450 us
  waiting for transfers between devices  893 us (61%)
  blocking collectives  394 us (27%)
  matrix products  59.5 us (4%)
  other arithmetic  50.2 us (3%)
  local copies, waits for them, and re-layouts  25.6 us (2%)
  between operations  16.9 us (1%)
  starting transfers between devices  14.8 us (1%)
    unnamed x20, waiting for transfers between devices  469 us
    psum x1, blocking collectives, on_device(): small_sum = lax.psum(own_layer(small), ('dp', 'tensor'))  325 us
    all_gather x5, waiting for transfers between devices, gather_rows(): return lax.all_gather(values.astype(BF16), 'tensor', axis=0, tiled=True)  174 us
    reduce_scatter x2, waiting for transfers between devices, sum_rows(): lax.psum_scatter(values.astype(BF16), 'tensor', scatter_dimension=0, tile...  149 us
    all_gather x3, blocking collectives, gather_rows(): return lax.all_gather(values.astype(BF16), 'tensor', axis=0, tiled=True)  69.1 us
    ppermute x10, waiting for transfers between devices, swapped(): return lax.ppermute(value, axis, [(0, 1), (1, 0)])  59.9 us
    psum x1, waiting for transfers between devices, on_device(): att_sum = lax.psum(own_layer(att_grads), 'dp').astype(F32)  40.1 us
  transfers between devices with their start and end apart: 24, of which 21 were waited for; matrix products, arithmetic and copies ran while one was open for 3% of the time, Pallas kernels for 0%

profile of v1, /device:TPU:0, one launch (start us, length us, event | category | flops | bytes accessed | tf_op | source)
XLA Modules:
  0.0 1453.7 jit_solution(7095868921573141971)
XLA Ops:
  8.0 2.0 collective-permute-start.1
  19.2 16.9 %collective-permute-done.2 = bf16[1024,384]{0,1:T(8,128)(2,1)S(1)} collective-permute-done((bf16[1024,384]{0,1:T(8,128)(2,1)S(1)}, bf16[1024,384]{0,1:T(8,128)(2,1)S(1)}, u32[]{:S(2)}, u32[]{:S(2)}) %collective-permute-start.2) | collective-permute-done | bytes 786464 | tf_op jit(solution)/shard_map/ppermute | solution.py:14
  36.2 30.4 %all-gather.6.cloned.1.call-done = bf16[1408,1024]{1,0:T(8,128)(2,1)} async-done(((bf16[88,1024]{1,0:T(8,128)(2,1)}), bf16[1408,1024]{1,0:T(8,128)(2,1)}) %all-gather.6.cloned.1.call-update) | async-done | bytes 2883600 | tf_op jit(solution)/shard_map/all_gather | solution.py:38
  66.7 2.0 slice.249
  74.2 1.7 copy-done.2
  78.1 2.0 pad_maximum_fusion
  80.8 74.0 %reduce-scatter.16.cloned.1.call-done = bf16[88,1024]{1,0:T(8,128)(2,1)} async-done(((bf16[1408,1024]{1,0:T(8,128)(2,1)}), bf16[88,1024]{1,0:T(8,128)(2,1)}) %reduce-scatter.16.cloned.1.call-update) | async-done | bytes 180240
  157.8 1.6 collective-permute-start.3
  159.4 21.7 %collective-permute-done.3 = bf16[2,1024,256]{2,1,0:T(8,128)(2,1)S(1)} collective-permute-done((bf16[2,1024,256]{2,1,0:T(8,128)(2,1)S(1)}, bf16[2,1024,256]{2,1,0:T(8,128)(2,1)S(1)}, u32[]{:S(2)}, u32[]{:S(2)}) %collective-permute-start.3) | collective-permute-done | bytes 1048608 | tf_op jit(solution)/shard_map/ppermute | solution.py:14
  182.5 21.7 %all-gather.8.cloned.1.call-done = bf16[1408,1024]{1,0:T(8,128)(2,1)} async-done(((bf16[88,1024]{1,0:T(8,128)(2,1)}), bf16[1408,1024]{1,0:T(8,128)(2,1)}) %all-gather.8.cloned.1.call-update) | async-done | bytes 2883600 | tf_op jit(solution)/shard_map/all_gather | solution.py:38
  204.1 2.0 slice.269
  206.2 5.1 multiply_convert_fusion.1
  212.1 2.4 convolution_convert_fusion.3
  214.7 74.2 %reduce-scatter.12.cloned.1.call-done = bf16[80,1024]{1,0:T(8,128)(2,1)} async-done(((bf16[1280,1024]{1,0:T(8,128)(2,1)}), bf16[80,1024]{1,0:T(8,128)(2,1)}) %reduce-scatter.12.cloned.1.call-update) | async-done | bytes 163856 | tf_op jit(solution)/shard_map/reduce_scatter | solution.py:42
  292.4 44.5 %all-gather.10.cloned.1.call-done = bf16[1280,1024]{1,0:T(8,128)(2,1)} async-done(((bf16[80,1024]{1,0:T(8,128)(2,1)}), bf16[1280,1024]{1,0:T(8,128)(2,1)}) %all-gather.10.cloned.1.call-update) | async-done | bytes 2621456 | tf_op jit(solution)/shard_map/all_gather | solution.py:38
  336.9 2.7 convolution_convert_fusion.6
  340.7 1.9 convolution_convert_fusion.19
  343.9 82.2 %all-reduce.12.cloned.1.call-done = bf16[128,1024]{1,0:T(8,128)(2,1)} async-done(((bf16[128,1024]{1,0:T(8,128)(2,1)}), bf16[128,1024]{1,0:T(8,128)(2,1)}) %all-reduce.12.cloned.1.call-update) | async-done | bytes 262160
  428.5 23.0 %all_gather.27 = bf16[128,1024]{1,0:T(8,128)(2,1)S(1)} all-gather(bf16[8,1024]{1,0:T(8,128)(2,1)S(1)} %fusion.127), channel_id=1, replica_groups=mesh['section'=2,'dp'=4,'tensor'=16] {'tensor'}, dimensions={0}, use_global_device_ids=true | all-gather | bytes 278528 | tf_op jit(solution)/shard_map/all_gather | solution.py:38
  454.4 82.6 %all-reduce.14.cloned.1.call-done = bf16[128,1024]{1,0:T(8,128)(2,1)} async-done(((bf16[128,1024]{1,0:T(8,128)(2,1)}), bf16[128,1024]{1,0:T(8,128)(2,1)}) %all-reduce.14.cloned.1.call-update) | async-done | bytes 262160
  541.0 23.0 %all_gather.28 = bf16[128,1024]{1,0:T(8,128)(2,1)S(1)} all-gather(bf16[8,1024]{1,0:T(8,128)(2,1)S(1)} %get-tuple-element.43), channel_id=1, replica_groups=mesh['section'=2,'dp'=4,'tensor'=16] {'tensor'}, dimensions={0}, use_global_device_ids=true | all-gather | bytes 278528 | tf_op jit(solution)/shard_map/all_gather | solution.py:38
  567.9 81.9 %all-reduce.16.cloned.1.call-done = bf16[128,1024]{1,0:T(8,128)(2,1)} async-done(((bf16[128,1024]{1,0:T(8,128)(2,1)}), bf16[128,1024]{1,0:T(8,128)(2,1)}) %all-reduce.16.cloned.1.call-update) | async-done | bytes 262160
  652.0 23.0 %all_gather.29 = bf16[128,1024]{1,0:T(8,128)(2,1)S(1)} all-gather(bf16[8,1024]{1,0:T(8,128)(2,1)S(1)} %get-tuple-element.40), channel_id=1, replica_groups=mesh['section'=2,'dp'=4,'tensor'=16] {'tensor'}, dimensions={0}, use_global_device_ids=true | all-gather | bytes 278528 | tf_op jit(solution)/shard_map/all_gather | solution.py:38
  678.4 1.8 convolution_convert_fusion.2
  680.3 1.9 pad_maximum_fusion.1
  682.3 74.0 %reduce-scatter.18.cloned.1.call-done = bf16[88,1024]{1,0:T(8,128)(2,1)} async-done(((bf16[1408,1024]{1,0:T(8,128)(2,1)}), bf16[88,1024]{1,0:T(8,128)(2,1)}) %reduce-scatter.18.cloned.1.call-update) | async-done | bytes 180240
  761.2 46.3 %all-gather.12.cloned.1.call-done = bf16[1408,1024]{1,0:T(8,128)(2,1)} async-done(((bf16[88,1024]{1,0:T(8,128)(2,1)}), bf16[1408,1024]{1,0:T(8,128)(2,1)}) %all-gather.12.cloned.1.call-update) | async-done | bytes 2883600 | tf_op jit(solution)/shard_map/all_gather | solution.py:38
  809.4 2.2 slice.286
  815.4 2.0 pad_maximum_fusion.2
  817.5 74.6 %reduce-scatter.20.cloned.1.call-done = bf16[88,1024]{1,0:T(8,128)(2,1)} async-done(((bf16[1408,1024]{1,0:T(8,128)(2,1)}), bf16[88,1024]{1,0:T(8,128)(2,1)}) %reduce-scatter.20.cloned.1.call-update) | async-done | bytes 180240
  909.0 31.4 %all-gather.14.cloned.1.call-done = bf16[1280,1024]{1,0:T(8,128)(2,1)} async-done(((bf16[80,1024]{1,0:T(8,128)(2,1)}), bf16[1280,1024]{1,0:T(8,128)(2,1)}) %all-gather.14.cloned.1.call-update) | async-done | bytes 2621456 | tf_op jit(solution)/shard_map/all_gather | solution.py:38
  940.4 2.7 convolution_convert_fusion.8
  943.1 4.8 fusion.8
  947.9 4.4 multiply_reduce_fusion
  953.5 2.0 fusion.12
  955.6 1.8 fusion.13
  960.8 1.6 collective-permute-start.7
  962.4 2.6 fusion.37
  965.0 14.7 %collective-permute-done.7 = bf16[1024,384]{0,1:T(8,128)(2,1)S(1)} collective-permute-done((bf16[1024,384]{0,1:T(8,128)(2,1)S(1)}, bf16[1024,384]{0,1:T(8,128)(2,1)S(1)}, u32[]{:S(2)}, u32[]{:S(2)}) %collective-permute-start.7) | collective-permute-done | bytes 786464 | tf_op jit(solution)/shard_map/ppermute | solution.py:14
  982.2 2.4 convolution_convert_fusion
  985.4 1.6 collective-permute-start.4
  987.0 2.1 collective-permute-done.4
  990.6 1.6 collective-permute-start.6
  992.2 2.2 collective-permute-done.6
  995.1 40.1 %all-reduce.18.cloned.1.call-done = (bf16[1024,384]{0,1:T(8,128)(2,1)}, bf16[1,2,1024,256]{3,2,1,0:T(8,128)(2,1)}) async-done(((bf16[1024,384]{0,1:T(8,128)(2,1)}, bf16[1,2,1024,256]{3,2,1,0:T(8,128)(2,1)}), (bf16[1024,384]{0,1:T(8,128)(2,1)}, bf16[1,2,1024,256]{3,2,1,0:T(8,128)(2,1)})) %all-reduce.18.cloned.1.call-update) | async-done | bytes 1835024 | tf_op jit(solution)/shard_map/psum | solution.py:231
  1038.3 74.7 %reduce-scatter.14.cloned.1.call-done = bf16[80,1024]{1,0:T(8,128)(2,1)} async-done(((bf16[1280,1024]{1,0:T(8,128)(2,1)}), bf16[80,1024]{1,0:T(8,128)(2,1)}) %reduce-scatter.14.cloned.1.call-update) | async-done | bytes 163856 | tf_op jit(solution)/shard_map/reduce_scatter | solution.py:42
  1115.8 1.7 collective-permute-start.9
  1119.8 324.9 %psum.23 = f32[6,1024]{1,0:T(8,128)S(1)} all-reduce(f32[6,1024]{1,0:T(8,128)S(1)} %fusion.124), channel_id=1, replica_groups=mesh['section'=2,'dp'=4,'tensor'=16] {'dp','tensor'}, use_global_device_ids=true, to_apply=%region_55.56 | all-reduce | flops 6144 | bytes 49152 | tf_op jit(solution)/shard_map/psum | solution.py:233
  (470 shorter events, 94.1 us)
Async XLA Ops:
  7.2 59.5 %all-gather.6.cloned.1.call-start = ((), (), s32[]{:S(2)}) async-start(), calls=%async_computation.5 | async-start | bytes 3063808 | tf_op jit(solution)/shard_map/all_gather | solution.py:38
  8.0 5.7 collective-permute-start.1
  10.7 3.7 collective-permute-start
  11.8 144.0 %copy-start.98 = (f32[80]{0:T(128)}, f32[80]{0:T(128)S(1)}, u32[]{:S(2)}) copy-start(f32[80]{0:T(128)S(1)} %broadcast_multiply_fusion.17) | copy-start | bytes 964
  13.0 142.9 %copy-start.105 = (f32[80]{0:T(128)}, f32[80]{0:T(128)S(1)}, u32[]{:S(2)}) copy-start(f32[80]{0:T(128)S(1)} %add_rsqrt_fusion.5) | copy-start | bytes 964
  15.8 141.1 %copy-start.77 = (f32[1,1024]{1,0:T(1,128)}, f32[1,1024]{1,0:T(1,128)S(1)}, u32[]{:S(2)}) copy-start(f32[1,1024]{1,0:T(1,128)S(1)} %get-tuple-element.79) | copy-start | bytes 12292
  15.8 273.0 %copy-start.63 = (f32[1,1024]{1,0:T(1,128)}, f32[1,1024]{1,0:T(1,128)S(1)}, u32[]{:S(2)}) copy-start(f32[1,1024]{1,0:T(1,128)S(1)} %get-tuple-element.76) | copy-start | bytes 12292
  15.8 274.4 %copy-start.66 = (f32[1,1024]{1,0:T(1,128)}, f32[1,1024]{1,0:T(1,128)S(1)}, u32[]{:S(2)}) copy-start(f32[1,1024]{1,0:T(1,128)S(1)} %get-tuple-element.75) | copy-start | bytes 12292
  17.6 137.1 %reduce-scatter.16.cloned.1.call-start = ((), (), s32[]{:S(2)}) async-start(), calls=%async_computation.15 | async-start | bytes 3063808
  17.8 18.3 %collective-permute-start.2 = (bf16[1024,384]{0,1:T(8,128)(2,1)S(1)}, bf16[1024,384]{0,1:T(8,128)(2,1)S(1)}, u32[]{:S(2)}, u32[]{:S(2)}) collective-permute-start(bf16[1024,384]{0,1:T(8,128)(2,1)S(1)} %bitcast_dynamic-update-slice_fusion), channel_id=1, source_target_pairs={{0,64},{64,0},{1,65},{65,1},{2,66},{66,2},{3,67},{67,3},{4,68},{68... | collective-permute-start | bytes 2359304 | tf_op jit(solution)/shard_map/ppermute | solution.py:14
  80.1 77.7 %copy-start.30 = (bf16[1,2,1024,256]{3,2,1,0:T(8,128)(2,1)S(1)}, bf16[1,2,1024,256]{3,2,1,0:T(8,128)(2,1)}, u32[]{:S(2)}) copy-start(bf16[1,2,1024,256]{3,2,1,0:T(8,128)(2,1)} %param.15) | copy-start | bytes 3145732
  80.1 124.0 %all-gather.8.cloned.1.call-start = ((), (), s32[]{:S(2)}) async-start(), calls=%async_computation.6 | async-start | bytes 3063808 | tf_op jit(solution)/shard_map/all_gather | solution.py:38
  80.8 75.9 %copy-start.79 = (f32[1,1024]{1,0:T(1,128)}, f32[1,1024]{1,0:T(1,128)S(1)}, u32[]{:S(2)}) copy-start(f32[1,1024]{1,0:T(1,128)S(1)} %get-tuple-element.74) | copy-start | bytes 12292
  156.1 132.7 %copy-start.103 = (f32[80]{0:T(128)}, f32[80]{0:T(128)S(1)}, u32[]{:S(2)}) copy-start(f32[80]{0:T(128)S(1)} %broadcast_multiply_fusion.16) | copy-start | bytes 964
  156.6 132.3 %copy-start.112 = (f32[80]{0:T(128)}, f32[80]{0:T(128)S(1)}, u32[]{:S(2)}) copy-start(f32[80]{0:T(128)S(1)} %add_rsqrt_fusion.3) | copy-start | bytes 964
  157.7 131.1 %reduce-scatter.12.cloned.1.call-start = ((), (), s32[]{:S(2)}) async-start(), calls=%async_computation.7 | async-start | bytes 2785280 | tf_op jit(solution)/shard_map/reduce_scatter | solution.py:42
  157.8 23.3 %collective-permute-start.3 = (bf16[2,1024,256]{2,1,0:T(8,128)(2,1)S(1)}, bf16[2,1024,256]{2,1,0:T(8,128)(2,1)S(1)}, u32[]{:S(2)}, u32[]{:S(2)}) collective-permute-start(bf16[2,1024,256]{2,1,0:T(8,128)(2,1)S(1)} %bitcast.321), channel_id=1, source_target_pairs={{0,64},{64,0},{1,65},{65,1},{2,66},{66,2},{3,67},{67,3},{4,68},{68... | collective-permute-start | bytes 3145736 | tf_op jit(solution)/shard_map/ppermute | solution.py:14
  214.4 75.9 %copy-start.89 = (f32[1,1024]{1,0:T(1,128)S(1)}, f32[1,1024]{1,0:T(1,128)}, u32[]{:S(2)}) copy-start(f32[1,1024]{1,0:T(1,128)} %get-tuple-element.78) | copy-start | bytes 12292
  214.4 122.4 %all-gather.10.cloned.1.call-start = ((), (), s32[]{:S(2)}) async-start(), calls=%async_computation.8 | async-start | bytes 2785280 | tf_op jit(solution)/shard_map/all_gather | solution.py:38
  291.1 134.9 %all-reduce.12.cloned.1.call-start = ((), (), s32[]{:S(2)}) async-start(), calls=%async_computation.12 | async-start | bytes 524288
  342.6 194.4 %all-reduce.14.cloned.1.call-start = ((), (), s32[]{:S(2)}) async-start(), calls=%async_computation.13 | async-start | bytes 524288
  454.4 195.5 %all-reduce.16.cloned.1.call-start = ((), (), s32[]{:S(2)}) async-start(), calls=%async_computation.14 | async-start | bytes 524288
  567.1 109.5 %copy-start.37 = (bf16[1280,128]{0,1:T(8,128)(2,1)S(1)}, bf16[1280,128]{0,1:T(8,128)(2,1)}, u32[]{:S(2)}) copy-start(bf16[1280,128]{0,1:T(8,128)(2,1)} %copy-done.36) | copy-start | bytes 983044
  567.1 189.2 %reduce-scatter.18.cloned.1.call-start = ((), (), s32[]{:S(2)}) async-start(), calls=%async_computation.16 | async-start | bytes 3063808
  682.2 75.9 %copy-start.101 = (f32[8]{0:T(128)S(1)}, f32[8]{0:T(128)}, u32[]{:S(2)}) copy-start(f32[8]{0:T(128)} %copy-done.100) | copy-start | bytes 100
  682.3 78.9 %copy-start.122 = (f32[128]{0:T(128)S(1)}, f32[128]{0:T(128)}, u32[]{:S(2)}) copy-start(f32[128]{0:T(128)} %copy-done.121) | copy-start | bytes 1540
  682.3 78.9 %copy-start.124 = (f32[128]{0:T(128)S(1)}, f32[128]{0:T(128)}, u32[]{:S(2)}) copy-start(f32[128]{0:T(128)} %copy-done.123) | copy-start | bytes 1540
  682.3 125.3 %all-gather.12.cloned.1.call-start = ((), (), s32[]{:S(2)}) async-start(), calls=%async_computation.9 | async-start | bytes 3063808 | tf_op jit(solution)/shard_map/all_gather | solution.py:38
  761.1 131.0 %reduce-scatter.20.cloned.1.call-start = ((), (), s32[]{:S(2)}) async-start(), calls=%async_computation.17 | async-start | bytes 3063808
  817.4 77.6 %copy-start.81 = (f32[1280]{0:T(1024)S(1)}, f32[1280]{0:T(1024)}, u32[]{:S(2)}) copy-start(f32[1280]{0:T(1024)} %copy-done.80) | copy-start | bytes 15364
  817.4 77.6 %copy-start.83 = (f32[1280]{0:T(1024)S(1)}, f32[1280]{0:T(1024)}, u32[]{:S(2)}) copy-start(f32[1280]{0:T(1024)} %copy-done.82) | copy-start | bytes 15364
  817.4 77.7 %copy-start.19 = (bf16[128,1024]{1,0:T(8,128)(2,1)S(1)}, bf16[128,1024]{1,0:T(8,128)(2,1)}, u32[]{:S(2)}) copy-start(bf16[128,1024]{1,0:T(8,128)(2,1)} %copy-done.18) | copy-start | bytes 786436
  817.4 77.7 %copy-start.51 = (bf16[128,256]{1,0:T(8,128)(2,1)S(1)}, bf16[128,256]{1,0:T(8,128)(2,1)}, u32[]{:S(2)}) copy-start(bf16[128,256]{1,0:T(8,128)(2,1)} %copy-done.50) | copy-start | bytes 196612
  817.4 122.9 %all-gather.14.cloned.1.call-start = ((), (), s32[]{:S(2)}) async-start(), calls=%async_computation.10 | async-start | bytes 2785280 | tf_op jit(solution)/shard_map/all_gather | solution.py:38
  894.8 140.4 %all-reduce.18.cloned.1.call-start = ((), (), s32[]{:S(2)}) async-start(), calls=%async_computation.18 | async-start | bytes 3670016 | tf_op jit(solution)/shard_map/psum | solution.py:231
  904.2 58.2 %collective-permute-start.8 = (bf16[2,1024,256]{2,1,0:T(8,128)(2,1)}, bf16[2,1024,256]{2,1,0:T(8,128)(2,1)}, u32[]{:S(2)}, u32[]{:S(2)}) collective-permute-start(bf16[2,1024,256]{2,1,0:T(8,128)(2,1)} %fusion.33), channel_id=1, source_target_pairs={{0,64},{64,0},{1,65},{65,1},{2,66},{66,2},{3,67},{67,3},{4,68},{68... | collective-permute-start | bytes 3145736 | tf_op jit(solution)/shard_map/ppermute | solution.py:14
  960.8 19.0 %collective-permute-start.7 = (bf16[1024,384]{0,1:T(8,128)(2,1)S(1)}, bf16[1024,384]{0,1:T(8,128)(2,1)S(1)}, u32[]{:S(2)}, u32[]{:S(2)}) collective-permute-start(bf16[1024,384]{0,1:T(8,128)(2,1)S(1)} %fusion.39), channel_id=1, source_target_pairs={{0,64},{64,0},{1,65},{65,1},{2,66},{66,2},{3,67},{67,3},{4,68},{68... | collective-permute-start | bytes 2359304 | tf_op jit(solution)/shard_map/ppermute | solution.py:14
  981.0 132.1 %reduce-scatter.14.cloned.1.call-start = ((), (), s32[]{:S(2)}) async-start(), calls=%async_computation.11 | async-start | bytes 2785280 | tf_op jit(solution)/shard_map/reduce_scatter | solution.py:42
  985.4 3.7 collective-permute-start.4
  990.6 3.9 collective-permute-start.6
  1038.2 77.4 %copy-start.87 = (f32[1024]{0:T(1024)S(1)}, f32[1024]{0:T(1024)}, u32[]{:S(2)}) copy-start(f32[1024]{0:T(1024)} %get-tuple-element.9) | copy-start | bytes 12292
  1038.2 77.4 %copy-start.88 = (f32[1024]{0:T(1024)S(1)}, f32[1024]{0:T(1024)}, u32[]{:S(2)}) copy-start(f32[1024]{0:T(1024)} %get-tuple-element.16) | copy-start | bytes 12292
  1038.2 77.4 %copy-start.96 = (f32[1024]{0:T(1024)S(1)}, f32[1024]{0:T(1024)}, u32[]{:S(2)}) copy-start(f32[1024]{0:T(1024)} %get-tuple-element.11) | copy-start | bytes 12292
  1038.2 77.4 %copy-start.97 = (f32[1024]{0:T(1024)S(1)}, f32[1024]{0:T(1024)}, u32[]{:S(2)}) copy-start(f32[1024]{0:T(1024)} %get-tuple-element.18) | copy-start | bytes 12292
  1038.3 79.4 %copy-start.76 = (f32[6,1024,64]{1,2,0:T(8,128)}, f32[6,1024,64]{1,2,0:T(8,128)S(1)}, u32[]{:S(2)}) copy-start(f32[6,1024,64]{1,2,0:T(8,128)S(1)} %fusion.71) | copy-start | bytes 4718596
  1114.3 332.4 %copy-start.1 = (s32[2,1280]{1,0:T(2,128)S(1)}, s32[2,1280]{1,0:T(2,128)}, u32[]{:S(2)}) copy-start(s32[2,1280]{1,0:T(2,128)} %param.10) | copy-start | bytes 30724
  1115.8 4.0 collective-permute-start.9
  1117.8 328.1 %collective-permute-start.5 = (bf16[80,512]{1,0:T(8,128)(2,1)S(1)}, bf16[80,512]{1,0:T(8,128)(2,1)S(1)}, u32[]{:S(2)}, u32[]{:S(2)}) collective-permute-start(bf16[80,512]{1,0:T(8,128)(2,1)S(1)} %bitcast.345), channel_id=1, source_target_pairs={{0,64},{64,0},{1,65},{65,1},{2,66},{66,2},{3,67},{67,3},{4,68},{68... | collective-permute-start | bytes 245768 | tf_op jit(solution)/shard_map/ppermute | solution.py:14
  (110 other events, 1667.5 us)
Sparse Core Ops, SparseCore 0:
  17.8 48.8 all-gather.5
  80.2 74.4 reduce-scatter.15
  157.8 46.2 all-gather.7
  214.6 74.2 reduce-scatter.11
  291.4 45.4 all-gather.9
  342.7 83.3 all-reduce.11
  454.5 82.4 all-reduce.13
  567.2 82.5 all-reduce.15
  682.4 73.9 reduce-scatter.17
  761.2 46.2 all-gather.11
  817.5 74.5 reduce-scatter.19
  894.9 45.4 all-gather.13
  981.1 54.0 all-reduce.17
  1038.7 74.3 reduce-scatter.13

commit v2 on v1

--- a/solution.py
+++ b/solution.py
@@ -1,13 +1,303 @@
 import jax
 import jax.numpy as jnp
 from jax import lax
+from jax.experimental import pallas as pl
+from jax.experimental.pallas import tpu as pltpu
 from jax.sharding import PartitionSpec as P
 
 HEAD = 64
 EPSILON = 1e-05
 MASKED = -1000000000.0
+
 F32 = jnp.float32
 BF16 = jnp.bfloat16
+SIDE = 4
+UP = (0, 2)
+DOWN = (1, 3)
+GATHER_COPIES = 32
+SUM_COPIES = 32
+
+
+def at_grid():
+    index = lax.axis_index("tensor")
+    return lax.div(index, SIDE), lax.rem(index, SIDE)
+
+
+def moved(place, axis, steps):
+    y, x = place
+    if axis == 0:
+        return lax.rem(y + steps % SIDE, SIDE), x
+    return y, lax.rem(x + steps % SIDE, SIDE)
+
+
+def greet(place):
+    barrier = pltpu.get_barrier_semaphore()
+    for axis in range(2):
+        for steps in (1, -1):
+            y, x = moved(place, axis, steps)
+            pl.semaphore_signal(
+                barrier,
+                inc=1,
+                device_id={"tensor": y * SIDE + x},
+                device_id_type=pl.DeviceIdType.MESH,
+            )
+    pl.semaphore_wait(barrier, 4)
+
+
+class Copies:
+    def __init__(self, place, send_sems, recv_sems):
+        self.place, self.send, self.recv, self.used = place, send_sems, recv_sems, 0
+        self.started = []
+
+    def start(self, source, target, axis, steps):
+        y, x = moved(self.place, axis, steps)
+        n = self.used
+        self.used += 1
+        copy = pltpu.make_async_remote_copy(
+            src_ref=source,
+            dst_ref=target,
+            send_sem=self.send.at[n],
+            recv_sem=self.recv.at[n],
+            device_id={"tensor": y * SIDE + x},
+            device_id_type=pl.DeviceIdType.MESH,
+        )
+        copy.start()
+        self.started.append(copy)
+        return copy
+
+    def finish(self):
+        for copy in self.started:
+            copy.wait_send()
+        self.started = []
+
+
+def gather(copies, bufs):
+    place = copies.place
+    jobs = []
+    for buf in bufs:
+        half = buf.shape[-1] // 2
+        for h in range(2):
+            jobs.append((buf, 1 - h, h, h * half, half))
+
+    def block(job, r, s, part=None):
+        buf, a, b, start, size = job
+        y, x = moved(moved(place, a, r), b, s)
+        if part is not None:
+            size = size // 2
+            start = start + part * size
+        return buf.at[y, x, :, pl.ds(start, size)]
+
+    def send(job, axis, steps, r, s, part=None):
+        ref = block(job, r, s, part)
+        return copies.start(ref, ref, axis, steps)
+
+    first, spread, ahead = [], [], []
+    for job in jobs:
+        a, b = job[1], job[2]
+        first.append([send(job, a, 1, 0, 0), send(job, a, -1, 0, 0)])
+    for job in jobs:
+        b = job[2]
+        spread.append({0: [send(job, b, 1, 0, 0), send(job, b, -1, 0, 0)]})
+    second = []
+    for i, job in enumerate(jobs):
+        a, b = job[1], job[2]
+        first[i][0].wait_recv()
+        one = send(job, a, 1, -1, 0, 0)
+        spread[i][3] = [send(job, b, 1, -1, 0), send(job, b, -1, -1, 0)]
+        first[i][1].wait_recv()
+        two = send(job, a, -1, 1, 0, 1)
+        spread[i][1] = [send(job, b, 1, 1, 0), send(job, b, -1, 1, 0)]
+        second.append([one, two])
+    for i, job in enumerate(jobs):
+        b = job[2]
+        spread[i][0][0].wait_recv()
+        ahead.append([send(job, b, 1, 0, -1)])
+    for i, job in enumerate(jobs):
+        b = job[2]
+        second[i][0].wait_recv()
+        second[i][1].wait_recv()
+        spread[i][2] = [send(job, b, 1, 2, 0), send(job, b, -1, 2, 0)]
+    for i, job in enumerate(jobs):
+        b = job[2]
+        for r in DOWN:
+            spread[i][r][1].wait_recv()
+            ahead[i].append(send(job, b, -1, r, 1))
+    for i, job in enumerate(jobs):
+        b = job[2]
+        spread[i][2][0].wait_recv()
+        ahead[i].append(send(job, b, 1, 2, -1))
+    for i, job in enumerate(jobs):
+        spread[i][0][1].wait_recv()
+        for r in DOWN:
+            spread[i][r][0].wait_recv()
+        spread[i][2][1].wait_recv()
+        for copy in ahead[i]:
+            copy.wait_recv()
+    copies.finish()
+
+
+def sum_blocks(copies, parts):
+    place = copies.place
+    jobs = []
+    for part, land in parts:
+        half = part.shape[-1] // 2
+        for h in range(2):
+            jobs.append((part, land, 15 * h, 1 - h, h, h * half, half))
+
+    def block(job, r, s, quarter=None):
+        part, _, _, a, b, start, size = job
+        y, x = moved(moved(place, a, r), b, s)
+        if quarter is not None:
+            size = size // 2
+            start = start + quarter * size
+        return part.at[y, x, :, pl.ds(start, size)]
+
+    def landing(job, n, quarter=None):
+        ref = job[1].at[job[2] + n]
+        if quarter is None:
+            return ref
+        size = job[6] // 2
+        return ref.at[:, pl.ds(quarter * size, size)]
+
+    def add(target, *others):
+        total = target[...].astype(F32)
+        for other in others:
+            total = total + other[...].astype(F32)
+        return total
+
+    far, near = [], []
+    for job in jobs:
+        b = job[4]
+        sent = {}
+        for r in (2, 3, 1, 0):
+            steps = 1 if r in UP else -1
+            sent[r] = copies.start(block(job, r, 2), landing(job, r), b, steps)
+        far.append(sent)
+    order = (2, 3, 1, 0)
+    for job in jobs:
+        b = job[4]
+        sent = {}
+        for r in order:
+            steps = -1 if r in UP else 1
+            sent[r] = [
+                copies.start(block(job, r, steps), landing(job, 4 + 2 * r + (0 if steps == 1 else 1)), b, steps)
+            ]
+        near.append(sent)
+    for r in order:
+        for i, job in enumerate(jobs):
+            b = job[4]
+            steps = 1 if r in UP else -1
+            far[i][r].wait_recv()
+            ref = block(job, r, steps)
+            ref[...] = add(ref, landing(job, r)).astype(BF16)
+            near[i][r].append(
+                copies.start(ref, landing(job, 4 + 2 * r + (0 if steps == 1 else 1)), b, steps)
+            )
+    opposite, last = [], []
+    for r in order[:3]:
+        for i, job in enumerate(jobs):
+            a = job[3]
+            for copy in near[i][r]:
+                copy.wait_recv()
+            ref = block(job, r, 0)
+            total = add(ref, landing(job, 4 + 2 * r), landing(job, 5 + 2 * r))
+            if r == 2:
+                ref[...] = total.astype(BF16)
+                opposite.append(
+                    [
+                        copies.start(block(job, 2, 0, 0), landing(job, 12, 0), a, 1),
+                        copies.start(block(job, 2, 0, 1), landing(job, 12, 1), a, -1),
+                    ]
+                )
+                last.append({})
+            else:
+                quarter = 0 if r == 1 else 1
+                opposite[i][quarter].wait_recv()
+                size = job[6] // 2
+                extra = landing(job, 12, quarter)[...].astype(F32)
+                low, high = total[:, :size], total[:, size:]
+                if quarter == 0:
+                    low = low + extra
+                else:
+                    high = high + extra
+                ref[:, pl.ds(0, size)] = low.astype(BF16)
+                ref[:, pl.ds(size, size)] = high.astype(BF16)
+                steps = 1 if r == 1 else -1
+                last[i][r] = copies.start(ref, landing(job, 13 if r == 1 else 14), a, steps)
+    results = []
+    for i, job in enumerate(jobs):
+        for copy in near[i][0]:
+            copy.wait_recv()
+        last[i][1].wait_recv()
+        last[i][3].wait_recv()
+        results.append(
+            add(block(job, 0, 0), landing(job, 4), landing(job, 5), landing(job, 13), landing(job, 14))
+        )
+    copies.finish()
+    return results
+
+
+def sems(n):
+    return [pltpu.SemaphoreType.DMA((n,)), pltpu.SemaphoreType.DMA((n,))]
+
+
+VM = pl.BlockSpec(memory_space=pltpu.VMEM)
+
+
+def gather_call(blocks, collective_id):
+    count = len(blocks)
+
+    def kernel(*refs):
+        ins, outs, (send, recv) = refs[:count], refs[count : 2 * count], refs[2 * count :]
+        place = at_grid()
+        greet(place)
+        for i, o in zip(ins, outs):
+            o[place[0], place[1]] = i[...]
+        gather(Copies(place, send, recv), outs)
+
+    return pl.pallas_call(
+        kernel,
+        out_shape=[jax.ShapeDtypeStruct((SIDE, SIDE) + b.shape, b.dtype) for b in blocks],
+        in_specs=[VM] * count,
+        out_specs=[VM] * count,
+        scratch_shapes=sems(GATHER_COPIES * count),
+        compiler_params=pltpu.CompilerParams(
+            collective_id=collective_id, has_side_effects=True, vmem_limit_bytes=48 << 20
+        ),
+    )(*blocks)
+
+
+def sum_call(partials, collective_id):
+    count = len(partials)
+
+    def kernel(*refs):
+        ins, outs = refs[:count], refs[count : 2 * count]
+        lands, (send, recv) = refs[2 * count : 3 * count], refs[3 * count : 3 * count + 2]
+        work = refs[3 * count + 2 :]
+        place = at_grid()
+        greet(place)
+        for i, w in zip(ins, work):
+            w[...] = i[...]
+        results = sum_blocks(Copies(place, send, recv), list(zip(work, lands)))
+        for n, out in enumerate(outs):
+            half = out.shape[-1] // 2
+            for h in range(2):
+                out[:, h * half : (h + 1) * half] = results[2 * n + h]
+
+    return pl.pallas_call(
+        kernel,
+        out_shape=[jax.ShapeDtypeStruct(p.shape[2:], F32) for p in partials],
+        in_specs=[VM] * count,
+        out_specs=[VM] * count,
+        scratch_shapes=[
+            pltpu.VMEM((30, p.shape[2], p.shape[3] // 2), BF16) for p in partials
+        ]
+        + sems(SUM_COPIES * count)
+        + [pltpu.VMEM(p.shape, BF16) for p in partials],
+        compiler_params=pltpu.CompilerParams(
+            collective_id=collective_id, has_side_effects=True, vmem_limit_bytes=48 << 20
+        ),
+    )(*partials)
 
 
 def swapped(value, axis):
@@ -34,30 +324,46 @@
     return jax.nn.gelu(values, approximate=False)
 
 
-def gather_rows(values):
-    return lax.all_gather(values.astype(BF16), "tensor", axis=0, tiled=True)
-
-
-def sum_rows(values):
-    return lax.psum_scatter(
-        values.astype(BF16), "tensor", scatter_dimension=0, tiled=True
-    ).astype(F32)
-
-
-def gather_both(enc, dec):
-    size, ra, rb = lax.axis_size("tensor"), enc.shape[0], dec.shape[0]
-    full = gather_rows(jnp.concatenate([enc, dec], 0)).reshape(size, ra + rb, -1)
-    return full[:, :ra].reshape(size * ra, -1), full[:, ra:].reshape(size * rb, -1)
-
-
-def sum_both(enc, dec):
-    size = lax.axis_size("tensor")
-    ra, rb = enc.shape[0] // size, dec.shape[0] // size
-    both = jnp.concatenate(
-        [enc.astype(BF16).reshape(size, ra, -1), dec.astype(BF16).reshape(size, rb, -1)], 1
-    )
-    mine = sum_rows(both.reshape(size * (ra + rb), -1))
-    return mine[:ra], mine[ra:]
+def folded(rows):
+    half = rows.shape[-1] // 2
+    return jnp.concatenate([rows[..., :half], rows[..., half:]], -2)
+
+
+def unfolded(rows):
+    count = rows.shape[-2] // 2
+    return jnp.concatenate([rows[..., :count, :], rows[..., count:, :]], -1)
+
+
+def gather_enc(rows, n):
+    (full,) = gather_call([rows.astype(BF16)], n)
+    return full.reshape(-1, rows.shape[-1])
+
+
+def gather_dec(rows, n):
+    (full,) = gather_call([folded(rows).astype(BF16)], n)
+    return unfolded(full).reshape(-1, rows.shape[-1])
+
+
+def gather_both(enc, dec, n):
+    full, small = gather_call([enc.astype(BF16), folded(dec).astype(BF16)], n)
+    return full.reshape(-1, enc.shape[-1]), unfolded(small).reshape(-1, dec.shape[-1])
+
+
+def in_blocks(part):
+    return part.astype(BF16).reshape(SIDE, SIDE, -1, part.shape[-1])
+
+
+def sum_enc(part, n):
+    return sum_call([in_blocks(part)], n)[0]
+
+
+def sum_dec(part, n):
+    return unfolded(sum_call([folded(in_blocks(part))], n)[0])
+
+
+def sum_both(enc, dec, n):
+    rows, small = sum_call([in_blocks(enc), folded(in_blocks(dec))], n)
+    return rows, unfolded(small)
 
 
 def dot(a, b):
@@ -148,40 +454,40 @@
 
     unit0, scale0 = norm_parts(x)
     h0 = unit0 * ge[0] + se[0]
-    full_h0, full_y = gather_both(h0, y)
+    full_h0, full_y = gather_both(h0, y, 1)
     qkv = dot(full_h0, slot(we, 0, 3)).astype(BF16)
     q, k, v = (slot(qkv, j, j + 1) for j in range(3))
     att_e, log_e = attend(q, k, v, allow_e)
     dqkv = dot(full_y, slot(wd, 0, 3)).astype(BF16)
     sq, sk, sv = (slot(dqkv, j, j + 1) for j in range(3))
     att_d, log_d = attend(sq, sk, sv, allow_d)
-    part_e, part_d = sum_both(dot_t(att_e, slot(we, 3, 4)), dot_t(att_d, slot(wd, 3, 4)))
+    part_e, part_d = sum_both(dot_t(att_e, slot(we, 3, 4)), dot_t(att_d, slot(wd, 3, 4)), 2)
     unit1, scale1 = norm_parts(h0 + part_e)
     h1 = unit1 * ge[1] + se[1]
     dunit0, dscale0 = norm_parts(y + part_d)
     d1 = dunit0 * gd[0] + sd[0]
-    full_h1, full_d1 = gather_both(h1, d1)
+    full_h1, full_d1 = gather_both(h1, d1, 3)
     hidden = gelu_exact(dot(full_h1, fe[0])).astype(BF16)
     cq = dot(full_d1, slot(wd, 4, 5)).astype(BF16)
-    unit2, scale2 = norm_parts(h1 + sum_rows(dot_t(hidden, fe[1])))
-    full_m = gather_rows(unit2 * ge[2] + se[2])
+    unit2, scale2 = norm_parts(h1 + sum_enc(dot_t(hidden, fe[1]), 4))
+    full_m = gather_enc(unit2 * ge[2] + se[2], 5)
     kvc = dot(full_m, slot(we, 4, 6)).astype(BF16)
     kc, vc = slot(kvc, 0, 1), slot(kvc, 1, 2)
 
     att_c, log_c = attend(cq, kc, vc, allow_c)
-    dunit1, dscale1 = norm_parts(d1 + sum_rows(dot_t(att_c, slot(wd, 5, 6))))
+    dunit1, dscale1 = norm_parts(d1 + sum_dec(dot_t(att_c, slot(wd, 5, 6)), 6))
     d2 = dunit1 * gd[1] + sd[1]
-    full_d2 = gather_rows(d2)
+    full_d2 = gather_dec(d2, 7)
     dhidden = gelu_exact(dot(full_d2, fd[0])).astype(BF16)
-    dunit2, dscale2 = norm_parts(d2 + sum_rows(dot_t(dhidden, fd[1])))
+    dunit2, dscale2 = norm_parts(d2 + sum_dec(dot_t(dhidden, fd[1]), 8))
     d3 = dunit2 * gd[2] + sd[2]
     dback2, dgain2, dshift2 = norm_back(cot, dunit2, dscale2, gd[2])
-    full_db2 = gather_rows(dback2)
+    full_db2 = gather_dec(dback2, 9)
     dpre, dup, ddown = feedforward_back(full_db2, full_d2, fd[0], fd[1])
     dback1, dgain1, dshift1 = norm_back(
-        dback2 + sum_rows(dot_t(dpre, fd[0])), dunit1, dscale1, gd[1]
-    )
-    full_db1 = gather_rows(dback1)
+        dback2 + sum_dec(dot_t(dpre, fd[0]), 10), dunit1, dscale1, gd[1]
+    )
+    full_db1 = gather_dec(dback1, 11)
     att_c_grad = dot(full_db1, slot(wd, 5, 6)).astype(BF16)
     d_w5 = t_dot(full_db1, att_c)
     cq_grad, kc_grad, vc_grad = attend_back(cq, kc, vc, log_c, allow_c, att_c_grad)
@@ -190,26 +496,26 @@
     e_w45 = t_dot(full_m, kvc_grad)
 
     mem_grad, d1_grad = sum_both(
-        dot_t(kvc_grad, slot(we, 4, 6)), dot_t(cq_grad, slot(wd, 4, 5))
+        dot_t(kvc_grad, slot(we, 4, 6)), dot_t(cq_grad, slot(wd, 4, 5)), 12
     )
     back2, gain2, shift2 = norm_back(mem_grad, unit2, scale2, ge[2])
     dback0, dgain0, dshift0 = norm_back(dback1 + d1_grad, dunit0, dscale0, gd[0])
-    full_b2, full_db0 = gather_both(back2, dback0)
+    full_b2, full_db0 = gather_both(back2, dback0, 13)
     pre, up, down = feedforward_back(full_b2, full_h1, fe[0], fe[1])
     att_d_grad = dot(full_db0, slot(wd, 3, 4)).astype(BF16)
     d_w3 = t_dot(full_db0, att_d)
     dqkv_grad = jnp.concatenate(attend_back(sq, sk, sv, log_d, allow_d, att_d_grad), 1)
     d_w012 = t_dot(full_y, dqkv_grad)
-    part_e, part_d = sum_both(dot_t(pre, fe[0]), dot_t(dqkv_grad, slot(wd, 0, 3)))
+    part_e, part_d = sum_both(dot_t(pre, fe[0]), dot_t(dqkv_grad, slot(wd, 0, 3)), 14)
     dec_grad = dback0 + part_d
     back1, gain1, shift1 = norm_back(back2 + part_e, unit1, scale1, ge[1])
-    full_b1 = gather_rows(back1)
+    full_b1 = gather_enc(back1, 15)
     att_e_grad = dot(full_b1, slot(we, 3, 4)).astype(BF16)
     e_w3 = t_dot(full_b1, att_e)
     qkv_grad = jnp.concatenate(attend_back(q, k, v, log_e, allow_e, att_e_grad), 1)
     e_w012 = t_dot(full_h0, qkv_grad)
     enc_grad, gain0, shift0 = norm_back(
-        back1 + sum_rows(dot_t(qkv_grad, slot(we, 0, 3))), unit0, scale0, ge[0]
+        back1 + sum_enc(dot_t(qkv_grad, slot(we, 0, 3)), 16), unit0, scale0, ge[0]
     )
 
     att_grads = jnp.stack(

time: 1460 us -> 771 us (0.53)
  waiting for transfers between devices: 893 us -> 1.72 us
  Pallas kernels: 0 us -> 292 us
  blocking collectives: 394 us -> 324 us
  other arithmetic: 50.2 us -> 31.9 us
    unnamed x20 -> x1, waiting for transfers between devices: 469 us -> 0.02 us
    pallas_call x0 -> x16, Pallas kernels: none -> 292 us  [the longest x8 148 us: gather_call(): pl.pallas_call(kernel, out_shape=[jax.ShapeDtypeStruct((SIDE, SIDE) + b.s...]
    all_gather x5 -> x0, waiting for transfers between devices: 174 us -> none  [gather_rows(): return lax.all_gather(values.astype(BF16), 'tensor', axis=0, tiled=True)]
    reduce_scatter x2 -> x0, waiting for transfers between devices: 149 us -> none  [sum_rows(): lax.psum_scatter(values.astype(BF16), 'tensor', scatter_dimension=0, tile...]
    all_gather x3 -> x0, blocking collectives: 69.1 us -> none  [gather_rows(): return lax.all_gather(values.astype(BF16), 'tensor', axis=0, tiled=True)]
    ppermute x10, waiting for transfers between devices: 59.9 us -> 1.7 us  [swapped(): return lax.ppermute(value, axis, [(0, 1), (1, 0)])]
    psum x1, waiting for transfers between devices: 40.1 us -> 0.01 us  [on_device(): att_sum = lax.psum(own_layer(att_grads), 'dp').astype(F32)]
  transfers between devices with their start and end apart: 24 -> 11, of which waited for: 21 -> 2; matrix products, arithmetic and copies ran while one was open for 3% -> 4% of each run, Pallas kernels for 0% -> 11%
where the time goes in v2:
time: 771 us; the launch traced here: 760 us
  blocking collectives  324 us (42%)
  Pallas kernels  292 us (38%)
  matrix products  55 us (7%)
  other arithmetic  31.9 us (4%)
  local copies, waits for them, and re-layouts  25.6 us (3%)
  between operations  17.1 us (2%)
  starting transfers between devices  12.3 us (2%)
    psum x1, blocking collectives, on_device(): small_sum = lax.psum(own_layer(small), ('dp', 'tensor'))  324 us
    pallas_call x8, Pallas kernels, gather_call(): pl.pallas_call(kernel, out_shape=[jax.ShapeDtypeStruct((SIDE, SIDE) + b.s...  148 us
    pallas_call x8, Pallas kernels, sum_call(): pl.pallas_call(kernel, out_shape=[jax.ShapeDtypeStruct(p.shape[2:], F32)...  144 us
    dot_general x17, matrix products, dot(): return jnp.dot(a, b, preferred_element_type=F32)  20.4 us
    dot_general x17, matrix products, t_dot(): lax.dot_general(a, b, (((0,), (0,)), ((), ())), preferred_element_type=F32)  17.3 us
    dot_general x17, matrix products, dot_t(): lax.dot_general(a, b, (((1,), (1,)), ((), ())), preferred_element_type=F32)  17.3 us
  transfers between devices with their start and end apart: 11, of which 2 were waited for; matrix products, arithmetic and copies ran while one was open for 4% of the time, Pallas kernels for 11%

profile of v2, /device:TPU:0, one launch (start us, length us, event | category | flops | bytes accessed | tf_op | source)
XLA Modules:
  0.0 759.9 jit_solution(9695754106021197680)
XLA Ops:
  8.1 2.0 collective-permute-start.1
  16.3 2.1 collective-permute-start.2
  27.0 24.8 %shard_map.144 = (bf16[4,4,80,1024]{3,2,1,0:T(8,128)(2,1)S(1)}, bf16[4,4,16,512]{3,2,1,0:T(8,128)(2,1)S(1)}) custom-call(bf16[80,1024]{1,0:T(8,128)(2,1)S(1)} %fusion.59.refs_0_, bf16[16,512]{1,0:T(8,128)(2,1)S(1)} %pad_maximum_fusion.21.refs_1_), custom_call_target="tpu_custom_call" | custom-call | tf_op jit(solution)/shard_map/pallas_call | solution.py:258
  57.6 1.2 fusion.14
  59.9 20.8 %shard_map.145 = (f32[80,1024]{1,0:T(8,128)S(1)}, f32[16,512]{1,0:T(8,128)S(1)}) custom-call(bf16[4,4,80,1024]{3,2,1,0:T(8,128)(2,1)S(1)} %bitcast.320, bf16[4,4,16,512]{3,2,1,0:T(8,128)(2,1)S(1)} %pad_maximum_fusion.3.refs_1_), custom_call_target="tpu_custom_call" | custom-call | tf_op jit(solution)/shard_map/pallas_call | solution.py:287
  82.8 20.0 %shard_map.146 = (bf16[4,4,80,1024]{3,2,1,0:T(8,128)(2,1)S(1)}, bf16[4,4,16,512]{3,2,1,0:T(8,128)(2,1)S(1)}) custom-call(bf16[80,1024]{1,0:T(8,128)(2,1)S(1)} %fusion.68.refs_0_, bf16[16,512]{1,0:T(8,128)(2,1)S(1)} %pad_maximum_fusion.22.refs_1_), custom_call_target="tpu_custom_call" | custom-call | tf_op jit(solution)/shard_map/pallas_call | solution.py:258
  104.1 1.7 convolution_convert_fusion.32
  105.8 2.7 broadcast_select_fusion.1
  108.5 5.4 multiply_convert_fusion.1
  114.8 20.1 %shard_map.147 = f32[80,1024]{1,0:T(8,128)S(1)} custom-call(bf16[4,4,80,1024]{3,2,1,0:T(8,128)(2,1)S(1)} %bitcast.321), custom_call_target="tpu_custom_call" | custom-call | tf_op jit(solution)/shard_map/pallas_call | solution.py:287
  135.6 19.1 %shard_map.148 = bf16[4,4,80,1024]{3,2,1,0:T(8,128)(2,1)S(1)} custom-call(bf16[80,1024]{1,0:T(8,128)(2,1)S(1)} %add_convert_fusion.1.refs_0_), custom_call_target="tpu_custom_call" | custom-call | tf_op jit(solution)/shard_map/pallas_call | solution.py:258
  154.8 1.9 convolution_convert_fusion.6
  159.5 15.0 %shard_map.149 = f32[16,512]{1,0:T(8,128)S(1)} custom-call(bf16[4,4,16,512]{3,2,1,0:T(8,128)(2,1)S(1)} %pad_maximum_fusion.5.refs_0_), custom_call_target="tpu_custom_call" | custom-call | tf_op jit(solution)/shard_map/pallas_call | solution.py:287
  176.8 14.6 %shard_map.150 = bf16[4,4,16,512]{3,2,1,0:T(8,128)(2,1)S(1)} custom-call(bf16[16,512]{1,0:T(8,128)(2,1)S(1)} %pad_maximum_fusion.23.refs_0_), custom_call_target="tpu_custom_call" | custom-call | tf_op jit(solution)/shard_map/pallas_call | solution.py:258
  191.4 1.4 fusion.44
  193.5 15.1 %shard_map.151 = f32[16,512]{1,0:T(8,128)S(1)} custom-call(bf16[4,4,16,512]{3,2,1,0:T(8,128)(2,1)S(1)} %pad_maximum_fusion.7.refs_0_), custom_call_target="tpu_custom_call" | custom-call | tf_op jit(solution)/shard_map/pallas_call | solution.py:287
  210.3 1.4 fusion.129
  212.6 14.8 %shard_map.152 = bf16[4,4,16,512]{3,2,1,0:T(8,128)(2,1)S(1)} custom-call(bf16[16,512]{1,0:T(8,128)(2,1)S(1)} %pad_maximum_fusion.24.refs_0_), custom_call_target="tpu_custom_call" | custom-call | tf_op jit(solution)/shard_map/pallas_call | solution.py:258
  227.5 1.5 add_convert_fusion.2
  229.1 1.4 fusion.22
  232.0 15.1 %shard_map.153 = f32[16,512]{1,0:T(8,128)S(1)} custom-call(bf16[4,4,16,512]{3,2,1,0:T(8,128)(2,1)S(1)} %pad_maximum_fusion.9.refs_0_), custom_call_target="tpu_custom_call" | custom-call | tf_op jit(solution)/shard_map/pallas_call | solution.py:287
  247.7 1.4 multiply_reduce_fusion.12
  249.1 1.4 fusion.156
  250.5 14.4 %shard_map.154 = bf16[4,4,16,512]{3,2,1,0:T(8,128)(2,1)S(1)} custom-call(bf16[16,512]{1,0:T(8,128)(2,1)S(1)} %pad_maximum_fusion.25.refs_0_), custom_call_target="tpu_custom_call" | custom-call | tf_op jit(solution)/shard_map/pallas_call | solution.py:258
  266.1 1.6 convolution_convert_fusion.23
  268.6 1.3 multiply_reduce_fusion.1
  272.9 1.2 convolution_convert_fusion.21
  274.1 2.0 convolution_convert_fusion.2
  276.3 20.2 %shard_map.155 = (f32[80,1024]{1,0:T(8,128)S(1)}, f32[16,512]{1,0:T(8,128)S(1)}) custom-call(bf16[4,4,80,1024]{3,2,1,0:T(8,128)(2,1)S(1)} %bitcast.318, bf16[4,4,16,512]{3,2,1,0:T(8,128)(2,1)S(1)} %pad_maximum_fusion.11.refs_1_), custom_call_target="tpu_custom_call" | custom-call | tf_op jit(solution)/shard_map/pallas_call | solution.py:287
  299.4 22.2 %shard_map.156 = (bf16[4,4,80,1024]{3,2,1,0:T(8,128)(2,1)S(1)}, bf16[4,4,16,512]{3,2,1,0:T(8,128)(2,1)S(1)}) custom-call(bf16[80,1024]{1,0:T(8,128)(2,1)S(1)} %get-tuple-element.67.refs_0_, bf16[16,512]{1,0:T(8,128)(2,1)S(1)} %pad_maximum_fusion.26.refs_1_), custom_call_target="tpu_custom_call" | custom-call | tf_op jit(solution)/shard_map/pallas_call | solution.py:258
  322.9 1.6 convolution_convert_fusion.25
  325.2 1.2 convolution_convert_fusion.15
  327.5 1.7 fusion.24
  330.9 1.7 fusion.23
  333.6 20.0 %shard_map.157 = (f32[80,1024]{1,0:T(8,128)S(1)}, f32[16,512]{1,0:T(8,128)S(1)}) custom-call(bf16[4,4,80,1024]{3,2,1,0:T(8,128)(2,1)S(1)} %bitcast.319, bf16[4,4,16,512]{3,2,1,0:T(8,128)(2,1)S(1)} %pad_maximum_fusion.13.refs_1_), custom_call_target="tpu_custom_call" | custom-call | tf_op jit(solution)/shard_map/pallas_call | solution.py:287
  354.1 18.1 %shard_map.158 = bf16[4,4,80,1024]{3,2,1,0:T(8,128)(2,1)S(1)} custom-call(bf16[80,1024]{1,0:T(8,128)(2,1)S(1)} %get-tuple-element.63.refs_0_), custom_call_target="tpu_custom_call" | custom-call | tf_op jit(solution)/shard_map/pallas_call | solution.py:258
  374.3 1.3 fusion.8
  375.6 3.9 multiply_reduce_fusion
  379.6 4.0 multiply_convert_fusion
  387.6 2.9 collective-permute-start.4
  392.7 1.2 collective-permute-start.7
  395.2 17.9 %shard_map.159 = f32[80,1024]{1,0:T(8,128)S(1)} custom-call(bf16[4,4,80,1024]{3,2,1,0:T(8,128)(2,1)S(1)} %bitcast.322), custom_call_target="tpu_custom_call" | custom-call | tf_op jit(solution)/shard_map/pallas_call | solution.py:287
  415.7 1.4 fusion.34
  419.1 1.4 collective-permute-start.5
  422.3 324.1 %psum.23 = f32[6,1024]{1,0:T(8,128)S(1)} all-reduce(f32[6,1024]{1,0:T(8,128)S(1)} %fusion.112), channel_id=1, replica_groups=mesh['section'=2,'dp'=4,'tensor'=16] {'dp','tensor'}, use_global_device_ids=true, to_apply=%region_47.48 | all-reduce | flops 6144 | bytes 49152 | tf_op jit(solution)/shard_map/psum | solution.py:539
  748.4 1.3 convert_element_type.288
  749.9 1.3 copy-done.14
  751.2 1.5 broadcast_in_dim.31
  (516 shorter events, 68.4 us)
Async XLA Ops:
  7.2 741.1 %all-reduce.3.cloned.1.call-start = ((), (), s32[]{:S(2)}) async-start(), calls=%async_computation | async-start | bytes 3670016 | tf_op jit(solution)/shard_map/psum | solution.py:537
  8.1 12.7 %collective-permute-start.1 = (f32[3,1024]{1,0:T(4,128)S(1)}, f32[3,1024]{1,0:T(4,128)S(1)}, u32[]{:S(2)}, u32[]{:S(2)}) collective-permute-start(f32[3,1024]{1,0:T(4,128)S(1)} %bitcast.395), channel_id=1, source_target_pairs={{0,64},{64,0},{1,65},{65,1},{2,66},{66,2},{3,67},{67,3},{4,68},{68... | collective-permute-start | bytes 36872 | tf_op jit(solution)/shard_map/ppermute | solution.py:304
  10.8 10.0 %collective-permute-start = (f32[3,1024]{1,0:T(4,128)S(1)}, f32[3,1024]{1,0:T(4,128)S(1)}, u32[]{:S(2)}, u32[]{:S(2)}) collective-permute-start(f32[3,1024]{1,0:T(4,128)S(1)} %bitcast.396), channel_id=1, source_target_pairs={{0,64},{64,0},{1,65},{65,1},{2,66},{66,2},{3,67},{67,3},{4,68},{68... | collective-permute-start | bytes 36872 | tf_op jit(solution)/shard_map/ppermute | solution.py:304
  16.3 35.5 %collective-permute-start.2 = (bf16[1024,384]{0,1:T(8,128)(2,1)S(1)}, bf16[1024,384]{0,1:T(8,128)(2,1)S(1)}, u32[]{:S(2)}, u32[]{:S(2)}) collective-permute-start(bf16[1024,384]{0,1:T(8,128)(2,1)S(1)} %bitcast_dynamic-update-slice_fusion), channel_id=1, source_target_pairs={{0,64},{64,0},{1,65},{65,1},{2,66},{66,2},{3,67},{67,3},{4,68},{68... | collective-permute-start | bytes 2359304 | tf_op jit(solution)/shard_map/ppermute | solution.py:304
  18.4 87.4 %collective-permute-start.3 = (bf16[2,1024,256]{2,1,0:T(8,128)(2,1)}, bf16[2,1024,256]{2,1,0:T(8,128)(2,1)}, u32[]{:S(2)}, u32[]{:S(2)}) collective-permute-start(bf16[2,1024,256]{2,1,0:T(8,128)(2,1)} %bitcast.24), channel_id=1, source_target_pairs={{0,64},{64,0},{1,65},{65,1},{2,66},{66,2},{3,67},{67,3},{4,68},{68... | collective-permute-start | bytes 3145736 | tf_op jit(solution)/shard_map/ppermute | solution.py:304
  19.2 32.7 %copy-start.115 = (f32[80]{0:T(128)}, f32[80]{0:T(128)S(1)}, u32[]{:S(2)}) copy-start(f32[80]{0:T(128)S(1)} %broadcast_multiply_fusion.17) | copy-start | bytes 964
  19.5 32.5 %copy-start.120 = (f32[80]{0:T(128)}, f32[80]{0:T(128)S(1)}, u32[]{:S(2)}) copy-start(f32[80]{0:T(128)S(1)} %add_rsqrt_fusion.5) | copy-start | bytes 964
  20.1 32.7 %copy-start.143 = (s32[128]{0:T(128)}, s32[128]{0:T(128)S(1)}, u32[]{:S(2)}) copy-start(s32[128]{0:T(128)S(1)} %fusion.146) | copy-start | bytes 1540
  20.8 34.7 %copy-start.89 = (s32[1280]{0:T(1024)}, s32[1280]{0:T(1024)S(1)}, u32[]{:S(2)}) copy-start(s32[1280]{0:T(1024)S(1)} %fusion.145) | copy-start | bytes 15364
  23.8 28.1 %copy-start.75 = (f32[1,1024]{1,0:T(1,128)}, f32[1,1024]{1,0:T(1,128)S(1)}, u32[]{:S(2)}) copy-start(f32[1,1024]{1,0:T(1,128)S(1)} %get-tuple-element.160) | copy-start | bytes 12292
  26.9 55.4 %copy-start.49 = (f32[1,1024]{1,0:T(1,128)}, f32[1,1024]{1,0:T(1,128)S(1)}, u32[]{:S(2)}) copy-start(f32[1,1024]{1,0:T(1,128)S(1)} %get-tuple-element.157) | copy-start | bytes 12292
  26.9 55.8 %copy-start.55 = (f32[1,1024]{1,0:T(1,128)}, f32[1,1024]{1,0:T(1,128)S(1)}, u32[]{:S(2)}) copy-start(f32[1,1024]{1,0:T(1,128)S(1)} %get-tuple-element.156) | copy-start | bytes 12292
  59.8 21.5 %copy-start.59 = (bf16[2,8,1024]{2,1,0:T(8,128)(2,1)S(1)}, bf16[2,8,1024]{2,1,0:T(8,128)(2,1)}, u32[]{:S(2)}) copy-start(bf16[2,8,1024]{2,1,0:T(8,128)(2,1)} %param.11) | copy-start | bytes 98308
  59.8 21.9 %copy-start.51 = (f32[1,1024]{1,0:T(1,128)S(1)}, f32[1,1024]{1,0:T(1,128)}, u32[]{:S(2)}) copy-start(f32[1,1024]{1,0:T(1,128)} %get-tuple-element.150) | copy-start | bytes 12292
  59.8 21.9 %copy-start.83 = (f32[1,1024]{1,0:T(1,128)S(1)}, f32[1,1024]{1,0:T(1,128)}, u32[]{:S(2)}) copy-start(f32[1,1024]{1,0:T(1,128)} %get-tuple-element.152) | copy-start | bytes 12292
  59.8 22.4 %copy-start.76 = (f32[1,1024]{1,0:T(1,128)S(1)}, f32[1,1024]{1,0:T(1,128)}, u32[]{:S(2)}) copy-start(f32[1,1024]{1,0:T(1,128)} %copy-done.75) | copy-start | bytes 12292
  59.8 22.4 %copy-start.116 = (f32[80]{0:T(128)S(1)}, f32[80]{0:T(128)}, u32[]{:S(2)}) copy-start(f32[80]{0:T(128)} %copy-done.115) | copy-start | bytes 964
  59.8 22.4 %copy-start.121 = (f32[80]{0:T(128)S(1)}, f32[80]{0:T(128)}, u32[]{:S(2)}) copy-start(f32[80]{0:T(128)} %copy-done.120) | copy-start | bytes 964
  59.8 22.8 %copy-start.73 = (f32[1,1024]{1,0:T(1,128)S(1)}, f32[1,1024]{1,0:T(1,128)}, u32[]{:S(2)}) copy-start(f32[1,1024]{1,0:T(1,128)} %get-tuple-element.159) | copy-start | bytes 12292
  81.3 21.6 %copy-start.146 = (f32[128]{0:T(128)S(1)}, f32[128]{0:T(128)}, u32[]{:S(2)}) copy-start(f32[128]{0:T(128)} %copy-done.145) | copy-start | bytes 1540
  81.3 21.6 %copy-start.148 = (f32[128]{0:T(128)S(1)}, f32[128]{0:T(128)}, u32[]{:S(2)}) copy-start(f32[128]{0:T(128)} %copy-done.147) | copy-start | bytes 1540
  81.3 22.2 %copy-start.86 = (f32[1280]{0:T(1024)S(1)}, f32[1280]{0:T(1024)}, u32[]{:S(2)}) copy-start(f32[1280]{0:T(1024)} %copy-done.85) | copy-start | bytes 15364
  81.3 22.2 %copy-start.88 = (f32[1280]{0:T(1024)S(1)}, f32[1280]{0:T(1024)}, u32[]{:S(2)}) copy-start(f32[1280]{0:T(1024)} %copy-done.87) | copy-start | bytes 15364
  82.5 52.5 %copy-start.118 = (f32[80]{0:T(128)}, f32[80]{0:T(128)S(1)}, u32[]{:S(2)}) copy-start(f32[80]{0:T(128)S(1)} %broadcast_multiply_fusion.16) | copy-start | bytes 964
  82.7 52.3 %copy-start.123 = (f32[80]{0:T(128)}, f32[80]{0:T(128)S(1)}, u32[]{:S(2)}) copy-start(f32[80]{0:T(128)S(1)} %add_rsqrt_fusion.3) | copy-start | bytes 964
  114.8 20.1 %copy-start.56 = (f32[1,1024]{1,0:T(1,128)S(1)}, f32[1,1024]{1,0:T(1,128)}, u32[]{:S(2)}) copy-start(f32[1,1024]{1,0:T(1,128)} %copy-done.55) | copy-start | bytes 12292
  114.8 20.1 %copy-start.74 = (f32[1,1024]{1,0:T(1,128)S(1)}, f32[1,1024]{1,0:T(1,128)}, u32[]{:S(2)}) copy-start(f32[1,1024]{1,0:T(1,128)} %get-tuple-element.159) | copy-start | bytes 12292
  114.8 20.6 %copy-start.60 = (f32[1,1024]{1,0:T(1,128)S(1)}, f32[1,1024]{1,0:T(1,128)}, u32[]{:S(2)}) copy-start(f32[1,1024]{1,0:T(1,128)} %get-tuple-element.155) | copy-start | bytes 12292
  114.8 20.6 %copy-start.105 = (f32[1,1024]{1,0:T(1,128)S(1)}, f32[1,1024]{1,0:T(1,128)}, u32[]{:S(2)}) copy-start(f32[1,1024]{1,0:T(1,128)} %get-tuple-element.158) | copy-start | bytes 12292
  276.2 20.2 %copy-start.61 = (f32[1,1024]{1,0:T(1,128)S(1)}, f32[1,1024]{1,0:T(1,128)}, u32[]{:S(2)}) copy-start(f32[1,1024]{1,0:T(1,128)} %get-tuple-element.155) | copy-start | bytes 12292
  276.2 20.2 %copy-start.126 = (f32[80]{0:T(128)S(1)}, f32[80]{0:T(128)}, u32[]{:S(2)}) copy-start(f32[80]{0:T(128)} %copy-done.125) | copy-start | bytes 964
  276.2 20.2 %copy-start.134 = (f32[80]{0:T(128)S(1)}, f32[80]{0:T(128)}, u32[]{:S(2)}) copy-start(f32[80]{0:T(128)} %copy-done.133) | copy-start | bytes 964
  276.2 21.6 %copy-start.48 = (f32[8,1024]{1,0:T(8,128)S(1)}, f32[8,1024]{1,0:T(8,128)}, u32[]{:S(2)}) copy-start(f32[8,1024]{1,0:T(8,128)} %get-tuple-element.70) | copy-start | bytes 98308
  276.2 21.6 %copy-start.53 = (f32[1,1024]{1,0:T(1,128)S(1)}, f32[1,1024]{1,0:T(1,128)}, u32[]{:S(2)}) copy-start(f32[1,1024]{1,0:T(1,128)} %get-tuple-element.150) | copy-start | bytes 12292
  276.2 21.6 %copy-start.92 = (f32[8]{0:T(128)S(1)}, f32[8]{0:T(128)}, u32[]{:S(2)}) copy-start(f32[8]{0:T(128)} %copy-done.91) | copy-start | bytes 100
  276.2 21.6 %copy-start.97 = (f32[8]{0:T(128)S(1)}, f32[8]{0:T(128)}, u32[]{:S(2)}) copy-start(f32[8]{0:T(128)} %copy-done.96) | copy-start | bytes 100
  299.2 25.3 %copy-start.17 = (f32[128,128]{0,1:T(8,128)S(1)}, f32[128,128]{0,1:T(8,128)}, u32[]{:S(2)}) copy-start(f32[128,128]{0,1:T(8,128)} %copy-done.16) | copy-start | bytes 196612
  299.2 25.3 %copy-start.132 = (f32[128]{0:T(128)S(1)}, f32[128]{0:T(128)}, u32[]{:S(2)}) copy-start(f32[128]{0:T(128)} %log_add_fusion.1) | copy-start | bytes 1540
  299.4 25.2 %copy-start.69 = (bf16[128,192]{0,1:T(8,128)(2,1)S(1)}, bf16[128,192]{0,1:T(8,128)(2,1)}, u32[]{:S(2)}) copy-start(bf16[128,192]{0,1:T(8,128)(2,1)} %copy-done.68) | copy-start | bytes 147460
  333.5 20.1 %copy-start.57 = (f32[1,1024]{1,0:T(1,128)S(1)}, f32[1,1024]{1,0:T(1,128)}, u32[]{:S(2)}) copy-start(f32[1,1024]{1,0:T(1,128)} %copy-done.55) | copy-start | bytes 12292
  333.5 20.1 %copy-start.119 = (f32[80]{0:T(128)S(1)}, f32[80]{0:T(128)}, u32[]{:S(2)}) copy-start(f32[80]{0:T(128)} %copy-done.118) | copy-start | bytes 964
  333.6 20.1 %copy-start.124 = (f32[80]{0:T(128)S(1)}, f32[80]{0:T(128)}, u32[]{:S(2)}) copy-start(f32[80]{0:T(128)} %copy-done.123) | copy-start | bytes 964
  387.6 33.5 %collective-permute-start.4 = (bf16[8,512]{1,0:T(8,128)(2,1)S(1)}, bf16[8,512]{1,0:T(8,128)(2,1)S(1)}, u32[]{:S(2)}, u32[]{:S(2)}) collective-permute-start(bf16[8,512]{1,0:T(8,128)(2,1)S(1)} %get-tuple-element.148), channel_id=1, source_target_pairs={{0,64},{64,0},{1,65},{65,1},{2,66},{66,2},{3,67},{67,3},{4,68},{68... | collective-permute-start | bytes 24584 | tf_op jit(solution)/shard_map/ppermute | solution.py:304
  391.2 24.5 %collective-permute-start.8 = (bf16[2,1024,256]{2,1,0:T(8,128)(2,1)S(1)}, bf16[2,1024,256]{2,1,0:T(8,128)(2,1)S(1)}, u32[]{:S(2)}, u32[]{:S(2)}) collective-permute-start(bf16[2,1024,256]{2,1,0:T(8,128)(2,1)S(1)} %fusion.30), channel_id=1, source_target_pairs={{0,64},{64,0},{1,65},{65,1},{2,66},{66,2},{3,67},{67,3},{4,68},{68... | collective-permute-start | bytes 3145736 | tf_op jit(solution)/shard_map/ppermute | solution.py:304
  392.7 21.8 %collective-permute-start.7 = (bf16[1024,384]{0,1:T(8,128)(2,1)S(1)}, bf16[1024,384]{0,1:T(8,128)(2,1)S(1)}, u32[]{:S(2)}, u32[]{:S(2)}) collective-permute-start(bf16[1024,384]{0,1:T(8,128)(2,1)S(1)} %fusion.36), channel_id=1, source_target_pairs={{0,64},{64,0},{1,65},{65,1},{2,66},{66,2},{3,67},{67,3},{4,68},{68... | collective-permute-start | bytes 2359304 | tf_op jit(solution)/shard_map/ppermute | solution.py:304
  394.2 26.3 %collective-permute-start.6 = (bf16[8,512]{1,0:T(8,128)(2,1)S(1)}, bf16[8,512]{1,0:T(8,128)(2,1)S(1)}, u32[]{:S(2)}, u32[]{:S(2)}) collective-permute-start(bf16[8,512]{1,0:T(8,128)(2,1)S(1)} %fusion.143), channel_id=1, source_target_pairs={{0,64},{64,0},{1,65},{65,1},{2,66},{66,2},{3,67},{67,3},{4,68},{68... | collective-permute-start | bytes 24584 | tf_op jit(solution)/shard_map/ppermute | solution.py:304
  418.3 4.0 collective-permute-start.9
  419.1 328.5 %collective-permute-start.5 = (bf16[80,512]{1,0:T(8,128)(2,1)S(1)}, bf16[80,512]{1,0:T(8,128)(2,1)S(1)}, u32[]{:S(2)}, u32[]{:S(2)}) collective-permute-start(bf16[80,512]{1,0:T(8,128)(2,1)S(1)} %bitcast.371), channel_id=1, source_target_pairs={{0,64},{64,0},{1,65},{65,1},{2,66},{66,2},{3,67},{67,3},{4,68},{68... | collective-permute-start | bytes 245768 | tf_op jit(solution)/shard_map/ppermute | solution.py:304
  (115 other events, 482.1 us)
Sparse Core Ops, SparseCore 0:
  417.2 54.5 all-reduce.2

commit v3 on v1

v3 whole, which is shorter than its diff:
```python
import jax
import jax.numpy as jnp
from jax import lax
from jax.experimental import pallas as pl
from jax.experimental.pallas import tpu as pltpu
from jax.sharding import PartitionSpec as P

HEAD = 64
EPSILON = 1e-05
MASKED = -1000000000.0
SCALE = HEAD ** (-0.5)
F32 = jnp.float32
BF16 = jnp.bfloat16
MESH = pl.DeviceIdType.MESH
VM = pl.BlockSpec(memory_space=pltpu.VMEM)
SIDE = 4
DEVICES = SIDE * SIDE
UP = (0, 2)
DOWN = (1, 3)
RING_COPIES = 32
INV_SQRT2 = 0.7071067811865476
INV_SQRT_2PI = 0.3989422804014327
FAR_FIRST = (10, 2, 8, 6, 14, 11, 9, 7, 13, 5, 15, 1, 3, 4, 12)


def norm_parts(values):
    center = values - jnp.mean(values, -1, keepdims=True)
    scale = lax.rsqrt(jnp.mean(center * center, -1, keepdims=True) + EPSILON)
    return center * scale, scale


def norm_back(grad, unit, scale, gains):
    inner = grad * gains
    back = scale * (
        inner
        - jnp.mean(inner, -1, keepdims=True)
        - unit * jnp.mean(inner * unit, -1, keepdims=True)
    )
    return back, jnp.sum(grad * unit, 0, keepdims=True), jnp.sum(grad, 0, keepdims=True)


def gelu_parts(u):
    cdf = 0.5 * (1.0 + lax.erf(u * INV_SQRT2))
    return u * cdf, cdf + u * (INV_SQRT_2PI * jnp.exp(-0.5 * u * u))


def dot(a, b):
    return jnp.dot(a, b, preferred_element_type=F32)


def dot_t(a, b):
    return lax.dot_general(a, b, (((1,), (1,)), ((), ())), preferred_element_type=F32)


def t_dot(a, b):
    return lax.dot_general(a, b, (((0,), (0,)), ((), ())), preferred_element_type=F32)


def scores_of(queries, key_rows, allowed):
    return jnp.where(allowed, dot_t(queries, key_rows) * SCALE, MASKED)


def attend(queries, key_rows, value_rows, allowed):
    scores = scores_of(queries, key_rows, allowed)
    row_max = jnp.max(scores, -1, keepdims=True)
    exponent = jnp.exp(scores - row_max)
    row_sum = jnp.sum(exponent, -1, keepdims=True)
    probs_low = (exponent / row_sum).astype(BF16)
    return dot(probs_low, value_rows).astype(BF16), row_max + jnp.log(row_sum)


def attend_back(queries, key_rows, value_rows, log_total, allowed, attended_grad):
    probs = jnp.exp(scores_of(queries, key_rows, allowed) - log_total)
    value_grad = t_dot(probs.astype(BF16), attended_grad)
    probs_grad = dot_t(attended_grad, value_rows)
    scores_grad = (probs * (probs_grad - jnp.sum(probs * probs_grad, -1, keepdims=True))).astype(
        BF16
    )
    query_grad = dot(scores_grad, key_rows) * SCALE
    key_grad = t_dot(scores_grad, queries) * SCALE
    return query_grad.astype(BF16), key_grad.astype(BF16), value_grad.astype(BF16)


def at_grid():
    index = lax.axis_index("tensor")
    return lax.div(index, SIDE), lax.rem(index, SIDE)


def moved(place, dy, dx):
    return lax.rem(place[0] + dy % SIDE, SIDE), lax.rem(place[1] + dx % SIDE, SIDE)


def along(axis, steps):
    return (steps, 0) if axis == 0 else (0, steps)


def device_at(place):
    return {"tensor": place[0] * SIDE + place[1]}


def neighbours(place):
    return [device_at(moved(place, *along(axis, s))) for axis in range(2) for s in (1, -1)]


def greet(devices):
    barrier = pltpu.get_barrier_semaphore()
    for device in devices:
        pl.semaphore_signal(barrier, inc=1, device_id=device, device_id_type=MESH)
    pl.semaphore_wait(barrier, len(devices))


def sections():
    section, dp = lax.axis_index("section"), lax.axis_index("dp")
    zh, core = lax.div(dp, 2), lax.rem(dp, 2)
    return section, zh, core, {"section": 1 - section}, {"dp": zh * 2 + 1 - core}


class Links:
    def __init__(self, send_sems, recv_sems):
        self.send, self.recv, self.used, self.started = send_sems, recv_sems, 0, []

    def start(self, source, target, device):
        n = self.used
        self.used += 1
        copy = pltpu.make_async_remote_copy(
            src_ref=source,
            dst_ref=target,
            send_sem=self.send.at[n],
            recv_sem=self.recv.at[n],
            device_id=device,
            device_id_type=MESH,
        )
        copy.start()
        self.started.append(copy)
        return copy

    def finish(self):
        for copy in self.started:
            copy.wait_send()
        self.started = []


def sems(n):
    return [pltpu.SemaphoreType.DMA((n,)), pltpu.SemaphoreType.DMA((n,))]


def shape(dims, kind):
    return jax.ShapeDtypeStruct(tuple(dims), kind)


def params(collective_id):
    return pltpu.CompilerParams(
        collective_id=collective_id, has_side_effects=True, vmem_limit_bytes=56 << 20
    )


def fold(rows):
    half = rows.shape[1] // 2
    return jnp.concatenate([rows[:, :half], rows[:, half:]], 0)


def unfold(rows):
    count = rows.shape[0] // 2
    return jnp.concatenate([rows[:count], rows[count:]], 1)


def unfold_all(blocks):
    count, half = blocks.shape[2] // 2, blocks.shape[3]
    split = blocks.astype(F32).reshape(DEVICES, 2, count, half)
    low = split[:, 0].reshape(DEVICES * count, half)
    high = split[:, 1].reshape(DEVICES * count, half)
    return jnp.concatenate([low, high], 1).astype(BF16)


def fold_all(part):
    count, half = part.shape[0] // DEVICES, part.shape[1] // 2
    split = part.reshape(DEVICES, count, 2 * half)
    both = jnp.concatenate([split[:, :, :half], split[:, :, half:]], 1)
    return both.astype(BF16).reshape(SIDE, SIDE, 2 * count, half)


def gather(links, place, bufs, ready=None):
    jobs = []
    for buf in bufs:
        half = buf.shape[-1] // 2
        for h in range(2):
            jobs.append((buf, 1 - h, h, h * half, half))
    ready = ready or (lambda group: None)

    def send(job, axis, steps, r, s, part=None):
        buf, a, b, start, size = job
        y, x = moved(moved(place, *along(a, r)), *along(b, s))
        if part is not None:
            size = size // 2
            start = start + part * size
        ref = buf.at[y, x, :, pl.ds(start, size)]
        return links.start(ref, ref, device_at(moved(place, *along(axis, steps))))

    first, spread, second, ahead = [], [], [], []
    for job in jobs:
        first.append([send(job, job[1], 1, 0, 0), send(job, job[1], -1, 0, 0)])
    for job in jobs:
        spread.append({0: [send(job, job[2], 1, 0, 0), send(job, job[2], -1, 0, 0)]})
    ready([(0, 0)])
    for i, job in enumerate(jobs):
        a, b = job[1], job[2]
        first[i][0].wait_recv()
        one = send(job, a, 1, -1, 0, 0)
        spread[i][3] = [send(job, b, 1, -1, 0), send(job, b, -1, -1, 0)]
        first[i][1].wait_recv()
        two = send(job, a, -1, 1, 0, 1)
        spread[i][1] = [send(job, b, 1, 1, 0), send(job, b, -1, 1, 0)]
        second.append([one, two])
    for i, job in enumerate(jobs):
        spread[i][0][0].wait_recv()
        ahead.append([send(job, job[2], 1, 0, -1)])
    for i, job in enumerate(jobs):
        spread[i][0][1].wait_recv()
    ready([(0, 1), (0, 3), (1, 0), (3, 0)])
    for i, job in enumerate(jobs):
        second[i][0].wait_recv()
        second[i][1].wait_recv()
        spread[i][2] = [send(job, job[2], 1, 2, 0), send(job, job[2], -1, 2, 0)]
    for i, job in enumerate(jobs):
        for r in DOWN:
            spread[i][r][1].wait_recv()
            ahead[i].append(send(job, job[2], -1, r, 1))
    for i, job in enumerate(jobs):
        spread[i][2][0].wait_recv()
        ahead[i].append(send(job, job[2], 1, 2, -1))
    for i, job in enumerate(jobs):
        for r in DOWN:
            spread[i][r][0].wait_recv()
    ready([(1, 1), (1, 3), (3, 1), (3, 3)])
    for i, job in enumerate(jobs):
        ahead[i][0].wait_recv()
    ready([(0, 2), (2, 0)])
    for i, job in enumerate(jobs):
        spread[i][2][1].wait_recv()
        ahead[i][1].wait_recv()
        ahead[i][2].wait_recv()
    ready([(1, 2), (3, 2), (2, 1), (2, 3)])
    for i, job in enumerate(jobs):
        ahead[i][3].wait_recv()
    ready([(2, 2)])


PRODUCE = (
    [(2, 2), (2, 3), (2, 1), (3, 2), (1, 2), (2, 0), (0, 2)],
    [(3, 3), (3, 1), (1, 3), (1, 1), (3, 0), (1, 0), (0, 3), (0, 1), (0, 0)],
)


def sum_blocks(links, place, parts, produce=None):
    produce = produce or (lambda group: None)
    jobs = []
    for part, land in parts:
        half = part.shape[-1] // 2
        for h in range(2):
            jobs.append((part, land, 15 * h, 1 - h, h, h * half, half))

    def block(job, r, s, quarter=None):
        part, _, _, a, b, start, size = job
        y, x = moved(moved(place, *along(a, r)), *along(b, s))
        if quarter is not None:
            size = size // 2
            start = start + quarter * size
        return part.at[y, x, :, pl.ds(start, size)]

    def landing(job, n, quarter=None):
        ref = job[1].at[job[2] + n]
        if quarter is None:
            return ref
        size = job[6] // 2
        return ref.at[:, pl.ds(quarter * size, size)]

    def start(source, target, axis, steps):
        return links.start(source, target, device_at(moved(place, *along(axis, steps))))

    def add(target, *others):
        total = target[...].astype(F32)
        for other in others:
            total = total + other[...].astype(F32)
        return total

    def near_slot(job, r, steps):
        return landing(job, 4 + 2 * r + (0 if steps == 1 else 1))

    order = (2, 3, 1, 0)
    produce(PRODUCE[0])
    far = []
    for job in jobs:
        far.append(
            {r: start(block(job, r, 2), landing(job, r), job[4], 1 if r in UP else -1) for r in order}
        )
    produce(PRODUCE[1])
    near = []
    for job in jobs:
        sent = {}
        for r in order:
            steps = -1 if r in UP else 1
            sent[r] = [start(block(job, r, steps), near_slot(job, r, steps), job[4], steps)]
        near.append(sent)
    for r in order:
        for i, job in enumerate(jobs):
            steps = 1 if r in UP else -1
            far[i][r].wait_recv()
            ref = block(job, r, steps)
            ref[...] = add(ref, landing(job, r)).astype(BF16)
            near[i][r].append(start(ref, near_slot(job, r, steps), job[4], steps))
    opposite, last = [], []
    for r in order[:3]:
        for i, job in enumerate(jobs):
            for copy in near[i][r]:
                copy.wait_recv()
            ref = block(job, r, 0)
            total = add(ref, landing(job, 4 + 2 * r), landing(job, 5 + 2 * r))
            if r == 2:
                ref[...] = total.astype(BF16)
                opposite.append(
                    [
                        start(block(job, 2, 0, 0), landing(job, 12, 0), job[3], 1),
                        start(block(job, 2, 0, 1), landing(job, 12, 1), job[3], -1),
                    ]
                )
                last.append({})
            else:
                quarter = 0 if r == 1 else 1
                opposite[i][quarter].wait_recv()
                size = job[6] // 2
                extra = landing(job, 12, quarter)[...].astype(F32)
                low, high = total[:, :size], total[:, size:]
                if quarter == 0:
                    low = low + extra
                else:
                    high = high + extra
                ref[:, pl.ds(0, size)] = low.astype(BF16)
                ref[:, pl.ds(size, size)] = high.astype(BF16)
                last[i][r] = start(
                    ref, landing(job, 13 if r == 1 else 14), job[3], 1 if r == 1 else -1
                )
    results = []
    for i, job in enumerate(jobs):
        for copy in near[i][0]:
            copy.wait_recv()
        last[i][1].wait_recv()
        last[i][3].wait_recv()
        results.append(
            add(block(job, 0, 0), landing(job, 4), landing(job, 5), landing(job, 13), landing(job, 14))
        )
    return [jnp.concatenate(results[i : i + 2], 1) for i in range(0, len(results), 2)]


def gather_small(links, place, buf, rows):
    y, x = place
    buf[y, x] = fold(rows).astype(BF16)
    copies = []
    for d in FAR_FIRST:
        target = device_at(moved(place, d // SIDE, d % SIDE))
        copies.append(links.start(buf.at[y, x], buf.at[y, x], target))
    for copy in copies:
        copy.wait_recv()
    return unfold_all(buf[...])


def sum_small(links, place, work, land, part):
    work[...] = fold_all(part)
    copies = []
    for n, d in enumerate(FAR_FIRST):
        there = moved(place, d // SIDE, d % SIDE)
        copies.append(links.start(work.at[there[0], there[1]], land.at[n], device_at(there)))
    total = work[place[0], place[1]].astype(F32)
    for copy in copies:
        copy.wait_recv()
    return unfold(total + jnp.sum(land[...].astype(F32), 0))


def stacked(ref, place, group):
    blocks = []
    for dy, dx in group:
        y, x = moved(place, dy, dx)
        blocks.append(ref[y, x])
    return blocks[0] if len(blocks) == 1 else jnp.concatenate(blocks, 0)


def store_blocks(ref, place, group, rows):
    count = ref.shape[2]
    for n, (dy, dx) in enumerate(group):
        y, x = moved(place, dy, dx)
        ref[y, x] = rows[n * count : (n + 1) * count]


def wide(scale):
    return jnp.broadcast_to(scale, (scale.shape[0], 128))


def first_kernel(
    x, y, wt_in, gs_in, wt, gs, full_h0, h0, unit0, scale0, full_y, q, k, v, sq, sk, sv, *scratch
):
    xbuf, ybuf, send, recv = scratch
    place = at_grid()
    section, _, core, partner, sibling = sections()
    greet(neighbours(place) + [partner, sibling])
    links = Links(send, recv)
    half = wt_in.shape[0] // 2
    mine = pl.ds(core * half, half)
    gains_copy = links.start(gs_in, gs.at[section], partner)
    xbuf[place[0], place[1]] = x[...]
    ybuf[place[0], place[1]] = fold(y[...].astype(F32)).astype(BF16)
    passed = []

    def ready(group):
        if group == [(0, 0)]:
            passed.append(links.start(wt_in.at[mine], wt.at[section, mine], partner))
            gs[section] = gs_in[...]
            wt[section] = wt_in[...]
            gains_copy.wait_recv()
        if group == [(1, 1), (1, 3), (3, 1), (3, 3)]:
            passed[0].wait_recv()
            theirs = wt.at[1 - section, mine]
            passed.append(links.start(theirs, theirs, sibling))
        unit, scale = norm_parts(stacked(xbuf, place, group).astype(F32))
        rows = unit * gs[0, 0:1, :] + gs[0, 3:4, :]
        if group == [(0, 0)]:
            h0[...] = rows
            unit0[...] = unit
            scale0[...] = wide(scale)
        store_blocks(full_h0, place, group, rows.astype(BF16))

    gather(links, place, [xbuf, ybuf], ready)
    passed[1].wait_recv()
    count, width = x.shape
    for i in range(SIDE):
        rows = full_h0[i].reshape(SIDE * count, width)
        made = dot_t(rows, wt[0, 0 : 3 * HEAD, :]).astype(BF16)
        for j, ref in enumerate((q, k, v)):
            ref[i] = made[:, j * HEAD : (j + 1) * HEAD].reshape(SIDE, count, HEAD)
    rows = unfold_all(ybuf[...])
    full_y[...] = rows
    made = dot_t(rows, wt[1, 0 : 3 * HEAD, :]).astype(BF16)
    for j, ref in enumerate((sq, sk, sv)):
        ref[...] = made[:, j * HEAD : (j + 1) * HEAD]
    links.finish()


def first_call(x, y, wt, gs, collective_id):
    (rows, width), count = x.shape, y.shape[0]
    full = count * DEVICES
    return pl.pallas_call(
        first_kernel,
        out_shape=[
            shape((2, *wt.shape), BF16),
            shape((2, *gs.shape), F32),
            shape((SIDE, SIDE, rows, width), BF16),
            shape((rows, width), F32),
            shape((rows, width), F32),
            shape((rows, 128), F32),
            shape((full, width), BF16),
        ]
        + [shape((SIDE, SIDE, rows, HEAD), BF16)] * 3
        + [shape((full, HEAD), BF16)] * 3,
        in_specs=[VM] * 4,
        out_specs=[VM] * 13,
        scratch_shapes=[
            pltpu.VMEM((SIDE, SIDE, rows, width), BF16),
            pltpu.VMEM((SIDE, SIDE, 2 * count, width // 2), BF16),
        ]
        + sems(2 * RING_COPIES + 3),
        compiler_params=params(collective_id),
    )(x, y, wt, gs)


def forward_kernel(att_e, att_d, h0, y, wt, gs, ffn_in, *rest):
    (ffn, full_h1, full_m, full_d1, hidden, slope, kvc, cq, d1) = rest[:9]
    (unit1, scale1, unit2, scale2, dunit0, dscale0) = rest[9:15]
    (part, dpart, land_1, land_2, land_d, d1buf, send, recv) = rest[15:]
    place = at_grid()
    section, _, core, partner, sibling = sections()
    greet(neighbours(place) + [partner, sibling])
    links = Links(send, recv)
    passed = [links.start(ffn_in.at[core], ffn.at[section, core], partner)]

    def attended(group):
        rows = dot(stacked(att_e, place, group), wt[0, 3 * HEAD : 4 * HEAD, :])
        store_blocks(part, place, group, rows.astype(BF16))
        if group == PRODUCE[0]:
            dpart[...] = fold_all(dot(att_d[...], wt[1, 3 * HEAD : 4 * HEAD, :]))
        else:
            ffn[section] = ffn_in[...]

    sum_e, sum_d = sum_blocks(links, place, [(part, land_1), (dpart, land_d)], attended)
    passed[0].wait_recv()
    theirs = ffn.at[1 - section, core]
    passed.append(links.start(theirs, theirs, sibling))
    unit, scale = norm_parts(h0[...] + sum_e)
    unit1[...] = unit
    scale1[...] = wide(scale)
    h1 = unit * gs[0, 1:2, :] + gs[0, 4:5, :]
    full_h1[place[0], place[1]] = h1.astype(BF16)
    unit, scale = norm_parts(y[...].astype(F32) + unfold(sum_d))
    dunit0[...] = unit
    dscale0[...] = wide(scale)
    rows = unit * gs[1, 0:1, :] + gs[1, 3:4, :]
    d1[...] = rows
    d1buf[place[0], place[1]] = fold(rows).astype(BF16)

    def up(group):
        if group == [(0, 0)]:
            return
        if group == [(0, 1), (0, 3), (1, 0), (3, 0)]:
            passed[1].wait_recv()
            group = [(0, 0)] + group
        made, back = gelu_parts(dot(stacked(full_h1, place, group), ffn[0, 0]))
        store_blocks(hidden, place, group, made.astype(BF16))
        store_blocks(slope, place, group, back)

    gather(links, place, [full_h1, d1buf], up)
    links.finish()
    rows = unfold_all(d1buf[...])
    full_d1[...] = rows
    cq[...] = dot_t(rows, wt[1, 4 * HEAD : 5 * HEAD, :]).astype(BF16)

    def down(group):
        rows = dot_t(stacked(hidden, place, group), ffn[0, 1])
        store_blocks(part, place, group, rows.astype(BF16))

    (sum_e,) = sum_blocks(links, place, [(part, land_2)], down)
    unit, scale = norm_parts(h1 + sum_e)
    unit2[...] = unit
    scale2[...] = wide(scale)
    full_m[place[0], place[1]] = (unit * gs[0, 2:3, :] + gs[0, 5:6, :]).astype(BF16)

    def cross(group):
        rows = dot_t(stacked(full_m, place, group), wt[0, 4 * HEAD : 6 * HEAD, :])
        store_blocks(kvc, place, group, rows.astype(BF16))

    gather(links, place, [full_m], cross)
    links.finish()


def forward_call(att_e, att_d, h0, y, wt, gs, ffn, collective_id):
    (rows, width), count = h0.shape, y.shape[0]
    full, inner = count * DEVICES, ffn.shape[2]
    grid = (SIDE, SIDE)
    return pl.pallas_call(
        forward_kernel,
        out_shape=[
            shape((2, *ffn.shape), BF16),
            shape((*grid, rows, width), BF16),
            shape((*grid, rows, width), BF16),
            shape((full, width), BF16),
            shape((*grid, rows, inner), BF16),
            shape((*grid, rows, inner), F32),
            shape((*grid, rows, 2 * HEAD), BF16),
            shape((full, HEAD), BF16),
            shape((count, width), F32),
            shape((rows, width), F32),
            shape((rows, 128), F32),
            shape((rows, width), F32),
            shape((rows, 128), F32),
            shape((count, width), F32),
            shape((count, 128), F32),
        ],
        in_specs=[VM] * 7,
        out_specs=[VM] * 15,
        scratch_shapes=[
            pltpu.VMEM((*grid, rows, width), BF16),
            pltpu.VMEM((*grid, 2 * count, width // 2), BF16),
            pltpu.VMEM((30, rows, width // 2), BF16),
            pltpu.VMEM((30, rows, width // 2), BF16),
            pltpu.VMEM((30, 2 * count, width // 4), BF16),
            pltpu.VMEM((*grid, 2 * count, width // 2), BF16),
        ]
        + sems(6 * RING_COPIES + 2),
        compiler_params=params(collective_id),
    )(att_e, att_d, h0, y, wt, gs, ffn)


def decoder_kernel(cq, kvc, d1, cot, seg_d, seg_e, wt, ffn, gs, *rest):
    (d3, dback1, full_d2, full_db2, full_db1, hid_out, pre_out, att_out) = rest[:8]
    (cq_grad, kvc_grad, grads, g_bufs, s_work, s_land, probs, send, recv) = rest[8:]
    place = at_grid()
    greet([device_at(moved(place, d // SIDE, d % SIDE)) for d in range(1, DEVICES)])
    links = Links(send, recv)
    w5 = wt[1, 5 * HEAD : 6 * HEAD, :]
    kc, vc = kvc[:, :HEAD], kvc[:, HEAD:]
    scores = scores_of(cq[...], kc, seg_d[...] == seg_e[...])
    exponent = jnp.exp(scores - jnp.max(scores, -1, keepdims=True))
    probs[...] = exponent / jnp.sum(exponent, -1, keepdims=True)
    att = dot(probs[...].astype(BF16), vc).astype(BF16)
    att_out[...] = att
    part = sum_small(links, place, s_work.at[0], s_land.at[0], dot(att, w5))
    unit1, scale1 = norm_parts(d1[...] + part)
    d2 = unit1 * gs[1, 1:2, :] + gs[1, 4:5, :]
    full = gather_small(links, place, g_bufs.at[0], d2)
    full_d2[...] = full
    hidden, slope = gelu_parts(dot(full, ffn[1, 0]))
    hidden = hidden.astype(BF16)
    hid_out[...] = hidden
    part = sum_small(links, place, s_work.at[1], s_land.at[1], dot_t(hidden, ffn[1, 1]))
    unit2, scale2 = norm_parts(d2 + part)
    d3[...] = unit2 * gs[1, 2:3, :] + gs[1, 5:6, :]
    back2, gain2, shift2 = norm_back(cot[...].astype(F32), unit2, scale2, gs[1, 2:3, :])
    full = gather_small(links, place, g_bufs.at[1], back2)
    full_db2[...] = full
    pre = (dot(full, ffn[1, 1]) * slope).astype(BF16)
    pre_out[...] = pre
    part = sum_small(links, place, s_work.at[2], s_land.at[2], dot_t(pre, ffn[1, 0]))
    back1, gain1, shift1 = norm_back(back2 + part, unit1, scale1, gs[1, 1:2, :])
    dback1[...] = back1
    full = gather_small(links, place, g_bufs.at[2], back1)
    full_db1[...] = full
    att_grad = dot_t(full, w5).astype(BF16)
    p = probs[...]
    value_grad = t_dot(p.astype(BF16), att_grad)
    p_grad = dot_t(att_grad, vc)
    s_grad = (p * (p_grad - jnp.sum(p * p_grad, -1, keepdims=True))).astype(BF16)
    cq_grad[...] = (dot(s_grad, kc) * SCALE).astype(BF16)
    key_grad = t_dot(s_grad, cq[...]) * SCALE
    kvc_grad[...] = jnp.concatenate([key_grad, value_grad], 1).astype(BF16)
    grads[0:1, :] = gain1
    grads[1:2, :] = gain2
    grads[2:3, :] = shift1
    grads[3:4, :] = shift2
    grads[4:8, :] = jnp.zeros((4, grads.shape[1]), F32)
    links.finish()


def decoder_call(cq, kvc, d1, cot, seg_d, seg_e, wt, ffn, gs, collective_id):
    rows, width = d1.shape
    full, hidden = DEVICES * rows, ffn.shape[3]
    block = (SIDE, SIDE, 2 * rows, width // 2)
    return pl.pallas_call(
        decoder_kernel,
        out_shape=[
            shape((rows, width), F32),
            shape((rows, width), F32),
            shape((full, width), BF16),
            shape((full, width), BF16),
            shape((full, width), BF16),
            shape((full, hidden), BF16),
            shape((full, hidden), BF16),
            shape((full, HEAD), BF16),
            shape((full, HEAD), BF16),
            shape(kvc.shape, BF16),
            shape((8, width), F32),
        ],
        in_specs=[VM] * 9,
        out_specs=[VM] * 11,
        scratch_shapes=[
            pltpu.VMEM((3, *block), BF16),
            pltpu.VMEM((3, *block), BF16),
            pltpu.VMEM((3, DEVICES - 1, *block[2:]), BF16),
            pltpu.VMEM((full, kvc.shape[0]), F32),
        ]
        + sems(6 * (DEVICES - 1)),
        compiler_params=params(collective_id),
    )(cq, kvc, d1, cot, seg_d, seg_e, wt, ffn, gs)


def backward_kernel(*refs):
    (kvc_grad, cq_grad, dback1, wt, gs, ffn, unit1, scale1, unit2, scale2) = refs[:10]
    (dunit0, dscale0, slope, sq, sk, sv, log_d, seg_d, seg_dt) = refs[10:19]
    (full_b2, full_b1, full_db0, pre, dqkv_grad, att_grad, back1, dec_grad, grads) = refs[19:28]
    (part, dpart_1, dpart_2, land_1, land_2, dland_1, dland_2, dbuf, send, recv) = refs[28:]
    place = at_grid()
    greet(neighbours(place))
    links = Links(send, recv)

    def cross(group):
        rows = dot(stacked(kvc_grad, place, group), wt[0, 4 * HEAD : 6 * HEAD, :])
        store_blocks(part, place, group, rows.astype(BF16))

    dpart_1[...] = fold_all(dot(cq_grad[...], wt[1, 4 * HEAD : 5 * HEAD, :]))
    sum_e, sum_d = sum_blocks(links, place, [(part, land_1), (dpart_1, dland_1)], cross)
    back2, gain2, shift2 = norm_back(sum_e, unit2[...], scale2[:, 0:1], gs[0, 2:3, :])
    full_b2[place[0], place[1]] = back2.astype(BF16)
    dback0, dgain0, dshift0 = norm_back(
        dback1[...] + unfold(sum_d), dunit0[...], dscale0[:, 0:1], gs[1, 0:1, :]
    )
    dbuf[place[0], place[1]] = fold(dback0).astype(BF16)

    def down(group):
        rows = dot(stacked(full_b2, place, group), ffn[0, 1]) * stacked(slope, place, group)
        store_blocks(pre, place, group, rows.astype(BF16))

    gather(links, place, [full_b2, dbuf], down)
    links.finish()
    rows = unfold_all(dbuf[...])
    full_db0[...] = rows
    count = rows.shape[0]
    att_d_grad = dot_t(rows, wt[1, 3 * HEAD : 4 * HEAD, :]).astype(BF16)
    before = lax.broadcasted_iota(jnp.int32, (count, count), 1) <= lax.broadcasted_iota(
        jnp.int32, (count, count), 0
    )
    allowed = (seg_d[...] == seg_dt[...]) & before
    made = attend_back(sq[...], sk[...], sv[...], log_d[...], allowed, att_d_grad)
    made = jnp.concatenate([m.astype(F32) for m in made], 1).astype(BF16)
    dqkv_grad[...] = made
    dpart_2[...] = fold_all(dot(made, wt[1, 0 : 3 * HEAD, :]))

    def up(group):
        rows = dot_t(stacked(pre, place, group), ffn[0, 0])
        store_blocks(part, place, group, rows.astype(BF16))

    sum_e, sum_d = sum_blocks(links, place, [(part, land_2), (dpart_2, dland_2)], up)
    dec_grad[...] = dback0 + unfold(sum_d)
    rows, gain1, shift1 = norm_back(back2 + sum_e, unit1[...], scale1[:, 0:1], gs[0, 1:2, :])
    back1[...] = rows
    full_b1[place[0], place[1]] = rows.astype(BF16)

    def mixed(group):
        rows = dot_t(stacked(full_b1, place, group), wt[0, 3 * HEAD : 4 * HEAD, :])
        store_blocks(att_grad, place, group, rows.astype(BF16))

    gather(links, place, [full_b1], mixed)
    for i, row in enumerate((gain1, gain2, shift1, shift2, dgain0, dshift0)):
        grads[i : i + 1, :] = row
    grads[6:8, :] = jnp.zeros((2, grads.shape[1]), F32)
    links.finish()


def backward_call(args, collective_id):
    kvc_grad, cq_grad, dback1 = args[:3]
    rows, (count, width) = kvc_grad.shape[2], dback1.shape
    full, inner = count * DEVICES, args[5].shape[3]
    grid = (SIDE, SIDE)
    small = (*grid, 2 * count, width // 2)
    return pl.pallas_call(
        backward_kernel,
        out_shape=[
            shape((*grid, rows, width), BF16),
            shape((*grid, rows, width), BF16),
            shape((full, width), BF16),
            shape((*grid, rows, inner), BF16),
            shape((full, 3 * HEAD), BF16),
            shape((*grid, rows, HEAD), BF16),
            shape((rows, width), F32),
            shape((count, width), F32),
            shape((8, width), F32),
        ],
        in_specs=[VM] * 19,
        out_specs=[VM] * 9,
        scratch_shapes=[
            pltpu.VMEM((*grid, rows, width), BF16),
            pltpu.VMEM(small, BF16),
            pltpu.VMEM(small, BF16),
            pltpu.VMEM((30, rows, width // 2), BF16),
            pltpu.VMEM((30, rows, width // 2), BF16),
            pltpu.VMEM((30, 2 * count, width // 4), BF16),
            pltpu.VMEM((30, 2 * count, width // 4), BF16),
            pltpu.VMEM(small, BF16),
        ]
        + sems(7 * RING_COPIES),
        compiler_params=params(collective_id),
    )(*args)


def last_kernel(
    qkv_grad, wt, gs, back1, unit0, scale0, att, ffn, small, out3, dec, *rest
):
    (att_out, ffn_out, small_out, enc_out, out3_out, dec_out) = rest[:6]
    (part, land, work_a, work_f, core_a, core_f, side_a, side_f) = rest[6:14]
    (pass_a, pass_f, over_a, over_f, sums, fin, core_s, z_s, y_s, x_s) = rest[14:24]
    (enc, give_e, give_d, land_e, land_d, send, recv) = rest[24:]
    place = at_grid()
    section, zh, core, partner, sibling = sections()
    other = 1 - section
    zh_plus = lax.rem(zh + section, 2)
    plus = {"section": other, "dp": zh_plus * 2 + core}
    minus = {"section": other, "dp": (1 - zh_plus) * 2 + core}
    far = {"dp": (1 - zh) * 2 + core}
    columns = [device_at(moved(place, d, 0)) for d in (1, 2, 3)]
    rows = [device_at(moved(place, 0, d)) for d in (1, 2, 3)]
    greet([sibling, plus, minus, far, *columns, *rows])
    links = Links(send, recv)
    jobs = [
        (att, work_a, core_a, side_a, pass_a, over_a, att_out),
        (ffn, work_f, core_f, side_f, pass_f, over_f, ffn_out),
    ]
    step_core, step_side = [], []
    for grad, _, core_land, *_ in jobs:
        half = grad.shape[1] // 2
        step_core.append(
            links.start(grad.at[:, pl.ds((1 - core) * half, half)], core_land, sibling)
        )
    width = enc.shape[1] // 2
    there = pl.ds(pl.multiple_of(other * width, width), width)
    here = pl.ds(pl.multiple_of(section * width, width), width)
    give_d[...] = jnp.concatenate([out3[:, there], dec[:, there]], 0).astype(BF16)
    swap_d = links.start(give_d, land_d, partner)

    def heads(group):
        made = dot(stacked(qkv_grad, place, group), wt[0, 0 : 3 * HEAD, :])
        store_blocks(part, place, group, made.astype(BF16))
        if group == PRODUCE[0]:
            return
        for i, (grad, work, core_land, side, *_) in enumerate(jobs):
            half = grad.shape[1] // 2
            quarter = half // 2
            step_core[i].wait_recv()
            work[...] = (
                grad[:, pl.ds(core * half, half)].astype(F32) + core_land[...].astype(F32)
            ).astype(BF16)
            step_side.append(
                [
                    links.start(work.at[other, pl.ds(h * quarter, quarter)], side.at[n], d)
                    for n, (h, d) in enumerate(((zh_plus, plus), (1 - zh_plus, minus)))
                ]
            )

    (sum_e,) = sum_blocks(links, place, [(part, land)], heads)
    enc[...], gain0, shift0 = norm_back(
        back1[...] + sum_e, unit0[...], scale0[:, 0:1], gs[0, 0:1, :]
    )
    sums[...] = small[...]
    sums[0, 0:1, :] = gain0
    sums[0, 3:4, :] = shift0
    one = links.start(sums.at[1 - core], core_s, sibling)
    give_e[...] = enc[:, there].astype(BF16)
    swap_e = links.start(give_e, land_e, partner)
    step_pass = []
    for i, (grad, work, core_land, side, passing, over, _) in enumerate(jobs):
        quarter = grad.shape[1] // 4
        for copy in step_side[i]:
            copy.wait_recv()
        mine = work.at[section, pl.ds(zh * quarter, quarter)]
        mine[...] = (
            mine[...].astype(F32) + side[0].astype(F32) + side[1].astype(F32)
        ).astype(BF16)
        step_pass.append(
            [
                links.start(work.at[section, pl.ds(n * quarter, quarter)], passing.at[n], d)
                for n, d in enumerate((plus, minus))
            ]
        )

    def exchange(land_s, devices):
        copies = [links.start(fin.at[core], land_s.at[n], d) for n, d in enumerate(devices)]
        for copy in copies:
            copy.wait_recv()
        links.finish()
        fin[core] = fin[core] + land_s[0] + land_s[1] + land_s[2]

    one.wait_recv()
    fin[core] = sums[core] + core_s[...]
    exchange(y_s, columns)
    exchange(x_s, rows)
    step_over = []
    for i, (grad, work, core_land, side, passing, over, _) in enumerate(jobs):
        quarter = grad.shape[1] // 4
        ahead = []
        for n, device in enumerate((plus, minus)):
            step_pass[i][n].wait_recv()
            ahead.append(
                links.start(passing.at[n], over.at[pl.ds(n * quarter, quarter)], device)
            )
        step_over.append(ahead)
    exchange(z_s, [plus, minus, far])
    five = links.start(fin.at[core], fin.at[core], sibling)
    swap_e.wait_recv()
    swap_d.wait_recv()
    enc_out[section] = enc[:, here]
    enc_out[other] = land_e[...].astype(F32)
    got = land_d[...].astype(F32)
    count = out3.shape[0]
    out3_out[section] = out3[:, here]
    out3_out[other] = got[:count]
    dec_out[section] = dec[:, here]
    dec_out[other] = got[count:]
    last = []
    for i, (grad, work, core_land, side, passing, over, out) in enumerate(jobs):
        for copy in step_over[i]:
            copy.wait_recv()
        out[core] = (work[section].astype(F32) + over[...].astype(F32)).astype(BF16)
        last.append(links.start(out.at[core], out.at[core], sibling))
    five.wait_recv()
    small_out[...] = fin[section]
    for copy in last:
        copy.wait_recv()
    links.finish()


def last_call(args, collective_id):
    qkv_grad, back1, (att, ffn, small, out3, dec) = args[0], args[3], args[6:]
    rows, cols = back1.shape
    count, width = dec.shape[0], cols // 2
    grads = (att, ffn)

    def lands(lead):
        return [pltpu.VMEM((*lead(g), g.shape[2]), BF16) for g in grads]

    half = lambda g: (2, g.shape[1] // 2)
    quarter = lambda g: (2, g.shape[1] // 4)
    return pl.pallas_call(
        last_kernel,
        out_shape=[shape((*half(g), g.shape[2]), BF16) for g in grads]
        + [
            shape(small.shape[1:], F32),
            shape((2, rows, width), F32),
            shape((2, count, width), F32),
            shape((2, count, width), F32),
        ],
        in_specs=[VM] * 11,
        out_specs=[VM] * 6,
        scratch_shapes=[
            pltpu.VMEM((SIDE, SIDE, rows, cols), BF16),
            pltpu.VMEM((30, rows, width), BF16),
        ]
        + lands(half)
        + lands(half)
        + lands(quarter)
        + lands(quarter)
        + lands(lambda g: half(g)[1:])
        + [
            pltpu.VMEM(small.shape, F32),
            pltpu.VMEM(small.shape, F32),
            pltpu.VMEM(small.shape[1:], F32),
            pltpu.VMEM((3, *small.shape[1:]), F32),
            pltpu.VMEM((3, *small.shape[1:]), F32),
            pltpu.VMEM((3, *small.shape[1:]), F32),
            pltpu.VMEM((rows, cols), F32),
            pltpu.VMEM((rows, width), BF16),
            pltpu.VMEM((2 * count, width), BF16),
            pltpu.VMEM((rows, width), BF16),
            pltpu.VMEM((2 * count, width), BF16),
        ]
        + sems(RING_COPIES + 2 * 8 + 14),
        compiler_params=params(collective_id),
    )(*args)


def on_device(
    encoder_tokens,
    encoder_segments,
    decoder_tokens,
    decoder_segments,
    cotangent,
    attention_weight,
    feedforward_weight,
    norm_gain,
    norm_shift,
):
    section = lax.axis_index("section")
    mine = lambda a: lax.dynamic_index_in_dim(a, section, 0, keepdims=False)
    width, count = encoder_tokens.shape[2], decoder_tokens.shape[1]
    own_wt = jnp.swapaxes(attention_weight[0], 1, 2).reshape(6 * HEAD, width)
    own_gs = jnp.concatenate([norm_gain[0], norm_shift[0], jnp.zeros((2, width), F32)], 0)
    y = mine(decoder_tokens)
    e, c = mine(encoder_segments), mine(decoder_segments)
    position = jnp.arange(c.shape[0])
    allow_e = e[:, None] == e[None, :]
    allow_d = (c[:, None] == c[None, :]) & (position[:, None] >= position[None, :])
    flat = lambda a: a.reshape(-1, a.shape[-1])
    blocks = lambda a: a.reshape(SIDE, SIDE, -1, a.shape[-1])

    wt, gs, full_h0, h0, unit0, scale0, full_y, q, k, v, sq, sk, sv = first_call(
        mine(encoder_tokens), y, own_wt, own_gs, 1
    )
    q, k, v = flat(q), flat(k), flat(v)
    att_e, log_e = attend(q, k, v, allow_e)
    att_d, log_d = attend(sq, sk, sv, allow_d)
    (
        ffn, full_h1, full_m, full_d1, hidden, slope, kvc, cq, d1,
        unit1, scale1, unit2, scale2, dunit0, dscale0,
    ) = forward_call(blocks(att_e), att_d, h0, y, wt, gs, feedforward_weight[0], 2)
    (d3, dback1, full_d2, full_db2, full_db1, dhidden, dpre, att_c, cq_grad, kvc_grad, dsmall) = (
        decoder_call(
            cq, flat(kvc), d1, mine(cotangent), c[:, None], e[None, :], wt, ffn, gs, 3
        )
    )
    full_b2, full_b1, full_db0, pre, dqkv_grad, att_e_grad, back1, dec_grad, small_b = (
        backward_call(
            (
                blocks(kvc_grad), cq_grad, dback1, wt, gs, ffn, unit1, scale1, unit2, scale2,
                dunit0, dscale0, slope, sq, sk, sv, log_d, c[:, None], c[None, :],
            ),
            4,
        )
    )
    made = attend_back(q, k, v, log_e, allow_e, flat(att_e_grad))
    qkv_grad = jnp.concatenate(made, 1)

    att_grads = jnp.stack(
        [
            jnp.concatenate(
                [
                    t_dot(qkv_grad, flat(full_h0)),
                    t_dot(att_e, flat(full_b1)),
                    t_dot(kvc_grad, flat(full_m)),
                ],
                0,
            ),
            jnp.concatenate(
                [
                    t_dot(dqkv_grad, full_y),
                    t_dot(att_d, full_db0),
                    t_dot(cq_grad, full_d1),
                    t_dot(att_c, full_db1),
                ],
                0,
            ),
        ]
    ).astype(BF16)
    ffn_grads = jnp.stack(
        [
            jnp.concatenate(
                [t_dot(flat(full_h1), flat(pre)), t_dot(flat(full_b2), flat(hidden))], 0
            ),
            jnp.concatenate([t_dot(full_d2, dpre), t_dot(full_db2, dhidden)], 0),
        ]
    ).astype(BF16)
    none = jnp.zeros((1, width), F32)
    row = lambda a, i: a[i : i + 1]
    small = jnp.stack(
        [
            jnp.concatenate(
                [none, row(small_b, 0), row(small_b, 1), none, row(small_b, 2), row(small_b, 3)]
                + [none, none],
                0,
            ),
            jnp.concatenate(
                [row(small_b, 4), dsmall[0:2], row(small_b, 5), dsmall[2:4], none, none], 0
            ),
        ]
    )
    att_sum, ffn_sum, small_sum, enc_out, d3_out, dec_out = last_call(
        (
            blocks(qkv_grad), wt, gs, back1, unit0, scale0,
            att_grads, ffn_grads, small, d3, dec_grad,
        ),
        5,
    )
    att_sum = att_sum.reshape(6, HEAD, width).astype(F32)
    return (
        d3_out.astype(BF16),
        enc_out,
        dec_out,
        jnp.swapaxes(att_sum, 1, 2)[None],
        ffn_sum.reshape(feedforward_weight.shape).astype(F32),
        small_sum[None, :3],
        small_sum[None, 3:6],
    )


def solution(mesh):
    in_specs = (
        P("dp", "tensor", None),
        P("dp", None),
        P("dp", "tensor", None),
        P("dp", None),
        P("dp", "tensor", None),
        P("section", None, None, "tensor"),
        P("section", None, None, "tensor"),
        P("section", None, None),
        P("section", None, None),
    )
    out_specs = (
        P("dp", "tensor", "section"),
        P("dp", "tensor", "section"),
        P("dp", "tensor", "section"),
        P("section", None, None, "tensor"),
        P("section", None, None, "tensor"),
        P("section", None, None),
        P("section", None, None),
    )
    return jax.shard_map(
        on_device, mesh=mesh, in_specs=in_specs, out_specs=out_specs, check_vma=False
    )
```

time: 1460 us -> 376 us (0.26)
  waiting for transfers between devices: 893 us -> 0 us
  blocking collectives: 394 us -> 0 us
  Pallas kernels: 0 us -> 311 us
  other arithmetic: 50.2 us -> 13.2 us
  matrix products: 59.5 us -> 26.9 us
  between operations: 16.9 us -> 1.33 us
  starting transfers between devices: 14.8 us -> 0 us
    unnamed x20 -> x0, waiting for transfers between devices: 469 us -> none
    psum x1 -> x0, blocking collectives: 325 us -> none  [on_device(): small_sum = lax.psum(own_layer(small), ('dp', 'tensor'))]
    pallas_call x0 -> x5, Pallas kernels: none -> 311 us  [the longest x1 88.1 us: forward_call(): pl.pallas_call(forward_kernel, out_shape=[shape((2, *ffn.shape), BF16), s...]
    all_gather x5 -> x0, waiting for transfers between devices: 174 us -> none  [gather_rows(): return lax.all_gather(values.astype(BF16), 'tensor', axis=0, tiled=True)]
    reduce_scatter x2 -> x0, waiting for transfers between devices: 149 us -> none  [sum_rows(): lax.psum_scatter(values.astype(BF16), 'tensor', scatter_dimension=0, tile...]
    all_gather x3 -> x0, blocking collectives: 69.1 us -> none  [gather_rows(): return lax.all_gather(values.astype(BF16), 'tensor', axis=0, tiled=True)]
    ppermute x10 -> x0, waiting for transfers between devices: 59.9 us -> none  [swapped(): return lax.ppermute(value, axis, [(0, 1), (1, 0)])]
    psum x1 -> x0, waiting for transfers between devices: 40.1 us -> none  [on_device(): att_sum = lax.psum(own_layer(att_grads), 'dp').astype(F32)]
  transfers between devices with their start and end apart: 24 -> 0, of which waited for: 21 -> 0; matrix products, arithmetic and copies ran while one was open for 3% -> 0% of each run, Pallas kernels for 0% -> 0%
where the time goes in v3:
time: 376 us; the launch traced here: 370 us
  Pallas kernels  311 us (83%)
  matrix products  26.9 us (7%)
  local copies, waits for them, and re-layouts  17.6 us (5%)
  other arithmetic  13.2 us (4%)
    pallas_call x1, Pallas kernels, forward_call(): pl.pallas_call(forward_kernel, out_shape=[shape((2, *ffn.shape), BF16), s...  88.1 us
    pallas_call x1, Pallas kernels, backward_call(): pl.pallas_call(backward_kernel, out_shape=[shape((*grid, rows, width), BF...  85.7 us
    pallas_call x1, Pallas kernels, last_call(): pl.pallas_call(last_kernel, out_shape=[shape((*half(g), g.shape[2]), BF16...  60.4 us
    pallas_call x1, Pallas kernels, decoder_call(): pl.pallas_call(decoder_kernel, out_shape=[shape((rows, width), F32), shap...  46.7 us
    pallas_call x1, Pallas kernels, first_call(): pl.pallas_call(first_kernel, out_shape=[shape((2, *wt.shape), BF16), shap...  29.7 us
    dot_general x13, matrix products, t_dot(): lax.dot_general(a, b, (((0,), (0,)), ((), ())), preferred_element_type=F32)  18.3 us

profile of v3, /device:TPU:0, one launch (start us, length us, event | category | flops | bytes accessed | tf_op | source)
XLA Modules:
  0.0 369.6 jit_solution(8954782472294007533)
XLA Ops:
  0.7 0.7 fusion.61
  1.4 0.7 fusion.60
  2.1 1.2 constant_dynamic-slice_fusion.refs_18_
  3.3 1.3 fusion.20
  4.6 1.3 dynamic-slice_bitcast_fusion.1
  5.9 0.7 copy_bitcast_fusion
  6.7 0.6 pad_maximum_fusion.4.gs_in
  7.3 0.7 copy.18.seg_d.refs_17_
  8.0 0.7 dynamic-slice_bitcast_fusion.x
  8.7 29.7 %shard_map.144 = (bf16[2,384,1024]{2,1,0:T(8,128)(2,1)}, f32[2,8,1024]{2,1,0:T(8,128)}, bf16[4,4,80,1024]{3,2,1,0:T(8,128)(2,1)}, f32[80,1024]{1,0:T(8,128)}, f3...) custom-call(bf16[80,1024]{1,0:T(8,128)(2,1)} %dynamic-slice_bitcast_, ...), custom_call_target="tpu_custom_call" | custom-call | tf_op jit(solution)/shard_map/pallas_call | solution.py:449
  38.5 1.0 fusion.25
  39.5 1.6 convolution_convert_fusion.9.att_d
  41.0 0.7 copy.19.refs_16_
  41.8 2.7 fusion.24
  44.5 1.0 fusion.1
  45.5 1.8 copy-done.1
  47.2 1.3 fusion.12
  48.5 0.9 copy.16
  49.4 88.1 %shard_map.145 = (bf16[2,2,1024,256]{3,2,1,0:T(8,128)(2,1)}, bf16[4,4,80,1024]{3,2,1,0:T(8,128)(2,1)}, bf16[4,4,80,1024]{3,2,1,0:T(8,128)(2,1)}, bf16[128,1024]{...) custom-call(bf16[4,4,80,64]{3,2,1,0:T(8,128)(2,1)} %bitcast.108, ...), custom_call_target="tpu_custom_call" | custom-call | tf_op jit(solution)/shard_map/pallas_call | solution.py:545
  137.6 46.7 %shard_map.146 = (f32[8,1024]{1,0:T(8,128)}, f32[8,1024]{1,0:T(8,128)}, bf16[128,1024]{1,0:T(8,128)(2,1)}, bf16[128,1024]{1,0:T(8,128)(2,1)}, bf16[128,1024]{1,0...) custom-call(bf16[128,64]{1,0:T(8,128)(2,1)} %get-tuple-element.70.cq, ...), custom_call_target="tpu_custom_call" | custom-call | tf_op jit(solution)/shard_map/pallas_call | solution.py:633
  184.4 1.7 convolution_convert_fusion.7
  186.1 2.2 convolution_convert_fusion.4
  188.3 0.9 convolution_convert_fusion.6
  189.9 85.7 %shard_map.147 = (bf16[4,4,80,1024]{3,2,1,0:T(8,128)(2,1)}, bf16[4,4,80,1024]{3,2,1,0:T(8,128)(2,1)}, bf16[128,1024]{1,0:T(8,128)(2,1)}, bf16[4,4,80,256]{3,2,1,...) custom-call(bf16[4,4,80,128]{3,2,1,0:T(8,128)(2,1)} %bitcast.107, ...), custom_call_target="tpu_custom_call" | custom-call | tf_op jit(solution)/shard_map/pallas_call | solution.py:729
  275.7 3.2 fusion.14
  278.9 0.9 fusion.13
  279.9 1.5 pad_maximum_fusion.ffn
  281.4 0.9 copy-done.2
  282.3 1.2 convolution_convert_fusion.5
  283.7 0.6 pad_maximum_fusion.3.small
  284.8 1.2 maximum_bitcast_fusion.3
  286.0 4.2 %fusion.7 = bf16[1280,64]{0,1:T(8,128)(2,1)S(1)} fusion(bf16[1280,64]{1,0:T(8,128)(2,1)} %bitcast.109, f32[1280,1280]{0,1:T(8,128)} %copy-done.1, f32[1280]{0:T(1024)S(1)} %log_add_fusion), kind=kOutput, calls=%fused_computation.14 | convolution fusion | flops 213073920 | bytes 6886400 | tf_op jit(solution)/shard_map/dot_general | solution.py:56
  290.3 1.3 multiply_reduce_fusion
  291.7 1.3 multiply_convert_fusion
  292.9 2.2 fusion.11
  295.1 0.7 fusion.10
  295.9 1.0 copy-done.26
  296.9 0.7 convolution_convert_fusion.3
  297.9 1.3 pad_maximum_fusion.1.att
  299.2 1.1 copy.21
  300.2 60.4 %shard_map.148 = (bf16[2,192,1024]{2,1,0:T(8,128)(2,1)}, bf16[2,1024,256]{2,1,0:T(8,128)(2,1)}, f32[8,1024]{1,0:T(8,128)}, f32[2,80,512]{2,1,0:T(8,128)}, f32[2,8,512]{2,1,0:T(8,128)}, /*index=5*/f32[2,8,512]{2,1,0:T(8,128)}) custom-call(bf16[4,4,80,192]{3,2,1,0:T(8,128)(2,1)} %bitcast.104, bf16[2,384,1024]{2,1,0:T(8,128)(2,1)} %get-tuple-element.68.wt.refs_3_, ...), custom_call_target="tpu_custom_call" | custom-call | tf_op jit(solution)/shard_map/pallas_call | solution.py:895
  360.6 1.5 convert_element_type.51
  362.1 0.8 slice_bitcast_fusion
  362.9 0.6 copy.23
  364.2 2.5 convert_bitcast_fusion
  366.7 1.5 bitcast_convert_fusion
  368.1 0.7 copy.33
  368.9 0.6 copy.34
  (81 shorter events, 2.5 us)
Async XLA Ops:
  0.6 7.4 %copy-start = (bf16[2,80,1024]{2,1,0:T(8,128)(2,1)S(1)}, bf16[2,80,1024]{2,1,0:T(8,128)(2,1)}, u32[]{:S(2)}) copy-start(bf16[2,80,1024]{2,1,0:T(8,128)(2,1)} %param.9) | copy-start | bytes 983044
  44.5 2.8 copy-start.1
  44.5 2.8 copy-start.10
  137.6 46.8 %copy-start.15 = (bf16[128,1024]{1,0:T(8,128)(2,1)S(1)}, bf16[128,1024]{1,0:T(8,128)(2,1)}, u32[]{:S(2)}) copy-start(bf16[128,1024]{1,0:T(8,128)(2,1)} %get-tuple-element.94) | copy-start | bytes 786436
  137.6 48.5 %copy-start.3 = (bf16[4,4,80,1024]{3,2,1,0:T(8,128)(2,1)S(1)}, bf16[4,4,80,1024]{3,2,1,0:T(8,128)(2,1)}, u32[]{:S(2)}) copy-start(bf16[4,4,80,1024]{3,2,1,0:T(8,128)(2,1)} %get-tuple-element.90) | copy-start | bytes 7864324
  184.3 4.0 %copy-start.25 = (f32[8,1024]{1,0:T(8,128)S(1)}, f32[8,1024]{1,0:T(8,128)}, u32[]{:S(2)}) copy-start(f32[8,1024]{1,0:T(8,128)} %get-tuple-element.106) | copy-start | bytes 98308
  184.3 4.0 %copy-start.16 = (bf16[128,1024]{1,0:T(8,128)(2,1)S(1)}, bf16[128,1024]{1,0:T(8,128)(2,1)}, u32[]{:S(2)}) copy-start(bf16[128,1024]{1,0:T(8,128)(2,1)} %get-tuple-element.96) | copy-start | bytes 786436
  184.3 4.0 %copy-start.23 = (bf16[128,64]{1,0:T(8,128)(2,1)S(1)}, bf16[128,64]{1,0:T(8,128)(2,1)}, u32[]{:S(2)}) copy-start(bf16[128,64]{1,0:T(8,128)(2,1)} %get-tuple-element.95) | copy-start | bytes 49156
  184.3 4.9 %copy-start.13 = (bf16[128,1024]{1,0:T(8,128)(2,1)S(1)}, bf16[128,1024]{1,0:T(8,128)(2,1)}, u32[]{:S(2)}) copy-start(bf16[128,1024]{1,0:T(8,128)(2,1)} %get-tuple-element.101) | copy-start | bytes 786436
  184.3 4.9 %copy-start.21 = (bf16[128,256]{1,0:T(8,128)(2,1)S(1)}, bf16[128,256]{1,0:T(8,128)(2,1)}, u32[]{:S(2)}) copy-start(bf16[128,256]{1,0:T(8,128)(2,1)} %get-tuple-element.102) | copy-start | bytes 196612
  184.3 5.2 %copy-start.12 = (bf16[128,1024]{1,0:T(8,128)(2,1)S(1)}, bf16[128,1024]{1,0:T(8,128)(2,1)}, u32[]{:S(2)}) copy-start(bf16[128,1024]{1,0:T(8,128)(2,1)} %get-tuple-element.103) | copy-start | bytes 786436
  184.3 5.2 %copy-start.20 = (bf16[128,256]{1,0:T(8,128)(2,1)S(1)}, bf16[128,256]{1,0:T(8,128)(2,1)}, u32[]{:S(2)}) copy-start(bf16[128,256]{1,0:T(8,128)(2,1)} %get-tuple-element.104) | copy-start | bytes 196612
  189.9 85.7 %copy-start.28 = (bf16[4,4,80,256]{3,2,1,0:T(8,128)(2,1)S(1)}, bf16[4,4,80,256]{3,2,1,0:T(8,128)(2,1)}, u32[]{:S(2)}) copy-start(bf16[4,4,80,256]{3,2,1,0:T(8,128)(2,1)} %get-tuple-element.100) | copy-start | bytes 1966084
  275.7 3.2 copy-start.27
  275.7 3.2 copy-start.29
  279.8 2.5 copy-start.2
  279.9 3.6 copy-start.24
  279.9 10.3 %slice-start = ((s8[6553600]{0:T(1024)(128)(4,1)}), s8[2359296]{0:T(1024)(128)(4,1)S(1)}, s32[]{:S(2)}) async-start(s8[6553600]{0:T(1024)(128)(4,1)} %bitcast.102), calls=%async_computation | async-start | bytes 4718592
  281.4 2.9 copy-start.14
  281.4 2.9 copy-start.18
  281.4 3.1 copy-start.17
  281.4 3.1 copy-start.19
  284.8 5.5 %slice-start.1 = ((s8[6553600]{0:T(1024)(128)(4,1)}), s8[4194304]{0:T(1024)(128)(4,1)S(1)}, s32[]{:S(2)}) async-start(s8[6553600]{0:T(1024)(128)(4,1)} %bitcast.102), calls=%async_computation.1 | async-start | bytes 8388608
  286.0 4.3 %copy-start.4 = (bf16[4,4,80,64]{3,2,1,0:T(8,128)(2,1)S(1)}, bf16[4,4,80,64]{3,2,1,0:T(8,128)(2,1)}, u32[]{:S(2)}) copy-start(bf16[4,4,80,64]{3,2,1,0:T(8,128)(2,1)} %get-tuple-element.84) | copy-start | bytes 491524
  286.0 4.3 %copy-start.11 = (bf16[4,4,80,64]{3,2,1,0:T(8,128)(2,1)S(1)}, bf16[4,4,80,64]{3,2,1,0:T(8,128)(2,1)}, u32[]{:S(2)}) copy-start(bf16[4,4,80,64]{3,2,1,0:T(8,128)(2,1)} %get-tuple-element.63) | copy-start | bytes 491524
  292.9 2.2 copy-start.8
  295.1 1.7 copy-start.26
  296.9 0.9 copy-start.6
  296.9 1.0 copy-start.7
  360.6 6.0 %copy-start.5 = (bf16[2,1024,256]{2,1,0:T(8,128)(2,1)S(1)}, bf16[2,1024,256]{2,1,0:T(8,128)(2,1)}, u32[]{:S(2)}) copy-start(bf16[2,1024,256]{2,1,0:T(8,128)(2,1)} %get-tuple-element.113) | copy-start | bytes 3145732
  364.2 4.0 %copy-start.9 = (f32[2,80,512]{2,1,0:T(8,128)S(1)}, f32[2,80,512]{2,1,0:T(8,128)}, u32[]{:S(2)}) copy-start(f32[2,80,512]{2,1,0:T(8,128)} %get-tuple-element.150) | copy-start | bytes 983044
  364.2 4.7 %copy-start.22 = (f32[2,8,512]{2,1,0:T(8,128)S(1)}, f32[2,8,512]{2,1,0:T(8,128)}, u32[]{:S(2)}) copy-start(f32[2,8,512]{2,1,0:T(8,128)} %get-tuple-element.151) | copy-start | bytes 98308

commit v4 on v3

--- a/solution.py
+++ b/solution.py
@@ -18,6 +18,10 @@
 UP = (0, 2)
 DOWN = (1, 3)
 RING_COPIES = 32
+CHUNKS = ((0, 48), (48, 32))
+PAUSES = (1, 1, 1, 1, 1)
+LAG = 0
+RING = True
 INV_SQRT2 = 0.7071067811865476
 INV_SQRT_2PI = 0.3989422804014327
 FAR_FIRST = (10, 2, 8, 6, 14, 11, 9, 7, 13, 5, 15, 1, 3, 4, 12)
@@ -99,7 +103,7 @@
 
 
 def neighbours(place):
-    return [device_at(moved(place, *along(axis, s))) for axis in range(2) for s in (1, -1)]
+    return [device_at(moved(place, *along(axis, s))) for axis in range(2) for s in (1, 2, 3)]
 
 
 def greet(devices):
@@ -116,8 +120,8 @@
 
 
 class Links:
-    def __init__(self, send_sems, recv_sems):
-        self.send, self.recv, self.used, self.started = send_sems, recv_sems, 0, []
+    def __init__(self, send_sems, recv_sems, used=0):
+        self.send, self.recv, self.used, self.started = send_sems, recv_sems, used, []
 
     def start(self, source, target, device):
         n = self.used
@@ -179,69 +183,74 @@
     return both.astype(BF16).reshape(SIDE, SIDE, 2 * count, half)
 
 
-def gather(links, place, bufs, ready=None):
+def gather(links, place, views, ready=None):
     jobs = []
-    for buf in bufs:
+    for buf, low, rows in views:
         half = buf.shape[-1] // 2
         for h in range(2):
-            jobs.append((buf, 1 - h, h, h * half, half))
+            jobs.append((buf, 1 - h, h, h * half, half, pl.ds(low, rows)))
     ready = ready or (lambda group: None)
 
-    def send(job, axis, steps, r, s, part=None):
-        buf, a, b, start, size = job
+    def send(job, axis, steps, r, s):
+        buf, a, b, start, size, rows = job
         y, x = moved(moved(place, *along(a, r)), *along(b, s))
-        if part is not None:
-            size = size // 2
-            start = start + part * size
-        ref = buf.at[y, x, :, pl.ds(start, size)]
+        ref = buf.at[y, x, rows, pl.ds(start, size)]
         return links.start(ref, ref, device_at(moved(place, *along(axis, steps))))
 
-    first, spread, second, ahead = [], [], [], []
+    first, spread, ahead = [], [], []
     for job in jobs:
-        first.append([send(job, job[1], 1, 0, 0), send(job, job[1], -1, 0, 0)])
+        first.append({-d % SIDE: send(job, job[1], d, 0, 0) for d in (2, 1, 3)})
+    paths = ((1, 3), (3, 1)) if RING else ((2, 2), (1, 3), (3, 1))
     for job in jobs:
-        spread.append({0: [send(job, job[2], 1, 0, 0), send(job, job[2], -1, 0, 0)]})
+        spread.append({0: {s: send(job, job[2], d, 0, 0) for d, s in paths}})
     ready([(0, 0)])
-    for i, job in enumerate(jobs):
-        a, b = job[1], job[2]
-        first[i][0].wait_recv()
-        one = send(job, a, 1, -1, 0, 0)
-        spread[i][3] = [send(job, b, 1, -1, 0), send(job, b, -1, -1, 0)]
-        first[i][1].wait_recv()
-        two = send(job, a, -1, 1, 0, 1)
-        spread[i][1] = [send(job, b, 1, 1, 0), send(job, b, -1, 1, 0)]
-        second.append([one, two])
-    for i, job in enumerate(jobs):
-        spread[i][0][0].wait_recv()
-        ahead.append([send(job, job[2], 1, 0, -1)])
-    for i, job in enumerate(jobs):
-        spread[i][0][1].wait_recv()
+    yield
+    for r in (3, 1, 2):
+        for i, job in enumerate(jobs):
+            first[i][r].wait_recv()
+            spread[i][r] = {s: send(job, job[2], d, r, 0) for d, s in paths}
+    if RING:
+        for i, job in enumerate(jobs):
+            spread[i][0][3].wait_recv()
+            ahead.append({0: send(job, job[2], 1, 0, 3)})
+            spread[i][0][1].wait_recv()
+    else:
+        for i, job in enumerate(jobs):
+            spread[i][0][3].wait_recv()
+            spread[i][0][1].wait_recv()
+            ahead.append({r: spread[i][r][2] for r in range(SIDE)})
     ready([(0, 1), (0, 3), (1, 0), (3, 0)])
-    for i, job in enumerate(jobs):
-        second[i][0].wait_recv()
-        second[i][1].wait_recv()
-        spread[i][2] = [send(job, job[2], 1, 2, 0), send(job, job[2], -1, 2, 0)]
-    for i, job in enumerate(jobs):
+    yield
+    if RING:
         for r in DOWN:
-            spread[i][r][1].wait_recv()
-            ahead[i].append(send(job, job[2], -1, r, 1))
-    for i, job in enumerate(jobs):
-        spread[i][2][0].wait_recv()
-        ahead[i].append(send(job, job[2], 1, 2, -1))
-    for i, job in enumerate(jobs):
+            for i, job in enumerate(jobs):
+                spread[i][r][1].wait_recv()
+                ahead[i][r] = send(job, job[2], -1, r, 1)
+        for i, job in enumerate(jobs):
+            spread[i][2][3].wait_recv()
+            ahead[i][2] = send(job, job[2], 1, 2, 3)
         for r in DOWN:
-            spread[i][r][0].wait_recv()
+            for i, job in enumerate(jobs):
+                spread[i][r][3].wait_recv()
+    else:
+        for r in DOWN:
+            for i, job in enumerate(jobs):
+                spread[i][r][1].wait_recv()
+                spread[i][r][3].wait_recv()
     ready([(1, 1), (1, 3), (3, 1), (3, 3)])
     for i, job in enumerate(jobs):
         ahead[i][0].wait_recv()
     ready([(0, 2), (2, 0)])
+    yield
     for i, job in enumerate(jobs):
+        if not RING:
+            spread[i][2][3].wait_recv()
         spread[i][2][1].wait_recv()
         ahead[i][1].wait_recv()
-        ahead[i][2].wait_recv()
+        ahead[i][3].wait_recv()
     ready([(1, 2), (3, 2), (2, 1), (2, 3)])
     for i, job in enumerate(jobs):
-        ahead[i][3].wait_recv()
+        ahead[i][2].wait_recv()
     ready([(2, 2)])
 
 
@@ -251,28 +260,21 @@
 )
 
 
-def sum_blocks(links, place, parts, produce=None):
+def sum_blocks(links, place, views, produce=None):
     produce = produce or (lambda group: None)
     jobs = []
-    for part, land in parts:
+    for part, land, low, rows in views:
         half = part.shape[-1] // 2
         for h in range(2):
-            jobs.append((part, land, 15 * h, 1 - h, h, h * half, half))
-
-    def block(job, r, s, quarter=None):
-        part, _, _, a, b, start, size = job
+            jobs.append((part, land, 15 * h, 1 - h, h, h * half, half, pl.ds(low, rows)))
+
+    def block(job, r, s):
+        part, _, _, a, b, start, size, rows = job
         y, x = moved(moved(place, *along(a, r)), *along(b, s))
-        if quarter is not None:
-            size = size // 2
-            start = start + quarter * size
-        return part.at[y, x, :, pl.ds(start, size)]
-
-    def landing(job, n, quarter=None):
-        ref = job[1].at[job[2] + n]
-        if quarter is None:
-            return ref
-        size = job[6] // 2
-        return ref.at[:, pl.ds(quarter * size, size)]
+        return part.at[y, x, rows, pl.ds(start, size)]
+
+    def landing(job, n):
+        return job[1].at[job[2] + n, job[7]]
 
     def start(source, target, axis, steps):
         return links.start(source, target, device_at(moved(place, *along(axis, steps))))
@@ -288,67 +290,142 @@
 
     order = (2, 3, 1, 0)
     produce(PRODUCE[0])
-    far = []
-    for job in jobs:
-        far.append(
-            {r: start(block(job, r, 2), landing(job, r), job[4], 1 if r in UP else -1) for r in order}
-        )
-    produce(PRODUCE[1])
-    near = []
-    for job in jobs:
-        sent = {}
+    near = [{r: [] for r in order} for _ in jobs]
+    if RING:
+        far = []
+        for job in jobs:
+            far.append(
+                {
+                    r: start(block(job, r, 2), landing(job, r), job[4], 1 if r in UP else -1)
+                    for r in order
+                }
+            )
+        produce(PRODUCE[1])
+        for i, job in enumerate(jobs):
+            for r in order:
+                steps = -1 if r in UP else 1
+                near[i][r].append(
+                    start(block(job, r, steps), near_slot(job, r, steps), job[4], steps)
+                )
+        yield
         for r in order:
-            steps = -1 if r in UP else 1
-            sent[r] = [start(block(job, r, steps), near_slot(job, r, steps), job[4], steps)]
-        near.append(sent)
+            for i, job in enumerate(jobs):
+                steps = 1 if r in UP else -1
+                far[i][r].wait_recv()
+                ref = block(job, r, steps)
+                ref[...] = add(ref, landing(job, r)).astype(BF16)
+                near[i][r].append(start(ref, near_slot(job, r, steps), job[4], steps))
+    else:
+        for s in (2, 1, 3):
+            for r in order:
+                for i, job in enumerate(jobs):
+                    slot = landing(job, 4 * (s - 1) + r)
+                    near[i][r].append(start(block(job, r, s), slot, job[4], s))
+            if s == 2:
+                produce(PRODUCE[1])
+    yield
+    last = [{} for _ in jobs]
+    results = []
     for r in order:
-        for i, job in enumerate(jobs):
-            steps = 1 if r in UP else -1
-            far[i][r].wait_recv()
-            ref = block(job, r, steps)
-            ref[...] = add(ref, landing(job, r)).astype(BF16)
-            near[i][r].append(start(ref, near_slot(job, r, steps), job[4], steps))
-    opposite, last = [], []
-    for r in order[:3]:
+        if r == 0:
+            yield
         for i, job in enumerate(jobs):
             for copy in near[i][r]:
                 copy.wait_recv()
             ref = block(job, r, 0)
-            total = add(ref, landing(job, 4 + 2 * r), landing(job, 5 + 2 * r))
-            if r == 2:
+            if RING:
+                total = add(ref, landing(job, 4 + 2 * r), landing(job, 5 + 2 * r))
+            else:
+                total = add(ref, landing(job, r), landing(job, 4 + r), landing(job, 8 + r))
+            if r == 0:
+                results.append(total)
+            else:
                 ref[...] = total.astype(BF16)
-                opposite.append(
-                    [
-                        start(block(job, 2, 0, 0), landing(job, 12, 0), job[3], 1),
-                        start(block(job, 2, 0, 1), landing(job, 12, 1), job[3], -1),
-                    ]
-                )
-                last.append({})
-            else:
-                quarter = 0 if r == 1 else 1
-                opposite[i][quarter].wait_recv()
-                size = job[6] // 2
-                extra = landing(job, 12, quarter)[...].astype(F32)
-                low, high = total[:, :size], total[:, size:]
-                if quarter == 0:
-                    low = low + extra
-                else:
-                    high = high + extra
-                ref[:, pl.ds(0, size)] = low.astype(BF16)
-                ref[:, pl.ds(size, size)] = high.astype(BF16)
-                last[i][r] = start(
-                    ref, landing(job, 13 if r == 1 else 14), job[3], 1 if r == 1 else -1
-                )
-    results = []
+                last[i][r] = start(ref, landing(job, 11 + r), job[3], r)
     for i, job in enumerate(jobs):
-        for copy in near[i][0]:
-            copy.wait_recv()
-        last[i][1].wait_recv()
-        last[i][3].wait_recv()
-        results.append(
-            add(block(job, 0, 0), landing(job, 4), landing(job, 5), landing(job, 13), landing(job, 14))
-        )
+        for r in order[:3]:
+            last[i][r].wait_recv()
+            results[i] = results[i] + landing(job, 11 + r)[...].astype(F32)
     return [jnp.concatenate(results[i : i + 2], 1) for i in range(0, len(results), 2)]
+
+
+def run(chains, lag=0):
+    turn, active = 0, list(enumerate(chains))
+    while active:
+        for n, chain in list(active):
+            if turn >= n * lag:
+                try:
+                    next(chain)
+                except StopIteration:
+                    active.remove((n, chain))
+        turn += 1
+
+
+def pack_places():
+    section, zh, core, partner, sibling = sections()
+    zh_plus = lax.rem(zh + section, 2)
+    plus = {"section": 1 - section, "dp": zh_plus * 2 + core}
+    minus = {"section": 1 - section, "dp": (1 - zh_plus) * 2 + core}
+    return section, zh, core, sibling, zh_plus, plus, minus
+
+
+PACK_COPIES = 8
+
+
+def pack_scratch(rows, cols):
+    half, quarter = rows // 2, rows // 4
+    return [
+        pltpu.VMEM((2, half, cols), BF16),
+        pltpu.VMEM((2, half, cols), BF16),
+        pltpu.VMEM((2, quarter, cols), BF16),
+        pltpu.VMEM((2, quarter, cols), BF16),
+        pltpu.VMEM((half, cols), BF16),
+    ]
+
+
+def pause(n):
+    for _ in range(n):
+        yield
+
+
+def pack_sum(links, grad, out, scratch):
+    work, core_land, side, passing, over = scratch
+    section, zh, core, sibling, zh_plus, plus, minus = pack_places()
+    other = 1 - section
+    half = grad.shape[1] // 2
+    quarter = half // 2
+    first = links.start(grad.at[:, pl.ds((1 - core) * half, half)], core_land, sibling)
+    yield from pause(PAUSES[0])
+    first.wait_recv()
+    work[...] = (
+        grad[:, pl.ds(core * half, half)].astype(F32) + core_land[...].astype(F32)
+    ).astype(BF16)
+    second = [
+        links.start(work.at[other, pl.ds(h * quarter, quarter)], side.at[n], d)
+        for n, (h, d) in enumerate(((zh_plus, plus), (1 - zh_plus, minus)))
+    ]
+    yield from pause(PAUSES[1])
+    for copy in second:
+        copy.wait_recv()
+    mine = work.at[section, pl.ds(zh * quarter, quarter)]
+    mine[...] = (mine[...].astype(F32) + side[0].astype(F32) + side[1].astype(F32)).astype(BF16)
+    third = [
+        links.start(work.at[section, pl.ds(n * quarter, quarter)], passing.at[n], d)
+        for n, d in enumerate((plus, minus))
+    ]
+    yield from pause(PAUSES[2])
+    fourth = []
+    for n, device in enumerate((plus, minus)):
+        third[n].wait_recv()
+        fourth.append(links.start(passing.at[n], over.at[pl.ds(n * quarter, quarter)], device))
+    yield from pause(PAUSES[3])
+    for copy in fourth:
+        copy.wait_recv()
+    out[core] = (work[section].astype(F32) + over[...].astype(F32)).astype(BF16)
+    last = links.start(out.at[core], out.at[core], sibling)
+    yield from pause(PAUSES[4])
+    last.wait_recv()
+    links.finish()
 
 
 def gather_small(links, place, buf, rows):
@@ -375,19 +452,20 @@
     return unfold(total + jnp.sum(land[...].astype(F32), 0))
 
 
-def stacked(ref, place, group):
+def stacked(ref, place, group, low=0, rows=None):
+    rows = ref.shape[2] if rows is None else rows
     blocks = []
     for dy, dx in group:
         y, x = moved(place, dy, dx)
-        blocks.append(ref[y, x])
+        blocks.append(ref[y, x, low : low + rows])
     return blocks[0] if len(blocks) == 1 else jnp.concatenate(blocks, 0)
 
 
-def store_blocks(ref, place, group, rows):
-    count = ref.shape[2]
+def store_blocks(ref, place, group, values, low=0):
+    rows = values.shape[0] // len(group)
     for n, (dy, dx) in enumerate(group):
         y, x = moved(place, dy, dx)
-        ref[y, x] = rows[n * count : (n + 1) * count]
+        ref[y, x, low : low + rows] = values[n * rows : (n + 1) * rows]
 
 
 def wide(scale):
@@ -427,7 +505,8 @@
             scale0[...] = wide(scale)
         store_blocks(full_h0, place, group, rows.astype(BF16))
 
-    gather(links, place, [xbuf, ybuf], ready)
+    views = [(xbuf, 0, x.shape[0]), (ybuf, 0, ybuf.shape[2])]
+    run([gather(links, place, views, ready)])
     passed[1].wait_recv()
     count, width = x.shape
     for i in range(SIDE):
@@ -477,65 +556,84 @@
     place = at_grid()
     section, _, core, partner, sibling = sections()
     greet(neighbours(place) + [partner, sibling])
-    links = Links(send, recv)
-    passed = [links.start(ffn_in.at[core], ffn.at[section, core], partner)]
-
-    def attended(group):
-        rows = dot(stacked(att_e, place, group), wt[0, 3 * HEAD : 4 * HEAD, :])
-        store_blocks(part, place, group, rows.astype(BF16))
-        if group == PRODUCE[0]:
-            dpart[...] = fold_all(dot(att_d[...], wt[1, 3 * HEAD : 4 * HEAD, :]))
-        else:
-            ffn[section] = ffn_in[...]
-
-    sum_e, sum_d = sum_blocks(links, place, [(part, land_1), (dpart, land_d)], attended)
-    passed[0].wait_recv()
-    theirs = ffn.at[1 - section, core]
-    passed.append(links.start(theirs, theirs, sibling))
-    unit, scale = norm_parts(h0[...] + sum_e)
-    unit1[...] = unit
-    scale1[...] = wide(scale)
-    h1 = unit * gs[0, 1:2, :] + gs[0, 4:5, :]
-    full_h1[place[0], place[1]] = h1.astype(BF16)
-    unit, scale = norm_parts(y[...].astype(F32) + unfold(sum_d))
-    dunit0[...] = unit
-    dscale0[...] = wide(scale)
-    rows = unit * gs[1, 0:1, :] + gs[1, 3:4, :]
-    d1[...] = rows
-    d1buf[place[0], place[1]] = fold(rows).astype(BF16)
-
-    def up(group):
-        if group == [(0, 0)]:
-            return
-        if group == [(0, 1), (0, 3), (1, 0), (3, 0)]:
-            passed[1].wait_recv()
-            group = [(0, 0)] + group
-        made, back = gelu_parts(dot(stacked(full_h1, place, group), ffn[0, 0]))
-        store_blocks(hidden, place, group, made.astype(BF16))
-        store_blocks(slope, place, group, back)
-
-    gather(links, place, [full_h1, d1buf], up)
-    links.finish()
-    rows = unfold_all(d1buf[...])
-    full_d1[...] = rows
-    cq[...] = dot_t(rows, wt[1, 4 * HEAD : 5 * HEAD, :]).astype(BF16)
-
-    def down(group):
-        rows = dot_t(stacked(hidden, place, group), ffn[0, 1])
-        store_blocks(part, place, group, rows.astype(BF16))
-
-    (sum_e,) = sum_blocks(links, place, [(part, land_2)], down)
-    unit, scale = norm_parts(h1 + sum_e)
-    unit2[...] = unit
-    scale2[...] = wide(scale)
-    full_m[place[0], place[1]] = (unit * gs[0, 2:3, :] + gs[0, 5:6, :]).astype(BF16)
-
-    def cross(group):
-        rows = dot_t(stacked(full_m, place, group), wt[0, 4 * HEAD : 6 * HEAD, :])
-        store_blocks(kvc, place, group, rows.astype(BF16))
-
-    gather(links, place, [full_m], cross)
-    links.finish()
+    shared = Links(send, recv)
+    passed = [shared.start(ffn_in.at[core], ffn.at[section, core], partner)]
+
+    def chain(links, low, rows, with_dec):
+        here = pl.ds(low, rows)
+
+        def attended(group):
+            made = dot(stacked(att_e, place, group, low, rows), wt[0, 3 * HEAD : 4 * HEAD, :])
+            store_blocks(part, place, group, made.astype(BF16), low)
+            if with_dec and group == PRODUCE[0]:
+                dpart[...] = fold_all(dot(att_d[...], wt[1, 3 * HEAD : 4 * HEAD, :]))
+            if low == 0 and group == PRODUCE[1]:
+                ffn[section] = ffn_in[...]
+
+        views = [(part, land_1, low, rows)]
+        if with_dec:
+            views.append((dpart, land_d, 0, dpart.shape[2]))
+        sums = yield from sum_blocks(links, place, views, attended)
+        unit, scale = norm_parts(h0[here] + sums[0])
+        unit1[here] = unit
+        scale1[here] = wide(scale)
+        h1 = unit * gs[0, 1:2, :] + gs[0, 4:5, :]
+        full_h1[place[0], place[1], here] = h1.astype(BF16)
+        views = [(full_h1, low, rows)]
+        if with_dec:
+            unit, scale = norm_parts(y[...].astype(F32) + unfold(sums[1]))
+            dunit0[...] = unit
+            dscale0[...] = wide(scale)
+            made = unit * gs[1, 0:1, :] + gs[1, 3:4, :]
+            d1[...] = made
+            d1buf[place[0], place[1]] = fold(made).astype(BF16)
+            views.append((d1buf, 0, d1buf.shape[2]))
+        if low == 0:
+            passed[0].wait_recv()
+            theirs = ffn.at[1 - section, core]
+            passed.append(shared.start(theirs, theirs, sibling))
+
+        def up(group):
+            if group == [(0, 0)]:
+                return
+            if group == [(0, 1), (0, 3), (1, 0), (3, 0)]:
+                if low == 0:
+                    passed[1].wait_recv()
+                group = [(0, 0)] + group
+            made, back = gelu_parts(dot(stacked(full_h1, place, group, low, rows), ffn[0, 0]))
+            store_blocks(hidden, place, group, made.astype(BF16), low)
+            store_blocks(slope, place, group, back, low)
+
+        yield from gather(links, place, views, up)
+        links.finish()
+        if with_dec:
+            made = unfold_all(d1buf[...])
+            full_d1[...] = made
+            cq[...] = dot_t(made, wt[1, 4 * HEAD : 5 * HEAD, :]).astype(BF16)
+
+        def down(group):
+            made = dot_t(stacked(hidden, place, group, low, rows), ffn[0, 1])
+            store_blocks(part, place, group, made.astype(BF16), low)
+
+        sums = yield from sum_blocks(links, place, [(part, land_2, low, rows)], down)
+        unit, scale = norm_parts(h1 + sums[0])
+        unit2[here] = unit
+        scale2[here] = wide(scale)
+        full_m[place[0], place[1], here] = (unit * gs[0, 2:3, :] + gs[0, 5:6, :]).astype(BF16)
+
+        def cross(group):
+            made = dot_t(stacked(full_m, place, group, low, rows), wt[0, 4 * HEAD : 6 * HEAD, :])
+            store_blocks(kvc, place, group, made.astype(BF16), low)
+
+        yield from gather(links, place, [(full_m, low, rows)], cross)
+        links.finish()
+
+    chains = []
+    for n, (low, rows) in enumerate(CHUNKS):
+        links = Links(send, recv, 2 + 6 * RING_COPIES * n)
+        chains.append(chain(links, low, rows, n == len(CHUNKS) - 1))
+    run(chains, LAG)
+    shared.finish()
 
 
 def forward_call(att_e, att_d, h0, y, wt, gs, ffn, collective_id):
@@ -571,7 +669,7 @@
             pltpu.VMEM((30, 2 * count, width // 4), BF16),
             pltpu.VMEM((*grid, 2 * count, width // 2), BF16),
         ]
-        + sems(6 * RING_COPIES + 2),
+        + sems(6 * RING_COPIES * len(CHUNKS) + 2),
         compiler_params=params(collective_id),
     )(att_e, att_d, h0, y, wt, gs, ffn)
 
@@ -661,63 +759,104 @@
 def backward_kernel(*refs):
     (kvc_grad, cq_grad, dback1, wt, gs, ffn, unit1, scale1, unit2, scale2) = refs[:10]
     (dunit0, dscale0, slope, sq, sk, sv, log_d, seg_d, seg_dt) = refs[10:19]
-    (full_b2, full_b1, full_db0, pre, dqkv_grad, att_grad, back1, dec_grad, grads) = refs[19:28]
-    (part, dpart_1, dpart_2, land_1, land_2, dland_1, dland_2, dbuf, send, recv) = refs[28:]
+    (full_h1, hidden, dec_ffn) = refs[19:22]
+    (full_b1, full_db0, dqkv_grad, att_grad, back1, dec_grad, grads, ffn_sum) = refs[22:30]
+    (full_b2, pre, part, dpart_1, dpart_2, land_1, land_2, dland_1, dland_2, dbuf) = refs[30:40]
+    (ffn_grad, *pack_refs, send, recv) = refs[40:]
     place = at_grid()
-    greet(neighbours(place))
-    links = Links(send, recv)
-
-    def cross(group):
-        rows = dot(stacked(kvc_grad, place, group), wt[0, 4 * HEAD : 6 * HEAD, :])
-        store_blocks(part, place, group, rows.astype(BF16))
-
-    dpart_1[...] = fold_all(dot(cq_grad[...], wt[1, 4 * HEAD : 5 * HEAD, :]))
-    sum_e, sum_d = sum_blocks(links, place, [(part, land_1), (dpart_1, dland_1)], cross)
-    back2, gain2, shift2 = norm_back(sum_e, unit2[...], scale2[:, 0:1], gs[0, 2:3, :])
-    full_b2[place[0], place[1]] = back2.astype(BF16)
-    dback0, dgain0, dshift0 = norm_back(
-        dback1[...] + unfold(sum_d), dunit0[...], dscale0[:, 0:1], gs[1, 0:1, :]
-    )
-    dbuf[place[0], place[1]] = fold(dback0).astype(BF16)
-
-    def down(group):
-        rows = dot(stacked(full_b2, place, group), ffn[0, 1]) * stacked(slope, place, group)
-        store_blocks(pre, place, group, rows.astype(BF16))
-
-    gather(links, place, [full_b2, dbuf], down)
-    links.finish()
-    rows = unfold_all(dbuf[...])
-    full_db0[...] = rows
-    count = rows.shape[0]
-    att_d_grad = dot_t(rows, wt[1, 3 * HEAD : 4 * HEAD, :]).astype(BF16)
-    before = lax.broadcasted_iota(jnp.int32, (count, count), 1) <= lax.broadcasted_iota(
-        jnp.int32, (count, count), 0
-    )
-    allowed = (seg_d[...] == seg_dt[...]) & before
-    made = attend_back(sq[...], sk[...], sv[...], log_d[...], allowed, att_d_grad)
-    made = jnp.concatenate([m.astype(F32) for m in made], 1).astype(BF16)
-    dqkv_grad[...] = made
-    dpart_2[...] = fold_all(dot(made, wt[1, 0 : 3 * HEAD, :]))
-
-    def up(group):
-        rows = dot_t(stacked(pre, place, group), ffn[0, 0])
-        store_blocks(part, place, group, rows.astype(BF16))
-
-    sum_e, sum_d = sum_blocks(links, place, [(part, land_2), (dpart_2, dland_2)], up)
-    dec_grad[...] = dback0 + unfold(sum_d)
-    rows, gain1, shift1 = norm_back(back2 + sum_e, unit1[...], scale1[:, 0:1], gs[0, 1:2, :])
-    back1[...] = rows
-    full_b1[place[0], place[1]] = rows.astype(BF16)
-
-    def mixed(group):
-        rows = dot_t(stacked(full_b1, place, group), wt[0, 3 * HEAD : 4 * HEAD, :])
-        store_blocks(att_grad, place, group, rows.astype(BF16))
-
-    gather(links, place, [full_b1], mixed)
-    for i, row in enumerate((gain1, gain2, shift1, shift2, dgain0, dshift0)):
-        grads[i : i + 1, :] = row
+    _, _, _, sibling, _, plus, minus = pack_places()
+    greet(neighbours(place) + [sibling, plus, minus])
+
+    def chain(links, low, rows, with_dec):
+        here = pl.ds(low, rows)
+
+        def cross(group):
+            made = dot(stacked(kvc_grad, place, group, low, rows), wt[0, 4 * HEAD : 6 * HEAD, :])
+            store_blocks(part, place, group, made.astype(BF16), low)
+            if with_dec and group == PRODUCE[0]:
+                dpart_1[...] = fold_all(dot(cq_grad[...], wt[1, 4 * HEAD : 5 * HEAD, :]))
+
+        views = [(part, land_1, low, rows)]
+        if with_dec:
+            views.append((dpart_1, dland_1, 0, dpart_1.shape[2]))
+        sums = yield from sum_blocks(links, place, views, cross)
+        back2, gain2, shift2 = norm_back(sums[0], unit2[here], scale2[here, 0:1], gs[0, 2:3, :])
+        full_b2[place[0], place[1], here] = back2.astype(BF16)
+        views = [(full_b2, low, rows)]
+        if with_dec:
+            dback0, dgain0, dshift0 = norm_back(
+                dback1[...] + unfold(sums[1]), dunit0[...], dscale0[:, 0:1], gs[1, 0:1, :]
+            )
+            dbuf[place[0], place[1]] = fold(dback0).astype(BF16)
+            views.append((dbuf, 0, dbuf.shape[2]))
+
+        def down(group):
+            made = dot(stacked(full_b2, place, group, low, rows), ffn[0, 1])
+            made = made * stacked(slope, place, group, low, rows)
+            store_blocks(pre, place, group, made.astype(BF16), low)
+
+        yield from gather(links, place, views, down)
+        links.finish()
+        ready_rows.append(rows)
+        views = [(part, land_2, low, rows)]
+        if with_dec:
+            made = unfold_all(dbuf[...])
+            full_db0[...] = made
+            count = made.shape[0]
+            att_d_grad = dot_t(made, wt[1, 3 * HEAD : 4 * HEAD, :]).astype(BF16)
+            before = lax.broadcasted_iota(jnp.int32, (count, count), 1) <= lax.broadcasted_iota(
+                jnp.int32, (count, count), 0
+            )
+            allowed = (seg_d[...] == seg_dt[...]) & before
+            made = attend_back(sq[...], sk[...], sv[...], log_d[...], allowed, att_d_grad)
+            made = jnp.concatenate([m.astype(F32) for m in made], 1).astype(BF16)
+            dqkv_grad[...] = made
+            dpart_2[...] = fold_all(dot(made, wt[1, 0 : 3 * HEAD, :]))
+            views.append((dpart_2, dland_2, 0, dpart_2.shape[2]))
+
+        def up(group):
+            made = dot_t(stacked(pre, place, group, low, rows), ffn[0, 0])
+            store_blocks(part, place, group, made.astype(BF16), low)
+
+        sums = yield from sum_blocks(links, place, views, up)
+        made, gain1, shift1 = norm_back(
+            back2 + sums[0], unit1[here], scale1[here, 0:1], gs[0, 1:2, :]
+        )
+        back1[here] = made
+        full_b1[place[0], place[1], here] = made.astype(BF16)
+        totals.append((gain1, gain2, shift1, shift2))
+        if with_dec:
+            dec_grad[...] = dback0 + unfold(sums[1])
+            grads[4:5, :] = dgain0
+            grads[5:6, :] = dshift0
+
+        def mixed(group):
+            made = dot_t(stacked(full_b1, place, group, low, rows), wt[0, 3 * HEAD : 4 * HEAD, :])
+            store_blocks(att_grad, place, group, made.astype(BF16), low)
+
+        yield from gather(links, place, [(full_b1, low, rows)], mixed)
+        links.finish()
+
+    def ffn_chain(links):
+        while len(ready_rows) < len(CHUNKS):
+            yield
+        whole = lambda ref: ref[...].reshape(DEVICES * ref.shape[2], ref.shape[3])
+        count = full_h1.shape[3]
+        ffn_grad[0, :count] = t_dot(whole(pre), whole(full_h1)).T.astype(BF16)
+        ffn_grad[1] = dec_ffn[...]
+        yield
+        ffn_grad[0, count:] = t_dot(whole(hidden), whole(full_b2)).T.astype(BF16)
+        yield from pack_sum(links, ffn_grad, ffn_sum, pack_refs)
+
+    totals, chains, ready_rows = [], [], []
+    for n, (low, rows) in enumerate(CHUNKS):
+        links = Links(send, recv, PACK_COPIES + 7 * RING_COPIES * n)
+        chains.append(chain(links, low, rows, n == len(CHUNKS) - 1))
+    chains.append(ffn_chain(Links(send, recv)))
+    run(chains, LAG)
+    for i in range(4):
+        grads[i : i + 1, :] = sum(total[i] for total in totals)
     grads[6:8, :] = jnp.zeros((2, grads.shape[1]), F32)
-    links.finish()
 
 
 def backward_call(args, collective_id):
@@ -730,18 +869,19 @@
         backward_kernel,
         out_shape=[
             shape((*grid, rows, width), BF16),
-            shape((*grid, rows, width), BF16),
             shape((full, width), BF16),
-            shape((*grid, rows, inner), BF16),
             shape((full, 3 * HEAD), BF16),
             shape((*grid, rows, HEAD), BF16),
             shape((rows, width), F32),
             shape((count, width), F32),
             shape((8, width), F32),
+            shape((2, width, inner), BF16),
         ],
-        in_specs=[VM] * 19,
-        out_specs=[VM] * 9,
+        in_specs=[VM] * 22,
+        out_specs=[VM] * 8,
         scratch_shapes=[
+            pltpu.VMEM((*grid, rows, width), BF16),
+            pltpu.VMEM((*grid, rows, inner), BF16),
             pltpu.VMEM((*grid, rows, width), BF16),
             pltpu.VMEM(small, BF16),
             pltpu.VMEM(small, BF16),
@@ -750,117 +890,91 @@
             pltpu.VMEM((30, 2 * count, width // 4), BF16),
             pltpu.VMEM((30, 2 * count, width // 4), BF16),
             pltpu.VMEM(small, BF16),
+            pltpu.VMEM((2, 2 * width, inner), BF16),
         ]
-        + sems(7 * RING_COPIES),
+        + pack_scratch(2 * width, inner)
+        + sems(PACK_COPIES + 7 * RING_COPIES * len(CHUNKS)),
         compiler_params=params(collective_id),
     )(*args)
 
 
-def last_kernel(
-    qkv_grad, wt, gs, back1, unit0, scale0, att, ffn, small, out3, dec, *rest
-):
-    (att_out, ffn_out, small_out, enc_out, out3_out, dec_out) = rest[:6]
-    (part, land, work_a, work_f, core_a, core_f, side_a, side_f) = rest[6:14]
-    (pass_a, pass_f, over_a, over_f, sums, fin, core_s, z_s, y_s, x_s) = rest[14:24]
-    (enc, give_e, give_d, land_e, land_d, send, recv) = rest[24:]
+def last_kernel(qkv_grad, wt, gs, back1, unit0, scale0, att, small, out3, dec, *rest):
+    (att_out, small_out, enc_out, out3_out, dec_out, part, land, *pack_refs) = rest[:12]
+    (fin, core_s, y_s, x_s, z_s, late, late_t, late_p) = rest[12:20]
+    (enc, give_e, give_d, land_e, land_d, send, recv) = rest[20:]
     place = at_grid()
-    section, zh, core, partner, sibling = sections()
+    section, zh, core, sibling, _, plus, minus = pack_places()
     other = 1 - section
-    zh_plus = lax.rem(zh + section, 2)
-    plus = {"section": other, "dp": zh_plus * 2 + core}
-    minus = {"section": other, "dp": (1 - zh_plus) * 2 + core}
+    partner = {"section": other}
     far = {"dp": (1 - zh) * 2 + core}
     columns = [device_at(moved(place, d, 0)) for d in (1, 2, 3)]
     rows = [device_at(moved(place, 0, d)) for d in (1, 2, 3)]
-    greet([sibling, plus, minus, far, *columns, *rows])
-    links = Links(send, recv)
-    jobs = [
-        (att, work_a, core_a, side_a, pass_a, over_a, att_out),
-        (ffn, work_f, core_f, side_f, pass_f, over_f, ffn_out),
-    ]
-    step_core, step_side = [], []
-    for grad, _, core_land, *_ in jobs:
-        half = grad.shape[1] // 2
-        step_core.append(
-            links.start(grad.at[:, pl.ds((1 - core) * half, half)], core_land, sibling)
-        )
+    tensor = [device_at(moved(place, d // SIDE, d % SIDE)) for d in FAR_FIRST]
+    packs = []
+    for d in range(1, 8):
+        mine = section * 4 + zh * 2 + core
+        there = lax.rem(mine + d, 8)
+        packs.append({"section": lax.div(there, 4), "dp": lax.rem(there, 4)})
+    greet(tensor + packs)
     width = enc.shape[1] // 2
     there = pl.ds(pl.multiple_of(other * width, width), width)
     here = pl.ds(pl.multiple_of(section * width, width), width)
-    give_d[...] = jnp.concatenate([out3[:, there], dec[:, there]], 0).astype(BF16)
-    swap_d = links.start(give_d, land_d, partner)
+
+    def early(links):
+        give_d[...] = jnp.concatenate([out3[:, there], dec[:, there]], 0).astype(BF16)
+        swap = links.start(give_d, land_d, partner)
+        one = links.start(small.at[1 - core], core_s, sibling)
+        yield
+        one.wait_recv()
+        fin[core] = small[core] + core_s[...]
+        for land_s, devices in ((y_s, columns), (x_s, rows), (z_s, [plus, minus, far])):
+            copies = [links.start(fin.at[core], land_s.at[n], d) for n, d in enumerate(devices)]
+            yield
+            for copy in copies:
+                copy.wait_recv()
+            links.finish()
+            fin[core] = fin[core] + land_s[0] + land_s[1] + land_s[2]
+        five = links.start(fin.at[core], fin.at[core], sibling)
+        yield
+        five.wait_recv()
+        swap.wait_recv()
+        links.finish()
 
     def heads(group):
         made = dot(stacked(qkv_grad, place, group), wt[0, 0 : 3 * HEAD, :])
         store_blocks(part, place, group, made.astype(BF16))
-        if group == PRODUCE[0]:
-            return
-        for i, (grad, work, core_land, side, *_) in enumerate(jobs):
-            half = grad.shape[1] // 2
-            quarter = half // 2
-            step_core[i].wait_recv()
-            work[...] = (
-                grad[:, pl.ds(core * half, half)].astype(F32) + core_land[...].astype(F32)
-            ).astype(BF16)
-            step_side.append(
-                [
-                    links.start(work.at[other, pl.ds(h * quarter, quarter)], side.at[n], d)
-                    for n, (h, d) in enumerate(((zh_plus, plus), (1 - zh_plus, minus)))
-                ]
-            )
-
-    (sum_e,) = sum_blocks(links, place, [(part, land)], heads)
-    enc[...], gain0, shift0 = norm_back(
-        back1[...] + sum_e, unit0[...], scale0[:, 0:1], gs[0, 0:1, :]
-    )
-    sums[...] = small[...]
-    sums[0, 0:1, :] = gain0
-    sums[0, 3:4, :] = shift0
-    one = links.start(sums.at[1 - core], core_s, sibling)
-    give_e[...] = enc[:, there].astype(BF16)
-    swap_e = links.start(give_e, land_e, partner)
-    step_pass = []
-    for i, (grad, work, core_land, side, passing, over, _) in enumerate(jobs):
-        quarter = grad.shape[1] // 4
-        for copy in step_side[i]:
-            copy.wait_recv()
-        mine = work.at[section, pl.ds(zh * quarter, quarter)]
-        mine[...] = (
-            mine[...].astype(F32) + side[0].astype(F32) + side[1].astype(F32)
-        ).astype(BF16)
-        step_pass.append(
-            [
-                links.start(work.at[section, pl.ds(n * quarter, quarter)], passing.at[n], d)
-                for n, d in enumerate((plus, minus))
-            ]
+
+    def rest_of(links):
+        (sum_e,) = yield from sum_blocks(links, place, [(part, land, 0, enc.shape[0])], heads)
+        made, gain0, shift0 = norm_back(
+            back1[...] + sum_e, unit0[...], scale0[:, 0:1], gs[0, 0:1, :]
         )
-
-    def exchange(land_s, devices):
-        copies = [links.start(fin.at[core], land_s.at[n], d) for n, d in enumerate(devices)]
+        enc[...] = made
+        quarter = width // 2
+        both = [row[:, i * quarter : (i + 1) * quarter] for row in (gain0, shift0) for i in range(4)]
+        late[...] = jnp.concatenate(both, 0)
+        copies = [links.start(late, late_t.at[n], d) for n, d in enumerate(tensor)]
+        give_e[...] = enc[:, there].astype(BF16)
+        swap = links.start(give_e, land_e, partner)
+        yield
         for copy in copies:
             copy.wait_recv()
         links.finish()
-        fin[core] = fin[core] + land_s[0] + land_s[1] + land_s[2]
-
-    one.wait_recv()
-    fin[core] = sums[core] + core_s[...]
-    exchange(y_s, columns)
-    exchange(x_s, rows)
-    step_over = []
-    for i, (grad, work, core_land, side, passing, over, _) in enumerate(jobs):
-        quarter = grad.shape[1] // 4
-        ahead = []
-        for n, device in enumerate((plus, minus)):
-            step_pass[i][n].wait_recv()
-            ahead.append(
-                links.start(passing.at[n], over.at[pl.ds(n * quarter, quarter)], device)
-            )
-        step_over.append(ahead)
-    exchange(z_s, [plus, minus, far])
-    five = links.start(fin.at[core], fin.at[core], sibling)
-    swap_e.wait_recv()
-    swap_d.wait_recv()
-    enc_out[section] = enc[:, here]
+        late[...] = late[...] + jnp.sum(late_t[...], 0)
+        copies = [links.start(late, late_p.at[n], d) for n, d in enumerate(packs)]
+        enc_out[section] = enc[:, here]
+        yield
+        for copy in copies:
+            copy.wait_recv()
+        swap.wait_recv()
+        links.finish()
+
+    chains = [
+        rest_of(Links(send, recv, 2 * PACK_COPIES + 16)),
+        pack_sum(Links(send, recv), att, att_out, pack_refs),
+        early(Links(send, recv, PACK_COPIES)),
+    ]
+    run(chains)
     enc_out[other] = land_e[...].astype(F32)
     got = land_d[...].astype(F32)
     count = out3.shape[0]
@@ -868,64 +982,53 @@
     out3_out[other] = got[:count]
     dec_out[section] = dec[:, here]
     dec_out[other] = got[count:]
-    last = []
-    for i, (grad, work, core_land, side, passing, over, out) in enumerate(jobs):
-        for copy in step_over[i]:
-            copy.wait_recv()
-        out[core] = (work[section].astype(F32) + over[...].astype(F32)).astype(BF16)
-        last.append(links.start(out.at[core], out.at[core], sibling))
-    five.wait_recv()
     small_out[...] = fin[section]
-    for copy in last:
-        copy.wait_recv()
-    links.finish()
+    total = late[...] + jnp.sum(late_p[...], 0)
+    quarter = width // 2
+    for i in range(8):
+        row = 0 if i < 4 else 3
+        cols = slice((i % 4) * quarter, (i % 4 + 1) * quarter)
+        added = jnp.where(section == 0, total[i : i + 1], 0.0)
+        small_out[row : row + 1, cols] = small_out[row : row + 1, cols] + added
 
 
 def last_call(args, collective_id):
-    qkv_grad, back1, (att, ffn, small, out3, dec) = args[0], args[3], args[6:]
+    back1, (att, small, out3, dec) = args[3], args[6:]
     rows, cols = back1.shape
     count, width = dec.shape[0], cols // 2
-    grads = (att, ffn)
-
-    def lands(lead):
-        return [pltpu.VMEM((*lead(g), g.shape[2]), BF16) for g in grads]
-
-    half = lambda g: (2, g.shape[1] // 2)
-    quarter = lambda g: (2, g.shape[1] // 4)
+    small_rows = small.shape[1:]
     return pl.pallas_call(
         last_kernel,
-        out_shape=[shape((*half(g), g.shape[2]), BF16) for g in grads]
-        + [
-            shape(small.shape[1:], F32),
+        out_shape=[
+            shape((2, att.shape[1] // 2, att.shape[2]), BF16),
+            shape(small_rows, F32),
             shape((2, rows, width), F32),
             shape((2, count, width), F32),
             shape((2, count, width), F32),
         ],
-        in_specs=[VM] * 11,
-        out_specs=[VM] * 6,
+        in_specs=[VM] * 10,
+        out_specs=[VM] * 5,
         scratch_shapes=[
             pltpu.VMEM((SIDE, SIDE, rows, cols), BF16),
             pltpu.VMEM((30, rows, width), BF16),
         ]
-        + lands(half)
-        + lands(half)
-        + lands(quarter)
-        + lands(quarter)
-        + lands(lambda g: half(g)[1:])
+        + pack_scratch(*att.shape[1:])
         + [
             pltpu.VMEM(small.shape, F32),
-            pltpu.VMEM(small.shape, F32),
-            pltpu.VMEM(small.shape[1:], F32),
-            pltpu.VMEM((3, *small.shape[1:]), F32),
-            pltpu.VMEM((3, *small.shape[1:]), F32),
-            pltpu.VMEM((3, *small.shape[1:]), F32),
+            pltpu.VMEM(small_rows, F32),
+            pltpu.VMEM((3, *small_rows), F32),
+            pltpu.VMEM((3, *small_rows), F32),
+            pltpu.VMEM((3, *small_rows), F32),
+            pltpu.VMEM((8, width // 2), F32),
+            pltpu.VMEM((DEVICES - 1, 8, width // 2), F32),
+            pltpu.VMEM((7, 8, width // 2), F32),
             pltpu.VMEM((rows, cols), F32),
             pltpu.VMEM((rows, width), BF16),
             pltpu.VMEM((2 * count, width), BF16),
             pltpu.VMEM((rows, width), BF16),
             pltpu.VMEM((2 * count, width), BF16),
         ]
-        + sems(RING_COPIES + 2 * 8 + 14),
+        + sems(2 * PACK_COPIES + 16 + RING_COPIES + DEVICES + 7),
         compiler_params=params(collective_id),
     )(*args)
 
@@ -969,14 +1072,14 @@
             cq, flat(kvc), d1, mine(cotangent), c[:, None], e[None, :], wt, ffn, gs, 3
         )
     )
-    full_b2, full_b1, full_db0, pre, dqkv_grad, att_e_grad, back1, dec_grad, small_b = (
-        backward_call(
-            (
-                blocks(kvc_grad), cq_grad, dback1, wt, gs, ffn, unit1, scale1, unit2, scale2,
-                dunit0, dscale0, slope, sq, sk, sv, log_d, c[:, None], c[None, :],
-            ),
-            4,
-        )
+    dec_ffn = jnp.concatenate([t_dot(full_d2, dpre), t_dot(full_db2, dhidden)], 0).astype(BF16)
+    full_b1, full_db0, dqkv_grad, att_e_grad, back1, dec_grad, small_b, ffn_sum = backward_call(
+        (
+            blocks(kvc_grad), cq_grad, dback1, wt, gs, ffn, unit1, scale1, unit2, scale2,
+            dunit0, dscale0, slope, sq, sk, sv, log_d, c[:, None], c[None, :],
+            full_h1, hidden, dec_ffn,
+        ),
+        4,
     )
     made = attend_back(q, k, v, log_e, allow_e, flat(att_e_grad))
     qkv_grad = jnp.concatenate(made, 1)
@@ -1002,14 +1105,6 @@
             ),
         ]
     ).astype(BF16)
-    ffn_grads = jnp.stack(
-        [
-            jnp.concatenate(
-                [t_dot(flat(full_h1), flat(pre)), t_dot(flat(full_b2), flat(hidden))], 0
-            ),
-            jnp.concatenate([t_dot(full_d2, dpre), t_dot(full_db2, dhidden)], 0),
-        ]
-    ).astype(BF16)
     none = jnp.zeros((1, width), F32)
     row = lambda a, i: a[i : i + 1]
     small = jnp.stack(
@@ -1024,10 +1119,10 @@
             ),
         ]
     )
-    att_sum, ffn_sum, small_sum, enc_out, d3_out, dec_out = last_call(
+    att_sum, small_sum, enc_out, d3_out, dec_out = last_call(
         (
             blocks(qkv_grad), wt, gs, back1, unit0, scale0,
-            att_grads, ffn_grads, small, d3, dec_grad,
+            att_grads, small, d3, dec_grad,
         ),
         5,
     )

time: 376 us -> 346 us (0.920)
  the two profiles are of different devices: /device:TPU:0 before, /device:TPU:1 now
where the time goes in v4:
time: 346 us; the launch traced here: 340 us
  Pallas kernels  284 us (82%)
  matrix products  23.6 us (7%)
  local copies, waits for them, and re-layouts  19 us (5%)
  other arithmetic  12.1 us (3%)
    pallas_call x1, Pallas kernels, backward_call(): pl.pallas_call(backward_kernel, out_shape=[shape((*grid, rows, width), BF...  99.9 us
    pallas_call x1, Pallas kernels, forward_call(): pl.pallas_call(forward_kernel, out_shape=[shape((2, *ffn.shape), BF16), s...  75.5 us
    pallas_call x1, Pallas kernels, decoder_call(): pl.pallas_call(decoder_kernel, out_shape=[shape((rows, width), F32), shap...  40.5 us
    pallas_call x1, Pallas kernels, last_call(): pl.pallas_call(last_kernel, out_shape=[shape((2, att.shape[1] // 2, att.s...  39.6 us
    pallas_call x1, Pallas kernels, first_call(): pl.pallas_call(first_kernel, out_shape=[shape((2, *wt.shape), BF16), shap...  28.6 us
    dot_general x11, matrix products, t_dot(): lax.dot_general(a, b, (((0,), (0,)), ((), ())), preferred_element_type=F32)  14.5 us
    unnamed x59, local copies, waits for them, and re-layouts  6.94 us

profile of v4, /device:TPU:1, one launch (start us, length us, event | category | flops | bytes accessed | tf_op | source)
XLA Modules:
  0.0 340.0 jit_solution(5284090683294910989)
XLA Ops:
  0.7 0.7 fusion.55
  1.4 0.7 fusion.54
  2.1 1.2 constant_dynamic-slice_fusion.refs_18_
  3.3 1.3 fusion.18
  4.6 1.3 dynamic-slice_bitcast_fusion.1
  5.9 0.7 copy_bitcast_fusion
  6.7 0.6 pad_maximum_fusion.4.gs_in
  7.3 0.7 copy.18.seg_d.refs_17_
  8.0 0.7 dynamic-slice_bitcast_fusion.x
  8.7 28.6 %shard_map.144 = (bf16[2,384,1024]{2,1,0:T(8,128)(2,1)}, f32[2,8,1024]{2,1,0:T(8,128)}, bf16[4,4,80,1024]{3,2,1,0:T(8,128)(2,1)}, f32[80,1024]{1,0:T(8,128)}, f3...) custom-call(bf16[80,1024]{1,0:T(8,128)(2,1)} %dynamic-slice_bitcast_, ...), custom_call_target="tpu_custom_call" | custom-call | tf_op jit(solution)/shard_map/pallas_call | solution.py:528
  37.3 1.0 fusion.23
  38.3 1.6 convolution_convert_fusion.9.att_d
  39.9 0.8 copy.19.refs_16_
  40.6 2.7 fusion.22
  43.4 1.0 fusion.1
  44.3 1.7 copy-done.1
  46.1 1.3 fusion.12
  47.3 0.9 copy.16
  48.2 75.5 %shard_map.145 = (bf16[2,2,1024,256]{3,2,1,0:T(8,128)(2,1)}, bf16[4,4,80,1024]{3,2,1,0:T(8,128)(2,1)}, bf16[4,4,80,1024]{3,2,1,0:T(8,128)(2,1)}, bf16[128,1024]{...) custom-call(bf16[4,4,80,64]{3,2,1,0:T(8,128)(2,1)} %bitcast.88, ...), custom_call_target="tpu_custom_call" | custom-call | tf_op jit(solution)/shard_map/pallas_call | solution.py:643
  123.7 40.5 %shard_map.146 = (f32[8,1024]{1,0:T(8,128)}, f32[8,1024]{1,0:T(8,128)}, bf16[128,1024]{1,0:T(8,128)(2,1)}, bf16[128,1024]{1,0:T(8,128)(2,1)}, bf16[128,1024]{1,0...) custom-call(bf16[128,64]{1,0:T(8,128)(2,1)} %get-tuple-element.68.cq, ...), custom_call_target="tpu_custom_call" | custom-call | tf_op jit(solution)/shard_map/pallas_call | solution.py:731
  164.3 1.0 convolution_convert_fusion.7
  165.4 2.2 convolution_convert_fusion.4
  167.8 0.3 convolution_convert_fusion.1
  168.2 0.3 convolution_convert_fusion
  168.5 1.0 pad_maximum_fusion.1.refs_21_
  169.5 99.9 %shard_map.147 = (bf16[4,4,80,1024]{3,2,1,0:T(8,128)(2,1)}, bf16[128,1024]{1,0:T(8,128)(2,1)}, bf16[128,192]{1,0:T(8,128)(2,1)}, bf16[4,4,80,64]{3,2,1,0:T(8,128...) custom-call(bf16[4,4,80,128]{3,2,1,0:T(8,128)(2,1)} %bitcast.87, ...), custom_call_target="tpu_custom_call" | custom-call | tf_op jit(solution)/shard_map/pallas_call | solution.py:868
  269.5 3.0 convolution_convert_fusion.5
  272.5 0.8 fusion.21
  273.3 0.8 fusion.19
  274.3 0.6 pad_maximum_fusion.3.small
  275.2 0.3 convolution_convert_fusion.2
  275.6 4.9 %fusion.7 = bf16[1280,64]{0,1:T(8,128)(2,1)} fusion(bf16[1280,64]{1,0:T(8,128)(2,1)S(1)} %bitcast.89, f32[1280,1280]{0,1:T(8,128)} %copy-done.1, f32[1280]{0:T(1024)S(1)} %log_add_fusion), kind=kOutput, calls=%fused_computation.14 | convolution fusion | flops 213073920 | bytes 6886400 | tf_op jit(solution)/shard_map/dot_general | solution.py:60
  280.5 1.5 bitcast_convert_fusion
  281.9 1.9 multiply_reduce_fusion
  283.8 2.0 multiply_convert_fusion
  285.8 1.1 fusion.11
  287.0 0.7 fusion.10
  287.8 0.9 convolution_convert_fusion.3
  288.8 1.3 pad_maximum_fusion.att
  290.1 1.1 copy.21
  291.2 39.6 %shard_map.148 = (bf16[2,192,1024]{2,1,0:T(8,128)(2,1)}, f32[8,1024]{1,0:T(8,128)}, f32[2,80,512]{2,1,0:T(8,128)}, f32[2,8,512]{2,1,0:T(8,128)}, f32[2,8,512]{2,1,0:T(8,128)}) custom-call(bf16[4,4,80,192]{3,2,1,0:T(8,128)(2,1)} %bitcast.84, bf16[2,384,1024]{2,1,0:T(8,128)(2,1)} %get-tuple-element.66.wt.refs_3_, f32[2,8,1024]{2,1,0:T(8,128)} %get-tuple-element.67.gs.refs_4_, ...), custom_call_target="tpu_custom_call" | custom-call | tf_op jit(solution)/shard_map/pallas_call | solution.py:1000
  330.8 1.4 convert_element_type.51
  332.2 0.8 slice_bitcast_fusion
  333.1 0.6 copy.23
  333.7 0.6 copy.22
  334.3 2.5 convert_bitcast_fusion
  336.7 1.7 copy.31
  338.4 1.4 copy.32
  (67 shorter events, 0.9 us)
Async XLA Ops:
  0.6 7.4 %copy-start = (bf16[2,80,1024]{2,1,0:T(8,128)(2,1)S(1)}, bf16[2,80,1024]{2,1,0:T(8,128)(2,1)}, u32[]{:S(2)}) copy-start(bf16[2,80,1024]{2,1,0:T(8,128)(2,1)} %param.9) | copy-start | bytes 983044
  43.3 2.7 copy-start.1
  43.4 2.7 copy-start.10
  123.7 40.6 %copy-start.15 = (bf16[128,1024]{1,0:T(8,128)(2,1)S(1)}, bf16[128,1024]{1,0:T(8,128)(2,1)}, u32[]{:S(2)}) copy-start(bf16[128,1024]{1,0:T(8,128)(2,1)} %get-tuple-element.98) | copy-start | bytes 786436
  123.7 41.6 %copy-start.2 = (bf16[4,4,80,1024]{3,2,1,0:T(8,128)(2,1)S(1)}, bf16[4,4,80,1024]{3,2,1,0:T(8,128)(2,1)}, u32[]{:S(2)}) copy-start(bf16[4,4,80,1024]{3,2,1,0:T(8,128)(2,1)} %get-tuple-element.94) | copy-start | bytes 7864324
  164.2 3.3 copy-start.23
  164.2 3.4 copy-start.16
  164.2 3.4 copy-start.22
  164.3 3.6 %copy-start.13 = (bf16[128,1024]{1,0:T(8,128)(2,1)S(1)}, bf16[128,1024]{1,0:T(8,128)(2,1)}, u32[]{:S(2)}) copy-start(bf16[128,1024]{1,0:T(8,128)(2,1)} %get-tuple-element.84) | copy-start | bytes 786436
  164.3 3.6 %copy-start.21 = (bf16[128,256]{1,0:T(8,128)(2,1)S(1)}, bf16[128,256]{1,0:T(8,128)(2,1)}, u32[]{:S(2)}) copy-start(bf16[128,256]{1,0:T(8,128)(2,1)} %get-tuple-element.85) | copy-start | bytes 196612
  164.3 3.9 %copy-start.12 = (bf16[128,1024]{1,0:T(8,128)(2,1)S(1)}, bf16[128,1024]{1,0:T(8,128)(2,1)}, u32[]{:S(2)}) copy-start(bf16[128,1024]{1,0:T(8,128)(2,1)} %get-tuple-element.86) | copy-start | bytes 786436
  164.3 3.9 %copy-start.20 = (bf16[128,256]{1,0:T(8,128)(2,1)S(1)}, bf16[128,256]{1,0:T(8,128)(2,1)}, u32[]{:S(2)}) copy-start(bf16[128,256]{1,0:T(8,128)(2,1)} %get-tuple-element.87) | copy-start | bytes 196612
  269.4 5.5 %copy-start.14 = (bf16[128,1024]{1,0:T(8,128)(2,1)S(1)}, bf16[128,1024]{1,0:T(8,128)(2,1)}, u32[]{:S(2)}) copy-start(bf16[128,1024]{1,0:T(8,128)(2,1)} %get-tuple-element.97) | copy-start | bytes 786436
  269.4 5.5 %copy-start.18 = (bf16[128,64]{1,0:T(8,128)(2,1)S(1)}, bf16[128,64]{1,0:T(8,128)(2,1)}, u32[]{:S(2)}) copy-start(bf16[128,64]{1,0:T(8,128)(2,1)} %convolution_convert_fusion.9.att_d) | copy-start | bytes 49156
  269.4 5.7 %copy-start.17 = (bf16[128,1024]{1,0:T(8,128)(2,1)S(1)}, bf16[128,1024]{1,0:T(8,128)(2,1)}, u32[]{:S(2)}) copy-start(bf16[128,1024]{1,0:T(8,128)(2,1)} %get-tuple-element.96) | copy-start | bytes 786436
  269.5 5.7 %copy-start.19 = (bf16[128,192]{1,0:T(8,128)(2,1)S(1)}, bf16[128,192]{1,0:T(8,128)(2,1)}, u32[]{:S(2)}) copy-start(bf16[128,192]{1,0:T(8,128)(2,1)} %get-tuple-element.95) | copy-start | bytes 147460
  269.5 6.1 %copy-start.3 = (bf16[4,4,80,64]{3,2,1,0:T(8,128)(2,1)S(1)}, bf16[4,4,80,64]{3,2,1,0:T(8,128)(2,1)}, u32[]{:S(2)}) copy-start(bf16[4,4,80,64]{3,2,1,0:T(8,128)(2,1)} %get-tuple-element.88) | copy-start | bytes 491524
  275.2 6.8 %slice-start = ((s8[6553600]{0:T(1024)(128)(4,1)}), s8[4194304]{0:T(1024)(128)(4,1)S(1)}, s32[]{:S(2)}) async-start(s8[6553600]{0:T(1024)(128)(4,1)} %bitcast.82), calls=%async_computation | async-start | bytes 8388608
  275.5 4.9 %copy-start.4 = (bf16[2,1024,256]{2,1,0:T(8,128)(2,1)S(1)}, bf16[2,1024,256]{2,1,0:T(8,128)(2,1)}, u32[]{:S(2)}) copy-start(bf16[2,1024,256]{2,1,0:T(8,128)(2,1)} %get-tuple-element.109) | copy-start | bytes 3145732
  275.5 6.4 %slice-start.1 = ((s8[6553600]{0:T(1024)(128)(4,1)}), s8[2359296]{0:T(1024)(128)(4,1)S(1)}, s32[]{:S(2)}) async-start(s8[6553600]{0:T(1024)(128)(4,1)} %bitcast.82), calls=%async_computation.1 | async-start | bytes 4718592
  280.4 1.5 copy-start.11
  283.8 2.0 copy-start.9
  285.8 1.2 copy-start.8
  285.8 1.9 copy-start.6
  285.8 1.9 copy-start.24
  287.8 1.0 copy-start.5
  287.8 1.0 copy-start.7
